TPU v7x, 32 devices: a whole 2x2x4 slice. The times are simulated.
32 devices in a mesh: dp: 4 (over y, x), expert: 8 (over z, core).
Axes of the slice: x: 2, y: 2, z: 4, core: 2. Of those that a mesh axis runs over, the one named last changes fastest.
Arguments:
- tokens: bfloat16 [32768, 768], P(('dp', 'expert')), may hold values from -6 to 6
- cotangent: bfloat16 [32768, 768], P(('dp', 'expert')), may hold values from -6 to 6
- gain_one: float32 [768], replicated, may hold values from 0.1 to 1.9
- gain_two: float32 [768], replicated, may hold values from 0.1 to 1.9
- query_weight: bfloat16 [768, 768], replicated, may hold values from -0.02734375 to 0.02734375
- key_weight: bfloat16 [768, 768], replicated, may hold values from -0.21875 to 0.21875
- value_weight: bfloat16 [768, 768], replicated, may hold values from -0.21875 to 0.21875
- out_weight: bfloat16 [768, 768], replicated, may hold values from -3.5 to 3.5
- bias_table: float32 [32, 12], replicated, may hold values from -4 to 4
- router_weight: bfloat16 [768, 16], replicated, may hold values from -0.125 to 0.125
- expert_in: bfloat16 [16, 768, 3072], P('expert'), may hold values from -0.21875 to 0.21875
- expert_out: bfloat16 [16, 3072, 768], P('expert')
- lengths: int32 [32], P(('dp', 'expert')), may hold values from 256 to 1024, as said below
- routes: int32 [32768, 1], P(('dp', 'expert')), may hold values from 0 to 15; in each aligned block of 1024 rows (0 to 1023, 1024 to 2047, ...) at most 128 rows name the same one
Outputs:
- mixed: bfloat16 [32768, 768], P(('dp', 'expert'))
- grad_tokens: bfloat16 [32768, 768], P(('dp', 'expert'))
- grad_gain_one: float32 [768], replicated
- grad_gain_two: float32 [768], replicated
- grad_query_weight: float32 [768, 768], replicated
- grad_key_weight: float32 [768, 768], replicated
- grad_value_weight: float32 [768, 768], replicated
- grad_out_weight: float32 [768, 768], replicated
- grad_bias_table: float32 [32, 12], replicated
- grad_router: float32 [768, 16], replicated
- grad_expert_in: float32 [16, 768, 3072], P('expert', None, 'dp')
- grad_expert_out: float32 [16, 3072, 768], P('expert', 'dp')
Inputs may be any that keep to these rules, and one draw needn't show every extreme that they name: `lengths`: each sequence's first that many positions are real tokens, the rest padding. Some sequence has 1024 and some a quarter of 1024. `routes`: among the rows of one device (aligned blocks of 1024 rows), no expert is named by more than 128 rows, a bound that some block reaches.
All inputs are finite; a program needn't handle non-finite values.
Results may differ from a plain program's by a relative error of at most 0.017.
Values may be sent and summed in bfloat16 or wider, within the bound.
A program may use at most 384 MiB of HBM per device.

v0:
```python
import jax
import jax.numpy as jnp
from jax import lax
from jax.sharding import PartitionSpec as P

LENGTH = 1024


EPSILON = 1e-06
THRESHOLDS = (12, 16, 23, 32, 46, 64, 91)
HIGHEST = lax.Precision.HIGHEST


def bucket_of(offsets):
    distance = jnp.abs(offsets)
    distant = 8 + sum(((distance >= limit).astype(jnp.int32) for limit in THRESHOLDS))
    nearby = jnp.where(distance < 8, distance, distant)
    return nearby + 16 * (offsets > 0).astype(jnp.int32)


def rms_norm(values, gain):
    scaling = lax.rsqrt(jnp.mean(values * values, axis=-1, keepdims=True) + EPSILON)
    return values * scaling * gain


def bucket_onehot(block_start, block_rows, length, bucket_total):
    key_pos = jnp.arange(length, dtype=jnp.int32)[None, :]
    query_pos = (block_start + jnp.arange(block_rows, dtype=jnp.int32))[:, None]
    bucket_ids = bucket_of(key_pos - query_pos)
    return (
        bucket_ids[:, :, None] == jnp.arange(bucket_total, dtype=jnp.int32)[None, None, :]
    ).astype(jnp.bfloat16)


def block_scores(query_block, key_heads, bias_block, live_keys):
    raw_scores = (
        jnp.einsum("qhd,khd->hqk", query_block, key_heads, preferred_element_type=jnp.float32)
        + bias_block
    )
    return jnp.where(live_keys[None, None, :], raw_scores, -1e30)


def body(
    tokens,
    cotangent,
    gain_one,
    gain_two,
    query_weight,
    key_weight,
    value_weight,
    out_weight,
    bias_table,
    router_weight,
    expert_in,
    expert_out,
    lengths,
    routes,
):
    row_count, model_width = tokens.shape
    length = LENGTH
    bucket_total, head_count = bias_table.shape
    head_size = model_width // head_count
    expert_count = router_weight.shape[1]
    slot_most = 2 * row_count // expert_count
    local_experts = expert_in.shape[0]
    peer_count = lax.axis_size("expert")
    block_rows = min(512, length)
    buffer_shape = (peer_count, local_experts, slot_most, model_width)
    positions = jnp.arange(row_count, dtype=jnp.int32) % length
    valid_rows = (positions < jnp.repeat(lengths, length)).astype(jnp.float32)[:, None]
    route_ids = routes[:, 0]
    one_hot_int = (route_ids[:, None] == jnp.arange(expert_count, dtype=jnp.int32)[None, :]).astype(
        jnp.int32
    )
    before = jnp.cumsum(one_hot_int, axis=0) - one_hot_int
    rank_index = jnp.sum(before * one_hot_int, axis=1)
    slot_index = route_ids * slot_most + rank_index
    one_hot = one_hot_int.astype(jnp.float32)
    token_values = tokens.astype(jnp.float32)
    h_one = rms_norm(token_values, gain_one).astype(jnp.bfloat16)
    query = jnp.dot(h_one, query_weight, preferred_element_type=jnp.float32).astype(jnp.bfloat16)
    key_rows = jnp.dot(h_one, key_weight, preferred_element_type=jnp.float32).astype(jnp.bfloat16)
    value_rows = jnp.dot(h_one, value_weight, preferred_element_type=jnp.float32).astype(
        jnp.bfloat16
    )
    block_starts = list(range(0, length, block_rows))
    onehots = [bucket_onehot(start, block_rows, length, bucket_total) for start in block_starts]
    bias_blocks = [
        jnp.einsum(
            "qkb,bh->hqk",
            table_hot,
            bias_table,
            precision=HIGHEST,
            preferred_element_type=jnp.float32,
        )
        for table_hot in onehots
    ]
    attention_parts = []
    logsum_parts = []
    seq_index = 0
    seq_base = seq_index * length
    key_heads = key_rows.reshape(length, head_count, head_size)
    value_heads = value_rows.reshape(length, head_count, head_size)
    live_keys = jnp.arange(length, dtype=jnp.int32) < lengths[seq_index]
    for block_number, block_start in enumerate(block_starts):
        query_block = query[seq_base + block_start : seq_base + block_start + block_rows].reshape(
            block_rows, head_count, head_size
        )
        scores = block_scores(query_block, key_heads, bias_blocks[block_number], live_keys)
        row_max = jnp.max(scores, axis=-1, keepdims=True)
        exp_scores = jnp.exp(scores - row_max)
        exp_total = jnp.sum(exp_scores, axis=-1, keepdims=True)
        attn_probs = (exp_scores / exp_total).astype(jnp.bfloat16)
        block_out = jnp.einsum(
            "hqk,khd->qhd", attn_probs, value_heads, preferred_element_type=jnp.float32
        )
        attention_parts.append(block_out.reshape(block_rows, model_width))
        logsum_parts.append(row_max + jnp.log(exp_total))
    attention = jnp.concatenate(attention_parts, axis=0).astype(jnp.bfloat16)
    branch = jnp.dot(attention, out_weight, preferred_element_type=jnp.float32)
    middle = token_values + branch

    def norm_two(values, gain):
        return rms_norm(values, gain) * valid_rows

    h_two = norm_two(middle, gain_two).astype(jnp.bfloat16)
    logits = jnp.dot(h_two, router_weight, preferred_element_type=jnp.float32)
    router_probs = jax.nn.softmax(logits, axis=-1)
    gate_value = jnp.sum(router_probs * one_hot, axis=1, keepdims=True)
    send_rows = (
        jnp.zeros((expert_count * slot_most, model_width), jnp.bfloat16)
        .at[slot_index]
        .set(h_two)
        .reshape(buffer_shape)
    )
    first_weight, second_weight = (expert_in, expert_out)
    rows_all = lax.all_to_all(send_rows, "expert", split_axis=0, concat_axis=0, tiled=True)
    pre_act = jnp.einsum(
        "semd,edf->semf", rows_all, first_weight, preferred_element_type=jnp.float32
    )
    activated = jax.nn.gelu(pre_act).astype(jnp.bfloat16)
    partial_value = jnp.einsum(
        "semf,efd->semd", activated, second_weight, preferred_element_type=jnp.float32
    )
    produced = partial_value.astype(jnp.bfloat16)
    rows_kept = rows_all
    returned = lax.all_to_all(produced, "expert", split_axis=0, concat_axis=0, tiled=True)
    expert_rows = returned.reshape(expert_count * slot_most, model_width)[slot_index].astype(
        jnp.float32
    )
    mixed_out = ((middle + gate_value * expert_rows) * valid_rows).astype(jnp.bfloat16)
    grad_mixed = cotangent.astype(jnp.float32) * valid_rows
    grad_gate = jnp.sum(grad_mixed * expert_rows, axis=1, keepdims=True)
    grad_rows = (gate_value * grad_mixed).astype(jnp.bfloat16)
    grad_send = (
        jnp.zeros((expert_count * slot_most, model_width), jnp.bfloat16)
        .at[slot_index]
        .set(grad_rows)
        .reshape(buffer_shape)
    )
    grad_arrived = lax.all_to_all(grad_send, "expert", split_axis=0, concat_axis=0, tiled=True)
    rows_all = rows_kept
    pre_act = jnp.einsum(
        "semd,edf->semf", rows_all, first_weight, preferred_element_type=jnp.float32
    )
    activated, gelu_back = jax.vjp(jax.nn.gelu, pre_act)
    activated_low = activated.astype(jnp.bfloat16)
    grad_out_local = jnp.einsum(
        "semf,semd->efd", activated_low, grad_arrived, preferred_element_type=jnp.float32
    )
    grad_act = jnp.einsum(
        "semd,efd->semf", grad_arrived, second_weight, preferred_element_type=jnp.float32
    )
    grad_pre = gelu_back(grad_act)[0].astype(jnp.bfloat16)
    grad_in_local = jnp.einsum(
        "semd,semf->edf", rows_all, grad_pre, preferred_element_type=jnp.float32
    )
    grad_partial = jnp.einsum(
        "semf,edf->semd", grad_pre, first_weight, preferred_element_type=jnp.float32
    )
    grad_piece = grad_partial.astype(jnp.bfloat16)
    grad_back = lax.all_to_all(grad_piece, "expert", split_axis=0, concat_axis=0, tiled=True)
    grad_sent = grad_back.reshape(expert_count * slot_most, model_width)[slot_index].astype(
        jnp.float32
    )
    grad_logits = (grad_gate * gate_value * (one_hot - router_probs)).astype(jnp.bfloat16)
    grad_router = jnp.einsum("td,te->de", h_two, grad_logits, preferred_element_type=jnp.float32)
    grad_h_two = grad_sent + jnp.dot(
        grad_logits, router_weight.T, preferred_element_type=jnp.float32
    )
    _, norm_two_back = jax.vjp(norm_two, middle, gain_two)
    grad_middle_norm, grad_gain_two = norm_two_back(grad_h_two)
    grad_middle = grad_mixed + grad_middle_norm
    grad_branch = grad_middle.astype(jnp.bfloat16)
    grad_out_weight = jnp.einsum(
        "td,te->de", attention, grad_branch, preferred_element_type=jnp.float32
    )
    grad_attention = jnp.dot(grad_branch, out_weight.T, preferred_element_type=jnp.float32).astype(
        jnp.bfloat16
    )
    grad_query_parts = []
    grad_table = jnp.zeros((bucket_total, head_count), jnp.float32)
    seq_index = 0
    seq_base = seq_index * length
    key_heads = key_rows.reshape(length, head_count, head_size)
    value_heads = value_rows.reshape(length, head_count, head_size)
    live_keys = jnp.arange(length, dtype=jnp.int32) < lengths[seq_index]
    grad_key_heads = jnp.zeros((length, head_count, head_size), jnp.float32)
    grad_value_heads = jnp.zeros((length, head_count, head_size), jnp.float32)
    for block_number, block_start in enumerate(block_starts):
        row_slice = slice(seq_base + block_start, seq_base + block_start + block_rows)
        query_block = query[row_slice].reshape(block_rows, head_count, head_size)
        grad_block = grad_attention[row_slice].reshape(block_rows, head_count, head_size)
        scores = block_scores(query_block, key_heads, bias_blocks[block_number], live_keys)
        attn_probs = jnp.exp(scores - logsum_parts[seq_index * len(block_starts) + block_number])
        probs_low = attn_probs.astype(jnp.bfloat16)
        grad_probs = jnp.einsum(
            "qhd,khd->hqk", grad_block, value_heads, preferred_element_type=jnp.float32
        )
        inner_sum = jnp.sum(attn_probs * grad_probs, axis=-1, keepdims=True)
        grad_scores = (attn_probs * (grad_probs - inner_sum)).astype(jnp.bfloat16)
        grad_query_block = jnp.einsum(
            "hqk,khd->qhd", grad_scores, key_heads, preferred_element_type=jnp.float32
        )
        grad_query_parts.append(grad_query_block.reshape(block_rows, model_width))
        grad_key_heads = grad_key_heads + jnp.einsum(
            "hqk,qhd->khd", grad_scores, query_block, preferred_element_type=jnp.float32
        )
        grad_value_heads = grad_value_heads + jnp.einsum(
            "hqk,qhd->khd", probs_low, grad_block, preferred_element_type=jnp.float32
        )
        grad_table = grad_table + jnp.einsum(
            "hqk,qkb->bh", grad_scores, onehots[block_number], preferred_element_type=jnp.float32
        )
    grad_key_parts = grad_key_heads.reshape(length, model_width)
    grad_value_parts = grad_value_heads.reshape(length, model_width)
    grad_query = jnp.concatenate(grad_query_parts, axis=0).astype(jnp.bfloat16)
    grad_key = grad_key_parts.astype(jnp.bfloat16)
    grad_value = grad_value_parts.astype(jnp.bfloat16)
    grad_query_weight = jnp.einsum(
        "td,te->de", h_one, grad_query, preferred_element_type=jnp.float32
    )
    grad_key_weight = jnp.einsum("td,te->de", h_one, grad_key, preferred_element_type=jnp.float32)
    grad_value_weight = jnp.einsum(
        "td,te->de", h_one, grad_value, preferred_element_type=jnp.float32
    )
    grad_h_one = jnp.dot(grad_query, query_weight.T, preferred_element_type=jnp.float32)
    grad_h_one = grad_h_one + jnp.dot(grad_key, key_weight.T, preferred_element_type=jnp.float32)
    grad_h_one = grad_h_one + jnp.dot(
        grad_value, value_weight.T, preferred_element_type=jnp.float32
    )
    _, norm_one_back = jax.vjp(rms_norm, token_values, gain_one)
    grad_token_norm, grad_gain_one = norm_one_back(grad_h_one)
    grad_tokens = (grad_middle + grad_token_norm).astype(jnp.bfloat16)
    (
        grad_query_weight,
        grad_key_weight,
        grad_value_weight,
        grad_out_weight,
        grad_table,
        grad_router,
        grad_gain_one,
        grad_gain_two,
    ) = lax.psum(
        (
            grad_query_weight,
            grad_key_weight,
            grad_value_weight,
            grad_out_weight,
            grad_table,
            grad_router,
            grad_gain_one,
            grad_gain_two,
        ),
        ("dp", "expert"),
    )
    grad_expert_in, grad_expert_out = (
        lax.psum_scatter(
            grad_in_local.astype(jnp.bfloat16), "dp", scatter_dimension=2, tiled=True
        ).astype(jnp.float32),
        lax.psum_scatter(
            grad_out_local.astype(jnp.bfloat16), "dp", scatter_dimension=1, tiled=True
        ).astype(jnp.float32),
    )
    return (
        mixed_out,
        grad_tokens,
        grad_gain_one,
        grad_gain_two,
        grad_query_weight,
        grad_key_weight,
        grad_value_weight,
        grad_out_weight,
        grad_table,
        grad_router,
        grad_expert_in,
        grad_expert_out,
    )


def solution(mesh):
    placed = (
        P(("dp", "expert"), None),
        P(("dp", "expert"), None),
        P(),
        P(),
        P(),
        P(),
        P(),
        P(),
        P(),
        P(),
        P("expert", None, None),
        P("expert", None, None),
        P(("dp", "expert")),
        P(("dp", "expert"), None),
    )
    return jax.shard_map(
        body,
        mesh=mesh,
        in_specs=placed,
        out_specs=(
            P(("dp", "expert"), None),
            P(("dp", "expert"), None),
            P(),
            P(),
            P(),
            P(),
            P(),
            P(),
            P(),
            P(),
            P("expert", None, "dp"),
            P("expert", "dp", None),
        ),
        check_vma=False,
    )
```

profile of v0, /device:TPU:0, one launch (start us, length us, event | category | flops | bytes accessed | tf_op | source)
XLA Modules:
  0.0 1054.7 jit_solution(531729211421055246)
XLA Ops:
  12.5 4.5 reduce-window.6
  22.3 2.9 convolution_convert_fusion.2
  26.2 3.3 convolution_convert_fusion.1
  29.5 2.7 convolution_convert_fusion.3
  32.2 3.4 fusion.68
  35.7 23.9 %fusion.3 = f32[512,1024,12]{0,2,1:T(8,128)} fusion(s32[512,1024]{0,1:T(8,128)S(1)} %copy-done.17, f32[32,12]{0,1:T(8,128)S(1)} %copy-done.75), kind=kOutput, calls=%fused_computation.9 | convolution fusion | flops 2432696320 | bytes 27264512 | tf_op jit(solution)/shard_map/qkb,bh->hqk/dot_general | solution.py:89
  59.6 30.4 %copy.73 = f32[512,1024,12]{1,0,2:T(8,128)} copy(f32[512,1024,12]{0,2,1:T(8,128)} %fusion.3) | data formatting | bytes 50331648 | tf_op jit(solution)/shard_map/qkb,bh->hqk/dot_general | solution.py:89
  90.0 26.6 %fusion.1 = f32[512,1024,12]{0,2,1:T(8,128)} fusion(s32[512,1024]{0,1:T(8,128)} %fusion.68, f32[32,12]{0,1:T(8,128)S(1)} %copy-done.75), kind=kOutput, calls=%fused_computation.6 | convolution fusion | flops 2432696320 | bytes 27264512 | tf_op jit(solution)/shard_map/qkb,bh->hqk/dot_general | solution.py:89
  116.5 30.4 %copy.74 = f32[512,1024,12]{1,0,2:T(8,128)} copy(f32[512,1024,12]{0,2,1:T(8,128)} %fusion.1) | data formatting | bytes 50331648 | tf_op jit(solution)/shard_map/qkb,bh->hqk/dot_general | solution.py:89
  146.9 17.0 %fusion.142 = (f32[12,512]{1,0:T(8,128)}, f32[12,512,1024]{2,1,0:T(8,128)}) fusion(f32[512,1024,12]{1,0,2:T(8,128)} %copy.73, bf16[512,12,64]{0,2,1:T(8,128)(2,1)} %bitcast.174, bf16[1024,12,64]{0,2,1:T(8,128)(2,1)S(1)} %bitcast.166, pred[1024]{0:T(1024)(128)(4,1)S(1)} %get-tuple-element.82), kind=kOutput, calls=%fused_computation.197 | convolution fusion | flops 824174592 | bytes 52716544 | tf_op jit(solution)/shard_map/qhd,khd->hqk/dot_general | solution.py:37
  163.9 11.1 %fusion.21 = f32[12,512]{1,0:T(8,128)S(1)} fusion(f32[12,512,1024]{2,1,0:T(8,128)} %get-tuple-element.71, f32[12,512]{1,0:T(8,128)} %get-tuple-element.70), kind=kLoop, calls=%fused_computation.44 | loop fusion | flops 12576768 | bytes 25214976 | tf_op jit(solution)/shard_map/reduce_sum | solution.py:112
  175.0 11.3 %fusion.94 = bf16[12,64,512]{2,1,0:T(8,128)(2,1)} fusion(bf16[1024,12,64]{0,2,1:T(8,128)(2,1)S(1)} %bitcast.181, f32[12,512,1024]{2,1,0:T(8,128)} %get-tuple-element.71, f32[12,512]{1,0:T(8,128)S(1)} %fusion.21, f32[12,512]{1,0:T(8,128)S(1)} %copy-done.42), kind=kOutput, calls=%fused_computation.140 | convolution fusion | flops 824573952 | bytes 27574272 | tf_op jit(solution)/shard_map/hqk,khd->qhd/dot_general | solution.py:114
  186.3 16.9 %fusion.141 = (f32[12,512]{1,0:T(8,128)}, f32[12,512,1024]{2,1,0:T(8,128)}) fusion(f32[512,1024,12]{1,0,2:T(8,128)} %copy.74, bf16[512,12,64]{0,2,1:T(8,128)(2,1)S(1)} %bitcast.172, bf16[1024,12,64]{0,2,1:T(8,128)(2,1)S(1)} %bitcast.167, pred[1024]{0:T(1024)(128)(4,1)S(1)} %get-tuple-element.82), kind=kOutput, calls=%fused_computation.196 | convolution fusion | flops 824174592 | bytes 52716544 | tf_op jit(solution)/shard_map/qhd,khd->hqk/dot_general | solution.py:37
  203.2 11.1 %fusion.22 = f32[12,512]{1,0:T(8,128)S(1)} fusion(f32[12,512,1024]{2,1,0:T(8,128)} %get-tuple-element.69, f32[12,512]{1,0:T(8,128)} %get-tuple-element.68), kind=kLoop, calls=%fused_computation.45 | loop fusion | flops 12576768 | bytes 25214976 | tf_op jit(solution)/shard_map/reduce_sum | solution.py:112
  214.3 11.1 %fusion.93 = bf16[12,64,512]{2,1,0:T(8,128)(2,1)S(1)} fusion(bf16[1024,12,64]{0,2,1:T(8,128)(2,1)S(1)} %bitcast.182, f32[12,512,1024]{2,1,0:T(8,128)} %get-tuple-element.69, f32[12,512]{1,0:T(8,128)S(1)} %fusion.22, f32[12,512]{1,0:T(8,128)S(1)} %copy-done.44), kind=kOutput, calls=%fused_computation.139 | convolution fusion | flops 824573952 | bytes 27574272 | tf_op jit(solution)/shard_map/hqk,khd->qhd/dot_general | solution.py:114
  230.9 8.1 scatter_custom_fusion
  239.0 77.8 %all_to_all.20 = bf16[8,2,128,768]{3,2,1,0:T(8,128)(2,1)S(1)} all-to-all(bf16[8,2,128,768]{3,2,1,0:T(8,128)(2,1)} %bitcast.171), channel_id=1, replica_groups=mesh['dp'=4,'expert'=8] {'expert'}, dimensions={0} | all-to-all | bytes 6291456 | tf_op jit(solution)/shard_map/all_to_all | solution.py:137
  318.5 16.9 %fusion.37 = f32[2,8,128,3072]{3,2,1,0:T(8,128)} fusion(bf16[2,768,3072]{2,1,0:T(8,128)(2,1)} %param.24, bf16[8,2,128,768]{3,2,1,0:T(8,128)(2,1)S(1)} %all_to_all.20), kind=kOutput, calls=%fused_computation.60 | convolution fusion | flops 9663676416 | bytes 37748736 | tf_op jit(solution)/shard_map/semd,edf->semf/dot_general | solution.py:138
  335.4 18.8 %convert_bitcast_fusion.1 = bf16[8,2,128,768]{3,2,0,1:T(8,128)(2,1)S(1)} fusion(bf16[2,3072,768]{2,1,0:T(8,128)(2,1)} %param.25, f32[2,8,128,3072]{3,2,1,0:T(8,128)} %fusion.37), kind=kOutput, calls=%fused_computation.100 | convolution fusion | flops 9721872384 | bytes 37748736 | tf_op jit(solution)/shard_map/semf,efd->semd/dot_general | solution.py:142
  356.2 4.4 all-to-all-start.1
  360.7 2.8 copy.81
  365.1 67.1 %all-to-all-done.1 = bf16[8,2,128,768]{3,2,1,0:T(8,128)(2,1)} async-done(((bf16[8,2,128,768]{3,2,1,0:T(8,128)(2,1)}), bf16[8,2,128,768]{3,2,1,0:T(8,128)(2,1)}, u32[]{:S(2)}, u32[]{:S(2)}) %all-to-all-start.1) | async-done | bytes 3145760 | tf_op jit(solution)/shard_map/all_to_all | solution.py:147
  432.2 7.9 gather_fusion
  440.0 2.7 copy.80
  442.7 3.8 fusion.54
  448.3 7.3 scatter_custom_fusion.1
  455.6 76.4 %all_to_all.21 = bf16[8,2,128,768]{3,2,1,0:T(8,128)(2,1)} all-to-all(bf16[8,2,128,768]{3,2,1,0:T(8,128)(2,1)} %bitcast.170), channel_id=1, replica_groups=mesh['dp'=4,'expert'=8] {'expert'}, dimensions={0} | all-to-all | bytes 6291456 | tf_op jit(solution)/shard_map/all_to_all | solution.py:161
  531.9 23.8 %bitcast_convert_fusion = bf16[2,3072,768]{2,1,0:T(8,128)(2,1)} fusion(bf16[8,2,128,768]{3,2,1,0:T(8,128)(2,1)} %all_to_all.21, f32[2,8,128,3072]{3,2,1,0:T(8,128)} %fusion.37), kind=kOutput, calls=%fused_computation.48 | convolution fusion | flops 9725018112 | bytes 37748736 | tf_op jit(solution)/shard_map/semf,semd->efd/dot_general | solution.py:168
  555.8 30.6 %fusion.14 = bf16[8,2,128,3072]{3,2,0,1:T(8,128)(2,1)} fusion(f32[2,8,128,3072]{3,2,1,0:T(8,128)} %fusion.37, bf16[2,3072,768]{2,1,0:T(8,128)(2,1)} %param.25, bf16[8,2,128,768]{3,2,1,0:T(8,128)(2,1)} %all_to_all.21), kind=kOutput, calls=%fused_computation.22 | convolution fusion | flops 9789505536 | bytes 50331648 | tf_op jit(solution)/shard_map/semd,efd->semf/dot_general | solution.py:171
  586.4 16.3 %convert_bitcast_fusion = bf16[8,2,128,768]{3,2,0,1:T(8,128)(2,1)S(1)} fusion(bf16[8,2,128,3072]{3,2,0,1:T(8,128)(2,1)} %fusion.14, bf16[2,768,3072]{2,1,0:T(8,128)(2,1)} %param.24), kind=kOutput, calls=%fused_computation.97 | convolution fusion | flops 9665249280 | bytes 25165824 | tf_op jit(solution)/shard_map/semf,edf->semd/dot_general | solution.py:178
  604.6 4.4 all-to-all-start.3
  609.1 18.1 %bitcast_convert_fusion.1 = bf16[2,768,3072]{2,1,0:T(8,128)(2,1)} fusion(bf16[8,2,128,768]{3,2,1,0:T(8,128)(2,1)} %copy-done.30, bf16[8,2,128,3072]{3,2,0,1:T(8,128)(2,1)} %fusion.14), kind=kOutput, calls=%fused_computation.49 | convolution fusion | flops 9668395008 | bytes 25165824 | tf_op jit(solution)/shard_map/semd,semf->edf/dot_general | solution.py:175
  629.2 51.4 %all-to-all-done.3 = bf16[8,2,128,768]{3,2,1,0:T(8,128)(2,1)} async-done(((bf16[8,2,128,768]{3,2,1,0:T(8,128)(2,1)}), bf16[8,2,128,768]{3,2,1,0:T(8,128)(2,1)}, u32[]{:S(2)}, u32[]{:S(2)}) %all-to-all-start.3) | async-done | bytes 3145760 | tf_op jit(solution)/shard_map/all_to_all | solution.py:182
  680.6 7.9 gather_fusion.1
  690.6 4.1 multiply_reduce_fusion.2
  694.8 2.8 fusion.55
  700.9 20.9 %multiply_reduce_fusion.1 = (f32[12,512]{1,0:T(8,128)}, f32[12,512,1024]{2,1,0:T(8,128)}) fusion(f32[12,512,1024]{2,1,0:T(8,128)} %get-tuple-element.71, f32[12,512]{1,0:T(8,128)} %log_add_fusion.1, bf16[512,12,64]{0,2,1:T(8,128)(2,1)S(1)} %bitcast.176, bf16[1024,12,64]{0,2,1:T(8,128)(2,1)S(1)} %bitcast.183), kind=kOutput, calls=%fused_computation.38 | convolution fusion | flops 824174592 | bytes 52740096 | tf_op jit(solution)/shard_map/qhd,khd->hqk/dot_general | solution.py:217
  721.8 23.1 %multiply_convert_fusion.1 = bf16[12,512,1024]{2,1,0:T(8,128)(2,1)} fusion(f32[12,512,1024]{2,1,0:T(8,128)} %get-tuple-element.80, f32[12,512,1024]{2,1,0:T(8,128)} %get-tuple-element.71, f32[12,512]{1,0:T(8,128)} %get-tuple-element.79, f32[12,512]{1,0:T(8,128)} %log_add_fusion.1), kind=kLoop, calls=%fused_computation.37 | loop fusion | flops 25165824 | bytes 62963712 | tf_op jit(solution)/shard_map/convert_element_type | solution.py:221
  744.9 9.5 convolution_convert_fusion.5
  754.4 17.3 %multiply_reduce_fusion = (f32[12,512]{1,0:T(8,128)}, f32[12,512,1024]{2,1,0:T(8,128)}) fusion(f32[12,512,1024]{2,1,0:T(8,128)} %get-tuple-element.69, f32[12,512]{1,0:T(8,128)} %log_add_fusion, bf16[512,12,64]{0,2,1:T(8,128)(2,1)} %bitcast.178, bf16[1024,12,64]{0,2,1:T(8,128)(2,1)} %bitcast.180), kind=kOutput, calls=%fused_computation.35 | convolution fusion | flops 824174592 | bytes 52740096 | tf_op jit(solution)/shard_map/qhd,khd->hqk/dot_general | solution.py:217
  771.7 21.6 %multiply_convert_fusion = bf16[12,512,1024]{2,1,0:T(8,128)(2,1)} fusion(f32[12,512,1024]{2,1,0:T(8,128)} %get-tuple-element.78, f32[12,512,1024]{2,1,0:T(8,128)} %get-tuple-element.69, f32[12,512]{1,0:T(8,128)} %get-tuple-element.77, f32[12,512]{1,0:T(8,128)} %log_add_fusion), kind=kLoop, calls=%fused_computation.34 | loop fusion | flops 25165824 | bytes 62963712 | tf_op jit(solution)/shard_map/convert_element_type | solution.py:221
  793.3 8.6 convolution_convert_fusion.4
  802.0 2.8 fusion.98
  805.1 2.8 fusion.100
  807.9 12.1 %fusion.25 = f32[12,64,1024]{2,1,0:T(8,128)} fusion(bf16[512,12,64]{0,2,1:T(8,128)(2,1)S(1)} %bitcast.179, f32[12,512,1024]{2,1,0:T(8,128)} %get-tuple-element.69, f32[12,512]{1,0:T(8,128)S(1)} %copy-done.41), kind=kOutput, calls=%fused_computation.50 | convolution fusion | flops 817889280 | bytes 29122560 | tf_op jit(solution)/shard_map/hqk,qhd->khd/dot_general | solution.py:229
  820.0 13.0 %add_convert_fusion = bf16[12,64,1024]{2,1,0:T(8,128)(2,1)} fusion(f32[12,64,1024]{2,1,0:T(8,128)} %fusion.25, bf16[512,12,64]{0,2,1:T(8,128)(2,1)S(1)} %bitcast.177, f32[12,512,1024]{2,1,0:T(8,128)} %get-tuple-element.71, f32[12,512]{1,0:T(8,128)S(1)} %copy-done.40), kind=kOutput, calls=%fused_computation.92 | convolution fusion | flops 819462144 | bytes 30695424 | tf_op jit(solution)/shard_map/hqk,qhd->khd/dot_general | solution.py:229
  833.1 4.9 fusion.129
  838.0 2.3 fusion.144
  840.4 2.3 add_convert_fusion.1
  843.8 2.9 fusion.131
  847.5 2.6 fusion.126
  850.1 23.3 %copy.90 = bf16[12,512,1024]{1,0,2:T(8,128)(2,1)} copy(bf16[12,512,1024]{2,1,0:T(8,128)(2,1)} %multiply_convert_fusion.1) | data formatting | bytes 25165824 | tf_op jit(solution)/shard_map/convert_element_type | solution.py:221
  873.4 23.1 %copy.91 = bf16[12,512,1024]{1,0,2:T(8,128)(2,1)} copy(bf16[12,512,1024]{2,1,0:T(8,128)(2,1)} %multiply_convert_fusion) | data formatting | bytes 25165824 | tf_op jit(solution)/shard_map/convert_element_type | solution.py:221
  896.5 2.9 copy.95
  899.4 3.0 fusion.99
  904.2 2.1 fusion.50
  908.4 2.7 copy.96
  911.1 12.9 %fusion.95 = f32[32,12]{0,1:T(8,128)S(1)} fusion(bf16[12,512,1024]{1,0,2:T(8,128)(2,1)} %copy.90, s32[512,1024]{0,1:T(8,128)S(1)} %copy-done.18), kind=kOutput, calls=%fused_computation.141 | convolution fusion | flops 419430400 | bytes 14681600 | tf_op jit(solution)/shard_map/hqk,qkb->bh/dot_general | solution.py:232
  924.0 13.6 %fusion.97 = f32[32,12]{0,1:T(8,128)S(1)} fusion(f32[32,12]{0,1:T(8,128)S(1)} %fusion.95, bf16[12,512,1024]{1,0,2:T(8,128)(2,1)} %copy.91, s32[512,1024]{0,1:T(8,128)S(1)} %copy-done.19), kind=kOutput, calls=%fused_computation.143 | convolution fusion | flops 419430784 | bytes 14683136 | tf_op jit(solution)/shard_map/hqk,qkb->bh/dot_general | solution.py:232
  937.7 38.5 %all-reduce = (f32[768]{0:T(1024)}, f32[768]{0:T(1024)}, f32[32,12]{0,1:T(8,128)}, f32[768,16]{0,1:T(8,128)}) all-reduce(f32[768]{0:T(1024)S(1)} %get-tuple-element.50, f32[768]{0:T(1024)S(1)} %copy-done.81, f32[32,12]{0,1:T(8,128)S(1)} %fusion.97, f32[768,16]{0,1:T(8,128)S(1)} %copy-done.46), channel_id=1, replica_groups=mesh['dp'=4,'expert'=8] {'dp','expert'}, use_global_device_ids=true, to_apply=%region_20.21 | all-reduce | flops 14208 | bytes 113664 | tf_op jit(solution)/shard_map/psum | solution.py:264
  976.2 4.2 convert_element_type.315
  980.4 4.2 convert_element_type.313
  984.7 52.3 %all-reduce.4.cloned.1.call-done = (f32[768,768]{1,0:T(8,128)}, f32[768,768]{1,0:T(8,128)}, f32[768,768]{1,0:T(8,128)}, f32[768,768]{1,0:T(8,128)}) async-done(((f32[768,768]{1,0:T(8,128)}, f32[768,768]{1,0:T(8,128)}, f32[768,768]{1,0:T(8,128)}, f32[768,768]{1,0:T(8,128)}), (f32[768,768]{1,0:T(8,128)}, f32[768,768]{1,0:T(8,128)}, f32[768,768]{1,0:T(8,128)}, ...) | async-done | bytes 9437200 | tf_op jit(solution)/shard_map/psum | solution.py:264
  1037.0 3.4 copy.124
  (252 shorter events, 44.2 us)
Async XLA Ops:
  8.0 21.5 %copy-start = (bf16[768,768]{1,0:T(8,128)(2,1)S(1)}, bf16[768,768]{1,0:T(8,128)(2,1)}, u32[]{:S(2)}) copy-start(bf16[768,768]{1,0:T(8,128)(2,1)} %param.20) | copy-start | bytes 3538948
  10.5 11.7 %copy-start.76 = (f32[768]{0:T(1024)S(1)}, f32[768]{0:T(1024)}, u32[]{:S(2)}) copy-start(f32[768]{0:T(1024)} %param.16) | copy-start | bytes 9220
  21.1 4.0 copy-start.5
  22.2 7.2 copy-start.65
  22.3 3.9 copy-start.89
  26.2 160.1 %copy-start.20 = (bf16[512,768]{0,1:T(8,128)(2,1)}, bf16[512,768]{0,1:T(8,128)(2,1)S(1)}, u32[]{:S(2)}) copy-start(bf16[512,768]{0,1:T(8,128)(2,1)S(1)} %get-tuple-element.67) | copy-start | bytes 2359300
  26.2 3.3 copy-start.6
  29.5 156.8 %copy-start.3 = (bf16[1024,768]{0,1:T(8,128)(2,1)}, bf16[1024,768]{0,1:T(8,128)(2,1)S(1)}, u32[]{:S(2)}) copy-start(bf16[1024,768]{0,1:T(8,128)(2,1)S(1)} %convolution_convert_fusion.1) | copy-start | bytes 4718596
  29.5 6.2 copy-start.75
  32.2 3.5 copy-start.17
  163.9 11.1 %copy-start.24 = (bf16[1024,768]{0,1:T(8,128)(2,1)S(1)}, bf16[1024,768]{0,1:T(8,128)(2,1)}, u32[]{:S(2)}) copy-start(bf16[1024,768]{0,1:T(8,128)(2,1)} %convolution_convert_fusion.3) | copy-start | bytes 4718596
  163.9 11.1 %copy-start.42 = (f32[12,512]{1,0:T(8,128)S(1)}, f32[12,512]{1,0:T(8,128)}, u32[]{:S(2)}) copy-start(f32[12,512]{1,0:T(8,128)} %get-tuple-element.70) | copy-start | bytes 73732
  175.0 11.3 %copy-start.49 = (f32[12,512]{1,0:T(8,128)}, f32[12,512]{1,0:T(8,128)S(1)}, u32[]{:S(2)}) copy-start(f32[12,512]{1,0:T(8,128)S(1)} %fusion.21) | copy-start | bytes 73732
  203.2 11.1 %copy-start.25 = (bf16[1024,768]{0,1:T(8,128)(2,1)S(1)}, bf16[1024,768]{0,1:T(8,128)(2,1)}, u32[]{:S(2)}) copy-start(bf16[1024,768]{0,1:T(8,128)(2,1)} %convolution_convert_fusion.3) | copy-start | bytes 4718596
  203.2 11.1 %copy-start.44 = (f32[12,512]{1,0:T(8,128)S(1)}, f32[12,512]{1,0:T(8,128)}, u32[]{:S(2)}) copy-start(f32[12,512]{1,0:T(8,128)} %get-tuple-element.68) | copy-start | bytes 73732
  214.3 11.2 %copy-start.51 = (f32[12,512]{1,0:T(8,128)}, f32[12,512]{1,0:T(8,128)S(1)}, u32[]{:S(2)}) copy-start(f32[12,512]{1,0:T(8,128)S(1)} %fusion.22) | copy-start | bytes 73732
  214.3 11.2 %copy-start.7 = (bf16[1024,768]{0,1:T(8,128)(2,1)S(1)}, bf16[1024,768]{0,1:T(8,128)(2,1)}, u32[]{:S(2)}) copy-start(bf16[1024,768]{0,1:T(8,128)(2,1)} %copy-done.5) | copy-start | bytes 4718596
  214.3 11.2 %copy-start.87 = (bf16[768,768]{1,0:T(8,128)(2,1)S(1)}, bf16[768,768]{1,0:T(8,128)(2,1)}, u32[]{:S(2)}) copy-start(bf16[768,768]{1,0:T(8,128)(2,1)} %param.21) | copy-start | bytes 3538948
  214.3 11.2 %copy-start.91 = (bf16[12,64,512]{2,1,0:T(8,128)(2,1)S(1)}, bf16[12,64,512]{2,1,0:T(8,128)(2,1)}, u32[]{:S(2)}) copy-start(bf16[12,64,512]{2,1,0:T(8,128)(2,1)} %fusion.94) | copy-start | bytes 2359300
  225.5 3.4 copy-start.55
  225.5 3.4 copy-start.71
  227.2 3.7 copy-start.61
  229.3 134.2 %copy-start.10 = (bf16[1024,768]{0,1:T(8,128)(2,1)}, bf16[1024,768]{0,1:T(8,128)(2,1)S(1)}, u32[]{:S(2)}) copy-start(bf16[1024,768]{0,1:T(8,128)(2,1)S(1)} %multiply_convert_fusion.3) | copy-start | bytes 4718596
  356.2 76.0 %all-to-all-start.1 = ((bf16[8,2,128,768]{3,2,1,0:T(8,128)(2,1)}), bf16[8,2,128,768]{3,2,1,0:T(8,128)(2,1)}, u32[]{:S(2)}, u32[]{:S(2)}) async-start(bf16[8,2,128,768]{3,2,1,0:T(8,128)(2,1)} %copy.79), calls=%async_computation.1 | async-start | bytes 6291456 | tf_op jit(solution)/shard_map/all_to_all | solution.py:147
  360.6 2.9 copy-start.57
  360.6 3.8 copy-start.47
  360.6 615.6 %reduce-scatter.5.cloned.1.call-start = ((), (), s32[]{:S(2)}) async-start(), calls=%async_computation.7 | async-start | bytes 11796480 | tf_op jit(solution)/shard_map/reduce_scatter | solution.py:281
  365.0 77.7 %copy-start.63 = (f32[1024]{0:T(1024)}, f32[1024]{0:T(1024)S(1)}, u32[]{:S(2)}) copy-start(f32[1024]{0:T(1024)S(1)} %fusion.107) | copy-start | bytes 12292
  365.1 67.1 %copy-start.73 = (s32[1024]{0:T(1024)}, s32[1024]{0:T(1024)S(1)}, u32[]{:S(2)}) copy-start(s32[1024]{0:T(1024)S(1)} %broadcast_clamp_fusion) | copy-start | bytes 12292
  604.6 76.0 %all-to-all-start.3 = ((bf16[8,2,128,768]{3,2,1,0:T(8,128)(2,1)}), bf16[8,2,128,768]{3,2,1,0:T(8,128)(2,1)}, u32[]{:S(2)}, u32[]{:S(2)}) async-start(bf16[8,2,128,768]{3,2,1,0:T(8,128)(2,1)} %copy.84), calls=%async_computation.3 | async-start | bytes 6291456 | tf_op jit(solution)/shard_map/all_to_all | solution.py:182
  609.0 371.4 %reduce-scatter.3.cloned.1.call-start = ((), (), s32[]{:S(2)}) async-start(), calls=%async_computation.6 | async-start | bytes 11796480 | tf_op jit(solution)/shard_map/reduce_scatter | solution.py:278
  627.2 53.4 %copy-start.74 = (s32[1024]{0:T(1024)S(1)}, s32[1024]{0:T(1024)}, u32[]{:S(2)}) copy-start(s32[1024]{0:T(1024)} %copy-done.73) | copy-start | bytes 12292
  627.2 409.7 %all-reduce.4.cloned.1.call-start = ((), (), s32[]{:S(2)}) async-start(), calls=%async_computation.8 | async-start | bytes 18874368 | tf_op jit(solution)/shard_map/psum | solution.py:264
  629.2 61.2 %copy-start.69 = (f32[1024]{0:T(1024)}, f32[1024]{0:T(1024)S(1)}, u32[]{:S(2)}) copy-start(f32[1024]{0:T(1024)S(1)} %mul.297) | copy-start | bytes 12292
  690.5 4.2 copy-start.83
  690.5 4.2 copy-start.2
  690.6 4.2 copy-start.12
  690.6 4.2 copy-start.13
  721.8 23.1 %copy-start.4 = (bf16[1024,768]{0,1:T(8,128)(2,1)S(1)}, bf16[1024,768]{0,1:T(8,128)(2,1)}, u32[]{:S(2)}) copy-start(bf16[1024,768]{0,1:T(8,128)(2,1)} %copy-done.3) | copy-start | bytes 4718596
  793.3 8.7 copy-start.8
  793.3 8.7 copy-start.37
  793.3 8.7 copy-start.66
  793.3 8.7 copy-start.77
  801.9 2.9 copy-start.39
  802.0 2.9 copy-start.15
  802.0 2.9 copy-start.92
  802.0 3.0 copy-start.94
  807.9 12.2 %copy-start.40 = (f32[12,512]{1,0:T(8,128)S(1)}, f32[12,512]{1,0:T(8,128)}, u32[]{:S(2)}) copy-start(f32[12,512]{1,0:T(8,128)} %log_add_fusion.1) | copy-start | bytes 73732
  807.9 30.1 %slice-start.3 = ((s8[12582912]{0:T(1024)(128)(4,1)}), s8[4194304]{0:T(1024)(128)(4,1)S(1)}, s32[]{:S(2)}) async-start(s8[12582912]{0:T(1024)(128)(4,1)} %bitcast.164), calls=%async_computation.12 | async-start | bytes 8388608
  807.9 30.0 %slice-start.4 = ((s8[12582912]{0:T(1024)(128)(4,1)}), s8[4194304]{0:T(1024)(128)(4,1)S(1)}, s32[]{:S(2)}) async-start(s8[12582912]{0:T(1024)(128)(4,1)} %bitcast.164), calls=%async_computation.13 | async-start | bytes 8388608
  820.0 13.0 %copy-start.78 = (f32[768]{0:T(1024)S(1)}, f32[768]{0:T(1024)}, u32[]{:S(2)}) copy-start(f32[768]{0:T(1024)} %param.16) | copy-start | bytes 9220
  820.0 17.9 %slice-start.5 = ((s8[12582912]{0:T(1024)(128)(4,1)}), s8[4194304]{0:T(1024)(128)(4,1)S(1)}, s32[]{:S(2)}) async-start(s8[12582912]{0:T(1024)(128)(4,1)} %bitcast.164), calls=%async_computation.14 | async-start | bytes 8388608
  833.0 4.9 copy-start.22
  833.0 7.2 slice-start
  833.0 7.2 slice-start.1
  840.3 3.5 copy-start.9
  840.3 3.5 copy-start.79
  896.5 2.9 copy-start.38
  899.4 3.0 copy-start.29
  899.4 3.0 copy-start.90
  911.1 12.9 %copy-start.19 = (s32[512,1024]{0,1:T(8,128)S(1)}, s32[512,1024]{0,1:T(8,128)}, u32[]{:S(2)}) copy-start(s32[512,1024]{0,1:T(8,128)} %fusion.68) | copy-start | bytes 6291460
  924.0 13.7 %copy-start.46 = (f32[768,16]{0,1:T(8,128)S(1)}, f32[768,16]{0,1:T(8,128)}, u32[]{:S(2)}) copy-start(f32[768,16]{0,1:T(8,128)} %fusion.126) | copy-start | bytes 147460
  924.0 13.7 %copy-start.81 = (f32[768]{0:T(1024)S(1)}, f32[768]{0:T(1024)}, u32[]{:S(2)}) copy-start(f32[768]{0:T(1024)} %get-tuple-element.48) | copy-start | bytes 9220
  1037.0 3.4 copy-start.33
  (42 other events, 75.2 us)
Sparse Core Ops, SparseCore 0:
  555.9 93.9 reduce-scatter.4
  653.3 94.9 reduce-scatter.2
Sparse Core Ops, SparseCore 1:
  846.8 190.1 all-reduce.3
where the time goes:
time: 1060 us; the launch traced here: 1050 us
  matrix products  383 us (36%)
  blocking collectives  193 us (18%)
  local copies, waits for them, and re-layouts  182 us (17%)
  waiting for transfers between devices  171 us (16%)
  other arithmetic  99.8 us (9%)
  between operations  17.7 us (2%)
    all_to_all x1, blocking collectives, body(): lax.all_to_all(send_rows, 'expert', split_axis=0, concat_axis=0, tiled=True)  77.8 us
    all_to_all x1, blocking collectives, body(): lax.all_to_all(grad_send, 'expert', split_axis=0, concat_axis=0, tiled=True)  76.4 us
    all_to_all x1, waiting for transfers between devices, body(): lax.all_to_all(produced, 'expert', split_axis=0, concat_axis=0, tiled=True)  67.1 us
    dot_general x2, local copies, waits for them, and re-layouts, body(): jnp.einsum('qkb,bh->hqk', table_hot, bias_table, precision=HIGHEST, prefe...  60.8 us
    psum x1, waiting for transfers between devices, body(): lax.psum((grad_query_weight, grad_key_weight, grad_value_weight, grad_out...  52.3 us
    all_to_all x1, waiting for transfers between devices, body(): lax.all_to_all(grad_piece, 'expert', split_axis=0, concat_axis=0, tiled=T...  51.4 us
    dot_general x2, matrix products, body(): jnp.einsum('qkb,bh->hqk', table_hot, bias_table, precision=HIGHEST, prefe...  50.5 us
    convert_element_type x2, local copies, waits for them, and re-layouts, body(): grad_scores = (attn_probs * (grad_probs - inner_sum)).astype(jnp.bfloat16)  46.4 us
  transfers between devices with their start and end apart: 5, of which 3 were waited for; matrix products, arithmetic and copies ran while one was open for 32% of the time, Pallas kernels for 0%

commit v1 on v0

v1 whole, which is shorter than its diff:
```python
import functools

import jax
import jax.numpy as jnp
from jax import lax
from jax.experimental import pallas as pl
from jax.experimental.pallas import tpu as pltpu
from jax.sharding import PartitionSpec as P

BF = jnp.bfloat16
F32 = jnp.float32
I32 = jnp.int32
EPSILON = 1e-06
THRESHOLDS = (12, 16, 23, 32, 46, 64, 91)
HIGHEST = lax.Precision.HIGHEST
SUB = 128
WIDE = 512
QT = 256
RB = 256
BIG = 56 * 2**20
GELU_C = 0.7978845608028654
GELU_A = 0.044715


def bucket_of(offsets):
    distance = jnp.abs(offsets)
    distant = 8 + sum(((distance >= limit).astype(I32) for limit in THRESHOLDS))
    nearby = jnp.where(distance < 8, distance, distant)
    return nearby + 16 * (offsets > 0).astype(I32)


def dot(a, b):
    return lax.dot_general(a, b, (((1,), (0,)), ((), ())), preferred_element_type=F32)


def dot_nt(a, b):
    return lax.dot_general(a, b, (((1,), (1,)), ((), ())), preferred_element_type=F32)


def dot_tn(a, b):
    return lax.dot_general(a, b, (((0,), (0,)), ((), ())), preferred_element_type=F32)


def iota(shape, dim):
    return lax.broadcasted_iota(I32, shape, dim)


SMEM = pl.BlockSpec(memory_space=pltpu.SMEM)


def whole(*shape):
    return pl.BlockSpec(shape, lambda *i: (0,) * len(shape))


def rows_of(width):
    return pl.BlockSpec((RB, width), lambda i: (i, 0))


def struct(shape, kind):
    return jax.ShapeDtypeStruct(shape, kind)


def call(kernel, name, grid, in_specs, out_specs, out_shape, scratch=(), flops=0, moved=0, transcendentals=0):
    return pl.pallas_call(
        kernel,
        grid=grid,
        in_specs=in_specs,
        out_specs=out_specs,
        out_shape=out_shape,
        scratch_shapes=list(scratch),
        compiler_params=pltpu.CompilerParams(vmem_limit_bytes=BIG),
        cost_estimate=pl.CostEstimate(flops=int(flops), bytes_accessed=int(moved), transcendentals=int(transcendentals)),
        name=name,
    )


def slots_kernel(local, most, experts, row_ref, col_ref, srow_ref, scol_ref):
    L = row_ref.shape[1]
    route_r = row_ref[...]
    route_c = col_ref[...]
    hot_r = (iota((experts, L), 0) == route_r).astype(F32)
    hot_c = (iota((L, experts), 1) == route_c).astype(F32)
    upper = (iota((L, L), 0) < iota((L, L), 1)).astype(F32).astype(BF)
    lower = (iota((L, L), 1) < iota((L, L), 0)).astype(F32).astype(BF)
    rank_r = jnp.sum(dot(hot_r.astype(BF), upper) * hot_r, axis=0, keepdims=True).astype(I32)
    rank_c = jnp.sum(dot(lower, hot_c.astype(BF)) * hot_c, axis=1, keepdims=True).astype(I32)
    slot_r = (route_r // local) * most + rank_r
    slot_c = (route_c // local) * most + rank_c
    lane = iota((L, 128), 1)
    out_c = jnp.full((L, 128), -1, I32)
    for e in range(local):
        srow_ref[e:e + 1, :] = jnp.where(route_r % local == e, slot_r, -1)
        out_c = jnp.where((lane == e) & (route_c % local == e), slot_c, out_c)
    scol_ref[...] = out_c


def dispatch_rows(srow, values, rows):
    hot = (iota((rows, srow.shape[1]), 0) == srow).astype(F32).astype(BF)
    return dot(hot, values).astype(BF)


def cotangent_kernel(local, len_ref, srow_ref, cot_ref, *out_refs):
    L = cot_ref.shape[0]
    live = iota((L, 1), 0) < len_ref[0]
    values = jnp.where(live, cot_ref[...].astype(F32), 0.0).astype(BF)
    for e in range(local):
        out_refs[e][...] = dispatch_rows(srow_ref[e:e + 1, :], values, out_refs[e].shape[0])


def rms_scale(v):
    return lax.rsqrt(jnp.mean(v * v, axis=1, keepdims=True) + EPSILON)


def project_kernel(x_ref, gain_ref, wq_ref, wk_ref, wv_ref, h_ref, qkv_ref):
    D = x_ref.shape[1]
    x = x_ref[...].astype(F32)
    h = (x * rms_scale(x) * gain_ref[...]).astype(BF)
    h_ref[...] = h
    for n, w_ref in enumerate((wq_ref, wk_ref, wv_ref)):
        qkv_ref[:, n * D:(n + 1) * D] = dot(h, w_ref[...]).astype(BF)


def post_kernel(len_ref, x_ref, o_ref, wo_ref, gain_ref, middle_ref, h_ref):
    r = pl.program_id(0)
    middle = x_ref[...].astype(F32) + dot(o_ref[...], wo_ref[...])
    middle_ref[...] = middle
    live = iota((RB, 1), 0) + r * RB < len_ref[0]
    h = middle * rms_scale(middle) * gain_ref[...]
    h_ref[...] = jnp.where(live, h, 0.0).astype(BF)


def dispatch_kernel(e, srow_ref, h_ref, out_ref):
    out_ref[...] = dispatch_rows(srow_ref[e:e + 1, :], h_ref[...], out_ref.shape[0])


def expert_kernel(hot_ref, h_ref, g_ref, w1_ref, w2_ref, wr_ref, rows_ref, back_ref, d1_ref, d2_ref, dr_ref,
                  ht_s, gr_s, gate_s, act_s, gp_s, rows_s, sent_s):
    f = pl.program_id(0)
    last = pl.num_programs(0) - 1
    S = h_ref.shape[0]

    @pl.when(f == 0)
    def _():
        h = h_ref[...]
        ht_s[...] = h.T
        logits = dot(h, wr_ref[...])
        top = jnp.max(logits, axis=1, keepdims=True)
        ex = jnp.exp(logits - top)
        probs = ex / jnp.sum(ex, axis=1, keepdims=True)
        gate = jnp.sum(probs * hot_ref[...], axis=1, keepdims=True)
        gate_s[...] = jnp.broadcast_to(gate, gate_s.shape)
        gr_s[...] = (gate * g_ref[...].astype(F32)).astype(BF)

    w1 = w1_ref[0]
    w2 = w2_ref[0]
    for c in range(S // RB):
        sl = slice(c * RB, (c + 1) * RB)
        v = dot(h_ref[sl], w1)
        ga = dot_nt(gr_s[sl], w2)
        v2 = v * v
        t = jnp.tanh(v * (GELU_C + (GELU_C * GELU_A) * v2))
        half = 0.5 + 0.5 * t
        act = v * half
        slope = half + 2.0 * act * (1.0 - half) * (GELU_C + (3.0 * GELU_C * GELU_A) * v2)
        actb = act.astype(BF)
        gpre = (ga * slope).astype(BF)
        act_s[sl] = actb
        gp_s[sl] = gpre
        r = dot(actb, w2)
        s = dot_nt(gpre, w1)

        @pl.when(f == 0)
        def _():
            rows_s[sl] = r
            sent_s[sl] = s

        @pl.when(f > 0)
        def _():
            rows_s[sl] += r
            sent_s[sl] += s

    d1_ref[0] = dot(ht_s[...], gp_s[...]).astype(BF)
    d2_ref[0] = dot_tn(act_s[...], gr_s[...]).astype(BF)

    @pl.when(f == last)
    def _():
        rows = rows_s[...].astype(BF).astype(F32)
        gate = gate_s[:, :1]
        rows_ref[...] = (gate * rows).astype(BF)
        grad_gate = jnp.sum(rows * g_ref[...].astype(F32), axis=1, keepdims=True)
        logits = dot(h_ref[...], wr_ref[...])
        top = jnp.max(logits, axis=1, keepdims=True)
        ex = jnp.exp(logits - top)
        probs = ex / jnp.sum(ex, axis=1, keepdims=True)
        gl = (grad_gate * gate * (hot_ref[...] - probs)).astype(BF)
        dr_ref[...] = dot(ht_s[...], gl)
        back_ref[...] = (sent_s[...] + dot_nt(gl, wr_ref[...])).astype(BF)


def experts_run(e, parts, hot, h, g, first, second, router):
    S, D = h.shape
    FF = first.shape[2]
    FT = FF // parts
    E = router.shape[1]
    return call(
        expert_kernel, "experts", (parts,),
        [whole(1, E), whole(S, D), whole(S, D), pl.BlockSpec((1, D, FT), lambda f: (e, 0, f)), pl.BlockSpec((1, FT, D), lambda f: (e, f, 0)), whole(D, E)],
        [whole(S, D), whole(S, D), pl.BlockSpec((1, D, FT), lambda f: (f, 0, 0)), pl.BlockSpec((1, FT, D), lambda f: (f, 0, 0)), whole(D, E)],
        [struct((S, D), BF), struct((S, D), BF), struct((parts, D, FT), BF), struct((parts, FT, D), BF), struct((D, E), F32)],
        [pltpu.VMEM((D, S), BF), pltpu.VMEM((S, D), BF), pltpu.VMEM((S, 128), F32), pltpu.VMEM((S, FT), BF), pltpu.VMEM((S, FT), BF), pltpu.VMEM((S, D), F32), pltpu.VMEM((S, D), F32)],
        flops=12 * S * D * FF, moved=8 * D * FF + 8 * S * D, transcendentals=S * FF,
    )(hot, h, g, first, second, router)


def norm_back(v, gain, upstream):
    r = rms_scale(v)
    w = upstream * gain
    grad = r * w - v * (r * r * r) * jnp.mean(v * w, axis=1, keepdims=True)
    return grad, v * r * upstream


def combine_hot(scol, slots, e):
    return (iota((scol.shape[0], slots), 1) == scol[:, e:e + 1]).astype(F32).astype(BF)


def combine_kernel(local, len_ref, scol_ref, *refs):
    backs = refs[:local]
    middle_ref, cot_ref, o_ref, inv_ref, wo_ref, gain_ref, gm_ref, do_ref, dwo_ref, gain_out, acc_s, gain_s = refs[local:]
    r = pl.program_id(0)
    scol = scol_ref[...]
    gh = sum(dot(combine_hot(scol, b.shape[0], e), b[...]) for e, b in enumerate(backs))
    live = iota((RB, 1), 0) + r * RB < len_ref[0]
    up = jnp.where(live, gh, 0.0)
    gv, gg = norm_back(middle_ref[...], gain_ref[...], up)
    gm = jnp.where(live, cot_ref[...].astype(F32), 0.0) + gv
    gm_ref[...] = gm
    gb = gm.astype(BF)
    do_ref[...] = (dot_nt(gb, wo_ref[...]) * inv_ref[...]).astype(BF)
    dw = dot_tn(o_ref[...], gb)
    gs = jnp.sum(gg, axis=0, keepdims=True)

    @pl.when(r == 0)
    def _():
        acc_s[...] = dw
        gain_s[...] = gs

    @pl.when(r > 0)
    def _():
        acc_s[...] += dw
        gain_s[...] += gs

    @pl.when(r == pl.num_programs(0) - 1)
    def _():
        dwo_ref[...] = acc_s[...].astype(BF)
        gain_out[...] = gain_s[...]


def weights_kernel(h_ref, dq_ref, dk_ref, dv_ref, out_ref, acc_s):
    r = pl.program_id(0)
    D = h_ref.shape[1]
    h = h_ref[...]
    for n, ref in enumerate((dq_ref, dk_ref, dv_ref)):
        dw = dot_tn(h, ref[...])
        sl = slice(n * D, (n + 1) * D)

        @pl.when(r == 0)
        def _():
            acc_s[:, sl] = dw

        @pl.when(r > 0)
        def _():
            acc_s[:, sl] += dw

    @pl.when(r == pl.num_programs(0) - 1)
    def _():
        out_ref[...] = acc_s[...].astype(BF)


def tokens_kernel(x_ref, gain_ref, dq_ref, dk_ref, dv_ref, wq_ref, wk_ref, wv_ref, gm_ref, out_ref, gain_out):
    r = pl.program_id(0)
    gh = dot_nt(dq_ref[...], wq_ref[...]) + dot_nt(dk_ref[...], wk_ref[...]) + dot_nt(dv_ref[...], wv_ref[...])
    gv, gg = norm_back(x_ref[...].astype(F32), gain_ref[...], gh)
    out_ref[...] = (gm_ref[...] + gv).astype(BF)
    gs = jnp.sum(gg, axis=0, keepdims=True)

    @pl.when(r == 0)
    def _():
        gain_out[...] = gs

    @pl.when(r > 0)
    def _():
        gain_out[...] += gs


def mixed_kernel(local, len_ref, scol_ref, *refs):
    rows = refs[:local]
    middle_ref, out_ref = refs[local:]
    r = pl.program_id(0)
    scol = scol_ref[...]
    got = sum(dot(combine_hot(scol, b.shape[0], e), b[...]) for e, b in enumerate(rows))
    live = iota((RB, 1), 0) + r * RB < len_ref[0]
    out_ref[...] = jnp.where(live, middle_ref[...] + got, 0.0).astype(BF)


def near_bias(w_row):
    full = jnp.broadcast_to(w_row, (SUB, 512))
    return pltpu.roll(full, 0, 1, stride=1, stride_axis=0)[:, :384]


def attn_fwd_kernel(len_ref, far_ref, q_ref, k_ref, v_ref, w_ref, o_ref, inv_ref, p_ref):
    L = q_ref.shape[0]
    nb = L // SUB
    pair = pl.program_id(0)
    seq_len = len_ref[0]
    q = q_ref[...]
    k = k_ref[...]
    v = v_ref[...]
    lane = iota((L, 128), 1)
    row = iota((L, 128), 0)
    blk = row // SUB
    outs = []
    for a in range(2):
        head = 2 * pair + a
        own = (lane < 64) if a == 0 else (lane >= 64)
        base = 64 if a == 0 else 0
        al = lane - base
        c_left = far_ref[0, head]
        c_right = far_ref[1, head]
        kb = al % 8
        val = jnp.where(kb <= blk - 2, c_left, jnp.where(kb >= blk + 2, c_right, 0.0))
        hi = val.astype(BF).astype(F32)
        r1 = val - hi
        mid = r1.astype(BF).astype(F32)
        lo = r1 - mid
        qaug = jnp.where(al < 8, hi, jnp.where(al < 16, mid, jnp.where(al < 24, lo, jnp.where(al == 24, 1.0, 0.0)))).astype(BF)
        kaug = jnp.where(al < 24, (kb == blk).astype(F32), jnp.where((al == 24) & (row >= seq_len), -1e30, 0.0)).astype(BF)
        qa = jnp.where(own, q, qaug)
        ka = jnp.where(own, k, kaug)
        va = jnp.where(own, v, jnp.ones_like(v))
        near = near_bias(w_ref[0, a:a + 1, :])
        parts = []
        for t in range(L // QT):
            s = dot_nt(qa[t * QT:(t + 1) * QT], ka)
            rows = []
            for u in range(QT // SUB):
                b = t * (QT // SUB) + u
                lo_b, hi_b = max(b - 1, 0), min(b + 2, nb)
                su = s[u * SUB:(u + 1) * SUB]
                pieces = []
                if lo_b > 0:
                    pieces.append(su[:, :lo_b * SUB])
                pieces.append(su[:, lo_b * SUB:hi_b * SUB] + near[:, (lo_b - b + 1) * SUB:(hi_b - b + 1) * SUB])
                if hi_b < nb:
                    pieces.append(su[:, hi_b * SUB:])
                rows.append(jnp.concatenate(pieces, axis=1))
            s = jnp.concatenate(rows, axis=0)
            m = jnp.max(s, axis=1, keepdims=True)
            p = jnp.exp(s - m).astype(BF)
            p_ref[a, t * QT:(t + 1) * QT, :] = p
            parts.append(dot(p, va))
        outs.append(jnp.concatenate(parts, axis=0))
    first = lane < 64
    num = jnp.where(first, outs[0], outs[1])
    den = pltpu.roll(jnp.where(first, outs[1], outs[0]), 64, 1)
    inv = 1.0 / den
    inv_ref[...] = inv
    o_ref[...] = (num * inv).astype(BF)


def attn_fwd(lengths, far, qkv, w):
    L = qkv.shape[0]
    D = qkv.shape[1] // 3
    pairs = D // 128
    blk = lambda off: pl.BlockSpec((L, 128), lambda i, off=off: (0, off + i))
    return pl.pallas_call(
        attn_fwd_kernel,
        grid=(pairs,),
        in_specs=[SMEM, SMEM, blk(0), blk(pairs), blk(2 * pairs), pl.BlockSpec((1, 2, 512), lambda i: (i, 0, 0))],
        out_specs=[pl.BlockSpec((L, 128), lambda i: (0, i)), pl.BlockSpec((L, 128), lambda i: (0, i)), pl.BlockSpec((2, L, L), lambda i: (i, 0, 0))],
        out_shape=[jax.ShapeDtypeStruct((L, D), BF), jax.ShapeDtypeStruct((L, D), F32), jax.ShapeDtypeStruct((2 * pairs, L, L), BF)],
        compiler_params=pltpu.CompilerParams(vmem_limit_bytes=BIG),
        cost_estimate=pl.CostEstimate(flops=4 * 2 * pairs * L * L * 256, bytes_accessed=2 * pairs * L * L * 2 + 12 * L * D, transcendentals=2 * pairs * L * L),
        name="attention_forward",
    )(lengths, far, qkv, qkv, qkv, w)


def attn_bwd_kernel(q_ref, k_ref, v_ref, do_ref, o_ref, p_ref, dq_ref, dk_ref, dv_ref, near_ref, blk_ref):
    L = q_ref.shape[0]
    nb = L // SUB
    q = q_ref[...]
    k = k_ref[...]
    v = v_ref[...]
    do = do_ref[...]
    lane = iota((L, 128), 1)
    row = iota((L, 128), 0)
    blk = row // SUB
    prod = do.astype(F32) * o_ref[...].astype(F32)
    zero = jnp.zeros_like(q)
    dk = dv = None
    dqs = []
    for a in range(2):
        own = (lane < 64) if a == 0 else (lane >= 64)
        base = 64 if a == 0 else 0
        al = lane - base
        inner = jnp.sum(jnp.where(own, prod, 0.0), axis=1, keepdims=True)
        hi = inner.astype(BF)
        lo = (inner - hi.astype(F32)).astype(BF)
        doa = jnp.where(own, do, jnp.where(al == 0, hi, jnp.where(al == 1, lo, zero)))
        va = jnp.where(own, v, jnp.where((al == 0) | (al == 1), -1.0, 0.0).astype(BF))
        ka = jnp.where(own, k, (al == blk).astype(F32).astype(BF))
        qm = jnp.where(own, q, zero)
        dom = jnp.where(own, do, zero)
        near = None
        dq = []
        dsl = []
        for t in range(L // QT):
            sl = slice(t * QT, (t + 1) * QT)
            x = dot_nt(doa[sl], va)
            pt = p_ref[a, sl, :]
            dsf = pt.astype(F32) * x
            ds = dsf.astype(BF)
            dq.append(dot(ds, ka))
            ck = dot_tn(ds, qm[sl])
            cv = dot_tn(pt, dom[sl])
            dk = ck if dk is None else dk + ck
            dv = cv if dv is None else dv + cv
            for u in range(QT // SUB):
                b = t * (QT // SUB) + u
                pieces = []
                if b == 0:
                    pieces.append(jnp.zeros((SUB, SUB), F32))
                lo_b, hi_b = max(b - 1, 0), min(b + 2, nb)
                pieces.append(dsf[u * SUB:(u + 1) * SUB, lo_b * SUB:hi_b * SUB])
                if b == nb - 1:
                    pieces.append(jnp.zeros((SUB, SUB), F32))
                piece = jnp.concatenate(pieces, axis=1) if len(pieces) > 1 else pieces[0]
                near = piece if near is None else near + piece
        dq = jnp.concatenate(dq, axis=0)
        dqs.append(dq)
        far = pltpu.roll(dq, 64, 1) if a == 0 else dq
        left = jnp.sum(jnp.where((lane < 8) & (lane <= blk - 2), far, 0.0), axis=0, keepdims=True)
        right = jnp.sum(jnp.where((lane < 8) & (lane >= blk + 2), far, 0.0), axis=0, keepdims=True)
        blk_ref[0, a, 0:1, :] = left
        blk_ref[0, a, 1:2, :] = right
        full = jnp.concatenate([near, jnp.zeros((SUB, 128), F32)], axis=1)
        rows = SUB
        while rows > 8:
            rows //= 2
            full = full[:rows] + pltpu.roll(full[rows:], 512 - rows, 1)
        line = iota((8, 512), 0)
        for step in (4, 2, 1):
            full = jnp.where((line & step) > 0, pltpu.roll(full, 512 - step, 1), full)
        diag = jnp.sum(full, axis=0, keepdims=True)
        near_ref[0, a:a + 1, :] = diag
    dq_ref[...] = jnp.where(lane < 64, dqs[0], dqs[1]).astype(BF)
    dk_ref[...] = dk.astype(BF)
    dv_ref[...] = dv.astype(BF)


def attn_bwd(qkv, do, o, p):
    L = qkv.shape[0]
    D = qkv.shape[1] // 3
    pairs = D // 128
    blk = lambda off: pl.BlockSpec((L, 128), lambda i, off=off: (0, off + i))
    return pl.pallas_call(
        attn_bwd_kernel,
        grid=(pairs,),
        in_specs=[blk(0), blk(pairs), blk(2 * pairs), blk(0), blk(0), pl.BlockSpec((2, L, L), lambda i: (i, 0, 0))],
        out_specs=[blk(0), blk(0), blk(0), pl.BlockSpec((1, 2, 512), lambda i: (i, 0, 0)), pl.BlockSpec((1, 2, 2, 128), lambda i: (i, 0, 0, 0))],
        out_shape=[jax.ShapeDtypeStruct((L, D), BF)] * 3 + [jax.ShapeDtypeStruct((pairs, 2, 512), F32), jax.ShapeDtypeStruct((pairs, 2, 2, 128), F32)],
        compiler_params=pltpu.CompilerParams(vmem_limit_bytes=BIG),
        cost_estimate=pl.CostEstimate(flops=8 * 2 * pairs * L * L * 256, bytes_accessed=2 * pairs * L * L * 2 + 12 * L * D, transcendentals=0),
        name="attention_backward",
    )(qkv, qkv, qkv, do, o, p)


def body(tokens, cotangent, gain_one, gain_two, query_weight, key_weight, value_weight, out_weight, bias_table,
         router_weight, expert_in, expert_out, lengths, routes):
    L, D = tokens.shape
    buckets, heads = bias_table.shape
    experts = router_weight.shape[1]
    local = expert_in.shape[0]
    peers = lax.axis_size("expert")
    n_dp = lax.axis_size("dp")
    most = 2 * L // experts
    S = peers * most
    steps = L // RB
    me = lax.axis_index("expert")
    gain_1 = gain_one[None, :]
    gain_2 = gain_two[None, :]

    def exchange(values):
        moved = lax.all_to_all(values.reshape(peers, most, D), "expert", split_axis=0, concat_axis=0, tiled=True)
        return moved.reshape(S, D)

    srow, scol = call(
        functools.partial(slots_kernel, local, most, experts), "slots", (1,),
        [whole(1, L), whole(L, 1)], [whole(local, L), whole(L, 128)], [struct((local, L), I32), struct((L, 128), I32)],
        flops=4 * L * L * 128, moved=L * 1024,
    )(routes.reshape(1, L), routes)
    g_sent = call(
        functools.partial(cotangent_kernel, local), "dispatch_cotangent", (1,),
        [SMEM, whole(local, L), whole(L, D)], [whole(S, D)] * local, [struct((S, D), BF)] * local,
        flops=2 * local * S * L * D, moved=2 * (1 + local) * S * D,
    )(lengths, srow, cotangent)
    g_got = [exchange(v) for v in g_sent]

    h_one, qkv = call(
        project_kernel, "project", (steps,),
        [rows_of(D), whole(1, D), whole(D, D), whole(D, D), whole(D, D)], [rows_of(D), rows_of(3 * D)],
        [struct((L, D), BF), struct((L, 3 * D), BF)], flops=6 * L * D * D, moved=6 * D * D + 10 * L * D,
    )(tokens, gain_1, query_weight, key_weight, value_weight)

    places = jnp.arange(WIDE, dtype=I32)
    offsets = jnp.where(places < 3 * SUB, places - SUB, places - WIDE - SUB)
    hot_near = (bucket_of(offsets)[None, :] == jnp.arange(buckets, dtype=I32)[:, None]).astype(F32)
    near = jnp.dot(bias_table.T, hot_near, precision=HIGHEST).reshape(heads // 2, 2, WIDE)
    edge = buckets // 2
    far = jnp.stack([bias_table[edge - 1], bias_table[buckets - 1]])
    o, inv, p = attn_fwd(lengths, far, qkv, near)

    middle, h_two = call(
        post_kernel, "middle", (steps,),
        [SMEM, rows_of(D), rows_of(D), whole(D, D), whole(1, D)], [rows_of(D), rows_of(D)],
        [struct((L, D), F32), struct((L, D), BF)], flops=2 * L * D * D, moved=2 * D * D + 10 * L * D,
    )(lengths, tokens, o, out_weight, gain_2)
    h_got = []
    for e in range(local):
        sent = call(
            functools.partial(dispatch_kernel, e), "dispatch", (1,),
            [whole(local, L), whole(L, D)], whole(S, D), struct((S, D), BF), flops=2 * S * L * D, moved=4 * S * D,
        )(srow, h_two)
        h_got.append(exchange(sent))

    runs = []
    for e in range(local):
        hot = (jnp.arange(experts, dtype=I32) == me * local + e).astype(F32)[None, :]
        runs.append(experts_run(e, n_dp, hot, h_got[e], g_got[e], expert_in, expert_out, router_weight))
    backs = [exchange(run[1]) for run in runs]
    *rows_sent, backs[0] = lax.optimization_barrier((*[run[0] for run in runs], backs[0]))
    rows_got = [exchange(v) for v in rows_sent]
    d_first = [lax.psum_scatter(run[2], "dp", scatter_dimension=0, tiled=True) for run in runs]
    d_second = [lax.psum_scatter(run[3], "dp", scatter_dimension=0, tiled=True) for run in runs]
    d_router = sum(run[4] for run in runs)

    gm, do, d_out, d_gain_2 = call(
        functools.partial(combine_kernel, local), "combine", (steps,),
        [SMEM, rows_of(128)] + [whole(S, D)] * local + [rows_of(D)] * 4 + [whole(D, D), whole(1, D)],
        [rows_of(D), rows_of(D), whole(D, D), whole(1, D)],
        [struct((L, D), F32), struct((L, D), BF), struct((D, D), BF), struct((1, D), F32)],
        [pltpu.VMEM((D, D), F32), pltpu.VMEM((1, D), F32)],
        flops=2 * local * S * L * D + 4 * L * D * D, moved=4 * D * D + 20 * L * D,
    )(lengths, scol, *backs, middle, cotangent, o, inv, out_weight, gain_2)
    dq, dk, dv, near_sums, far_sums = attn_bwd(qkv, do, o, p)
    d_qkv = call(
        weights_kernel, "projection_gradients", (steps,),
        [rows_of(D)] * 4, whole(D, 3 * D), struct((D, 3 * D), BF), [pltpu.VMEM((D, 3 * D), F32)],
        flops=6 * L * D * D, moved=6 * D * D + 8 * L * D,
    )(h_one, dq, dk, dv)
    grad_tokens, d_gain_1 = call(
        tokens_kernel, "token_gradients", (steps,),
        [rows_of(D), whole(1, D)] + [rows_of(D)] * 3 + [whole(D, D)] * 3 + [rows_of(D)],
        [rows_of(D), whole(1, D)], [struct((L, D), BF), struct((1, D), F32)],
        flops=6 * L * D * D, moved=6 * D * D + 14 * L * D,
    )(tokens, gain_1, dq, dk, dv, query_weight, key_weight, value_weight, gm)
    d_table = jnp.dot(near_sums.reshape(heads, WIDE), hot_near.T, precision=HIGHEST).T
    far_sums = jnp.sum(far_sums.reshape(heads, 2, 128), axis=2)
    d_table = d_table.at[edge - 1].add(far_sums[:, 0]).at[buckets - 1].add(far_sums[:, 1])
    mixed = call(
        functools.partial(mixed_kernel, local), "mixed", (steps,),
        [SMEM, rows_of(128)] + [whole(S, D)] * local + [rows_of(D)], rows_of(D), struct((L, D), BF),
        flops=2 * local * S * L * D, moved=10 * S * D,
    )(lengths, scol, *rows_got, middle)

    both = ("dp", "expert")
    d_out = lax.psum(d_out, both).astype(F32)
    d_qkv = lax.psum(d_qkv, both).astype(F32)
    d_gain_1, d_gain_2, d_table, d_router = lax.psum((d_gain_1[0], d_gain_2[0], d_table, d_router), both)
    return (
        mixed,
        grad_tokens,
        d_gain_1,
        d_gain_2,
        d_qkv[:, :D],
        d_qkv[:, D:2 * D],
        d_qkv[:, 2 * D:],
        d_out,
        d_table,
        d_router,
        jnp.concatenate(d_first, axis=0).astype(F32),
        jnp.concatenate(d_second, axis=0).astype(F32),
    )


def solution(mesh):
    rows = P(("dp", "expert"), None)
    return jax.shard_map(
        body,
        mesh=mesh,
        in_specs=(rows, rows, P(), P(), P(), P(), P(), P(), P(), P(), P("expert", None, None), P("expert", None, None), P(("dp", "expert")), rows),
        out_specs=(rows, rows, P(), P(), P(), P(), P(), P(), P(), P(), P("expert", None, "dp"), P("expert", "dp", None)),
        check_vma=False,
    )
```

time: 1060 us -> 646 us (0.61)
  matrix products: 383 us -> 0.28 us
  Pallas kernels: 0 us -> 231 us
  local copies, waits for them, and re-layouts: 182 us -> 16.7 us
  other arithmetic: 99.8 us -> 14 us
  blocking collectives: 193 us -> 160 us
  starting transfers between devices: 9.02 us -> 28 us
    dot_general x37 -> x2, matrix products: 383 us -> 0.28 us  [the longest x1 0.14 us: body(): jnp.dot(bias_table.T, hot_near, precision=HIGHEST)]
    pallas_call x0 -> x14, Pallas kernels: none -> 231 us  [the longest x2 88.1 us: experts_run(): call(expert_kernel, 'experts', (parts,), [whole(1, E), whole(S, D), whole...]
    dot_general x2 -> x0, local copies, waits for them, and re-layouts: 60.8 us -> none  [body(): jnp.einsum('qkb,bh->hqk', table_hot, bias_table, precision=HIGHEST, prefe...]
    convert_element_type x6 -> x0, local copies, waits for them, and re-layouts: 53.5 us -> none  [the longest x2 46.4 us: body(): grad_scores = (attn_probs * (grad_probs - inner_sum)).astype(jnp.bfloat16)]
    all_to_all x2, blocking collectives: 154 us -> 102 us  [exchange(): lax.all_to_all(values.reshape(peers, most, D), 'expert', split_axis=0, co...]
    all_to_all x2 -> x6, waiting for transfers between devices: 118 us -> 70.9 us  [exchange(): lax.all_to_all(values.reshape(peers, most, D), 'expert', split_axis=0, co...]
    convert_element_type x7 -> x5, other arithmetic: 56.2 us -> 12.5 us  [the longest x1 4.13 us: body(): jnp.concatenate(d_second, axis=0).astype(F32)]
    psum x1, waiting for transfers between devices: 52.3 us -> 82.4 us  [body(): d_qkv = lax.psum(d_qkv, both).astype(F32)]
  transfers between devices with their start and end apart: 5 -> 11, of which waited for: 3 -> 4; matrix products, arithmetic and copies ran while one was open for 32% -> 3% of each run, Pallas kernels for 0% -> 25%
where the time goes in v1:
time: 646 us; the launch traced here: 641 us
  Pallas kernels  231 us (36%)
  waiting for transfers between devices  175 us (27%)
  blocking collectives  160 us (25%)
  starting transfers between devices  28 us (4%)
  between operations  16.8 us (3%)
  local copies, waits for them, and re-layouts  16.7 us (3%)
  other arithmetic  14 us (2%)
    all_to_all x2, blocking collectives, exchange(): lax.all_to_all(values.reshape(peers, most, D), 'expert', split_axis=0, co...  102 us
    pallas_call x2, Pallas kernels, experts_run(): call(expert_kernel, 'experts', (parts,), [whole(1, E), whole(S, D), whole...  88.1 us
    psum x1, waiting for transfers between devices, body(): d_qkv = lax.psum(d_qkv, both).astype(F32)  82.4 us
    all_to_all x6, waiting for transfers between devices, exchange(): lax.all_to_all(values.reshape(peers, most, D), 'expert', split_axis=0, co...  70.9 us
    psum x1, blocking collectives, body(): lax.psum((d_gain_1[0], d_gain_2[0], d_table, d_router), both)  57.8 us
    pallas_call x1, Pallas kernels, attn_bwd(): pl.pallas_call(attn_bwd_kernel, grid=(pairs,), in_specs=[blk(0), blk(pair...  33.7 us
    pallas_call x1, Pallas kernels, attn_fwd(): pl.pallas_call(attn_fwd_kernel, grid=(pairs,), in_specs=[SMEM, SMEM, blk(...  31.6 us
    all_to_all x6, starting transfers between devices, exchange(): lax.all_to_all(values.reshape(peers, most, D), 'expert', split_axis=0, co...  27.3 us
  transfers between devices with their start and end apart: 11, of which 4 were waited for; matrix products, arithmetic and copies ran while one was open for 3% of the time, Pallas kernels for 25%

profile of v1, /device:TPU:0, one launch (start us, length us, event | category | flops | bytes accessed | tf_op | source)
XLA Modules:
  0.0 640.9 jit_solution(5934408775327343862)
XLA Ops:
  8.7 1.7 copy.42.col_ref
  10.4 4.0 slots.1
  14.3 6.0 dispatch_cotangent.1
  20.3 44.3 %all_to_all.40 = bf16[8,128,768]{2,1,0:T(8,128)(2,1)} all-to-all(bf16[8,128,768]{2,1,0:T(8,128)(2,1)} %bitcast.37), channel_id=1, replica_groups=mesh['dp'=4,'expert'=8] {'expert'}, dimensions={0} | all-to-all | bytes 3145728 | tf_op jit(solution)/shard_map/all_to_all | solution.py:493
  64.6 4.2 all-to-all-start.1
  68.9 0.6 broadcast_in_dim.4.gain_ref
  69.4 0.6 broadcast_in_dim.5.gain_ref.refs_7_
  70.1 0.1 copy.52
  70.2 0.1 copy.53
  70.3 0.1 convolution_bitcast_fusion
  70.4 0.6 reshape.191.w_ref
  71.1 0.6 pad_maximum_fusion.far_ref
  71.6 8.0 %project.1 = (bf16[1024,768]{1,0:T(8,128)(2,1)}, bf16[1024,2304]{1,0:T(8,128)(2,1)}) custom-call(bf16[1024,768]{1,0:T(8,128)(2,1)} %x_ref.5, f32[1,768]{1,0:T(1,128)} %broadcast_in_dim.4.gain_ref, bf16[768,768]{1,0:T(8,128)(2,1)} %wq_ref.3, bf16[768,768]{1,0:T(8,128)(2,1)} %wk_ref.3, bf16[768,768]{1,0:T(8,128)(2,1)} %wv_ref.3), custom_call_target="tpu_custom_call" | custom-call | flops 3623878656 | bytes 11403264 | tf_op jit(solution)/shard_map/project/pallas_call | solution.py:508
  79.6 31.6 %attention_forward.1 = (bf16[1024,768]{1,0:T(8,128)(2,1)}, f32[1024,768]{1,0:T(8,128)}, bf16[12,1024,1024]{2,1,0:T(8,128)(2,1)}) custom-call(s32[1]{0:T(128)S(6)} %copy.60.len_ref, f32[2,12]{1,0:T(2,128)} %pad_maximum_fusion.far_ref, bf16[1024,2304]{1,0:T(8,128)(2,1)} %get-tuple-element.73.q_ref.k_ref.v_ref, ...), custom_call_target="tpu_custom_call" | custom-call | flops 12884901888 | bytes 34603008 | tf_op jit(solution)/shard_map/attention_forward/pallas_call | solution.py:375
  111.2 5.7 middle.1
  116.9 4.4 dispatch.2
  121.3 1.1 copy-done.3
  122.4 5.1 all-to-all-start
  127.5 4.4 dispatch.3
  131.9 33.5 %all-to-all-done = bf16[8,128,768]{2,1,0:T(8,128)(2,1)S(1)} async-done(((bf16[8,128,768]{2,1,0:T(8,128)(2,1)}), bf16[8,128,768]{2,1,0:T(8,128)(2,1)S(1)}, u32[]{:S(2)}, u32[]{:S(2)}) %all-to-all-start) | async-done | bytes 1572896 | tf_op jit(solution)/shard_map/all_to_all | solution.py:493
  165.3 1.1 copy-done.5
  166.5 3.8 all-to-all-start.2
  170.2 0.5 compare_convert_fusion.1.hot_ref
  170.8 0.8 copy.45.wr_ref
  171.6 44.0 %experts.2 = (bf16[1024,768]{1,0:T(8,128)(2,1)}, bf16[1024,768]{1,0:T(8,128)(2,1)}, bf16[4,768,768]{2,1,0:T(8,128)(2,1)}, bf16[4,768,768]{2,1,0:T(8,128)(2,1)}, f32[768,16]{1,0:T(8,128)}) custom-call(f32[1,16]{1,0:T(1,128)} %compare_convert_fusion.1.hot_ref, bf16[1024,768]{1,0:T(8,128)(2,1)} %bitcast.30, bf16[1024,768]{1,0:T(8,128)(2,1)} %bitcast.28, ...), custom_call_target="tpu_custom_call" | custom-call | flops 28991029248 | bytes 25165824 | tf_op jit(solution)/shard_map/experts/pallas_call | solution.py:205
  215.6 1.1 copy-done.6
  216.8 5.3 all-to-all-start.4
  222.1 0.5 compare_convert_fusion.hot_ref
  222.6 44.1 %experts.3 = (bf16[1024,768]{1,0:T(8,128)(2,1)}, bf16[1024,768]{1,0:T(8,128)(2,1)}, bf16[4,768,768]{2,1,0:T(8,128)(2,1)}, bf16[4,768,768]{2,1,0:T(8,128)(2,1)}, f32[768,16]{1,0:T(8,128)}) custom-call(f32[1,16]{1,0:T(1,128)} %compare_convert_fusion.hot_ref, bf16[1024,768]{1,0:T(8,128)(2,1)} %bitcast.31, bf16[1024,768]{1,0:T(8,128)(2,1)} %bitcast.25, ...), custom_call_target="tpu_custom_call" | custom-call | flops 28991029248 | bytes 25165824 | tf_op jit(solution)/shard_map/experts/pallas_call | solution.py:205
  266.7 1.1 copy-done.4
  267.8 5.1 all-to-all-start.7
  272.9 0.4 all-reduce.8.cloned.1.call-start
  273.4 37.4 %all-to-all-done.7 = bf16[8,128,768]{2,1,0:T(8,128)(2,1)S(1)} async-done(((bf16[8,128,768]{2,1,0:T(8,128)(2,1)}), bf16[8,128,768]{2,1,0:T(8,128)(2,1)S(1)}, u32[]{:S(2)}, u32[]{:S(2)}) %all-to-all-start.7) | async-done | bytes 1572896 | tf_op jit(solution)/shard_map/all_to_all | solution.py:493
  310.8 1.1 copy-done.7
  311.9 15.4 %combine.1 = (f32[1024,768]{1,0:T(8,128)}, bf16[1024,768]{1,0:T(8,128)(2,1)}, bf16[768,768]{1,0:T(8,128)(2,1)}, f32[1,768]{1,0:T(1,128)}) custom-call(s32[1]{0:T(128)S(6)} %copy.60.len_ref, s32[1024,128]{1,0:T(8,128)} %get-tuple-element.71.scol_ref, bf16[1024,768]{1,0:T(8,128)(2,1)} %bitcast.29, bf16[1024,768]{1,0:T(8,128)(2,1)} %bitcast.36, ...), custom_call_target="tpu_custom_call" | custom-call | flops 5637144576 | bytes 18087936 | tf_op jit(solution)/shard_map/combine/pallas_call | solution.py:546
  327.3 33.7 %attention_backward.1 = (bf16[1024,768]{1,0:T(8,128)(2,1)}, bf16[1024,768]{1,0:T(8,128)(2,1)}, bf16[1024,768]{1,0:T(8,128)(2,1)}, f32[6,2,512]{2,1,0:T(2,128)}, f32[6,2,2,128]{3,2,1,0:T(2,128)}) custom-call(bf16[1024,2304]{1,0:T(8,128)(2,1)} %get-tuple-element.73.q_ref.k_ref.v_ref, bf16[1024,2304]{1,0:T(8,128)(2,1)} %get-tuple-element.73.q_ref.k_ref.v_ref, ...), custom_call_target="tpu_custom_call" | custom-call | flops 25769803776 | bytes 34603008 | tf_op jit(solution)/shard_map/attention_backward/pallas_call | solution.py:465
  361.0 12.5 %projection_gradients.1 = bf16[768,2304]{1,0:T(8,128)(2,1)} custom-call(bf16[1024,768]{1,0:T(8,128)(2,1)} %get-tuple-element.96.h_ref, bf16[1024,768]{1,0:T(8,128)(2,1)} %get-tuple-element.89.dq_ref, bf16[1024,768]{1,0:T(8,128)(2,1)} %get-tuple-element.90.dk_ref, bf16[1024,768]{1,0:T(8,128)(2,1)} %get-tuple-element.91.dv_ref), custom_call_target="tpu_custom_call" | custom-call | flops 3623878656 | bytes 9830400 | tf_op jit(solution)/shard_map/projection_gradients/pallas_call | solution.py:555
  373.6 0.5 reduce-scatter.17.cloned.1.call-update
  374.1 0.5 reduce-scatter.19.cloned.1.call-update
  374.7 0.5 reduce-scatter.13.cloned.1.call-update
  375.3 0.7 reduce-scatter.15.cloned.1.call-update
  376.0 0.7 copy-done.1
  376.7 57.8 %all_to_all.41 = bf16[8,128,768]{2,1,0:T(8,128)(2,1)} all-to-all(bf16[8,128,768]{2,1,0:T(8,128)(2,1)S(1)} %bitcast.24), channel_id=1, replica_groups=mesh['dp'=4,'expert'=8] {'expert'}, dimensions={0} | all-to-all | bytes 3145728 | tf_op jit(solution)/shard_map/all_to_all | solution.py:493
  434.5 3.9 all-to-all-start.5
  438.5 9.6 %token_gradients.1 = (bf16[1024,768]{1,0:T(8,128)(2,1)}, f32[1,768]{1,0:T(1,128)}) custom-call(bf16[1024,768]{1,0:T(8,128)(2,1)} %x_ref.5, f32[1,768]{1,0:T(1,128)} %broadcast_in_dim.4.gain_ref, bf16[1024,768]{1,0:T(8,128)(2,1)} %get-tuple-element.89.dq_ref, bf16[1024,768]{1,0:T(8,128)(2,1)} %get-tuple-element.90.dk_ref, ...), custom_call_target="tpu_custom_call" | custom-call | flops 3623878656 | bytes 14548992 | tf_op jit(solution)/shard_map/token_gradients/pallas_call | solution.py:560
  448.1 0.7 reduce.5
  448.8 0.1 reduce_sum.11
  449.1 0.1 copy.55
  449.2 0.1 copy.54
  449.2 0.1 copy.48
  449.3 0.1 copy.49
  449.4 0.1 fusion
  449.6 0.1 scatter-add.6
  449.8 0.1 scatter-add.9
  449.9 57.8 %all-reduce.4 = (f32[768]{0:T(1024)}, f32[768]{0:T(1024)}, f32[32,12]{0,1:T(8,128)}, f32[768,16]{1,0:T(8,128)S(1)}) all-reduce(f32[768]{0:T(1024)S(1)} %reduce.5, f32[768]{0:T(1024)S(1)} %reduce.6, f32[32,12]{0,1:T(8,128)S(1)} %scatter-add.9, f32[768,16]{1,0:T(8,128)S(1)} %add.137), channel_id=1, replica_groups=mesh['dp'=4,'expert'=8] {'dp','expert'}, use_global_device_ids=true, to_apply=%region_0.1 | all-reduce | flops 14208 | bytes 113664 | tf_op jit(solution)/shard_map/psum | solution.py:578
  507.7 0.8 copy.50
  508.5 82.4 %all-reduce.8.cloned.1.call-done = (bf16[768,2304]{1,0:T(8,128)(2,1)}, bf16[768,768]{1,0:T(8,128)(2,1)}) async-done(((bf16[768,2304]{1,0:T(8,128)(2,1)}, bf16[768,768]{1,0:T(8,128)(2,1)}), (bf16[768,2304]{1,0:T(8,128)(2,1)}, bf16[768,768]{1,0:T(8,128)(2,1)})) %all-reduce.8.cloned.1.call-update) | async-done | bytes 4718608 | tf_op jit(solution)/shard_map/psum | solution.py:577
  590.9 3.2 convert_element_type.107
  594.1 3.1 fusion.7
  597.2 1.1 copy-done.2
  598.3 7.5 %mixed.1 = bf16[1024,768]{1,0:T(8,128)(2,1)} custom-call(s32[1]{0:T(128)S(6)} %copy.60.len_ref, s32[1024,128]{1,0:T(8,128)} %get-tuple-element.71.scol_ref, bf16[1024,768]{1,0:T(8,128)(2,1)} %bitcast.27, bf16[1024,768]{1,0:T(8,128)(2,1)} %bitcast.26, f32[1024,768]{1,0:T(8,128)} %get-tuple-element.83.refs_2_), custom_call_target="tpu_custom_call" | custom-call | flops 3221225472 | bytes 7864320 | tf_op jit(solution)/shard_map/mixed/pallas_call | solution.py:569
  605.8 4.1 maximum_convert_fusion.1
  609.9 19.0 %reduce-scatter.15.cloned.1.call-done = bf16[1,768,768]{2,1,0:T(8,128)(2,1)} async-done(((bf16[4,768,768]{2,1,0:T(8,128)(2,1)}), bf16[1,768,768]{2,1,0:T(8,128)(2,1)}) %reduce-scatter.15.cloned.1.call-update) | async-done | bytes 1179664
  628.9 4.1 maximum_convert_fusion
  (48 shorter events, 0.7 us)
Async XLA Ops:
  64.6 4.3 copy-start.14
  64.6 4.8 copy-start.15
  64.6 5.4 copy-start.10
  64.6 56.7 %all-to-all-start.1 = ((bf16[8,128,768]{2,1,0:T(8,128)(2,1)}), bf16[8,128,768]{2,1,0:T(8,128)(2,1)S(1)}, u32[]{:S(2)}, u32[]{:S(2)}) async-start(bf16[8,128,768]{2,1,0:T(8,128)(2,1)} %bitcast.4), calls=%async_computation.1 | async-start | bytes 3145728 | tf_op jit(solution)/shard_map/all_to_all | solution.py:493
  121.3 1.1 copy-start.3
  122.4 42.9 %all-to-all-start = ((bf16[8,128,768]{2,1,0:T(8,128)(2,1)}), bf16[8,128,768]{2,1,0:T(8,128)(2,1)S(1)}, u32[]{:S(2)}, u32[]{:S(2)}) async-start(bf16[8,128,768]{2,1,0:T(8,128)(2,1)} %bitcast.34), calls=%async_computation | async-start | bytes 3145728 | tf_op jit(solution)/shard_map/all_to_all | solution.py:493
  165.3 1.1 copy-start.5
  165.3 5.4 copy-start.11
  166.5 49.1 %all-to-all-start.2 = ((bf16[8,128,768]{2,1,0:T(8,128)(2,1)}), bf16[8,128,768]{2,1,0:T(8,128)(2,1)S(1)}, u32[]{:S(2)}, u32[]{:S(2)}) async-start(bf16[8,128,768]{2,1,0:T(8,128)(2,1)} %bitcast.33), calls=%async_computation.2 | async-start | bytes 3145728 | tf_op jit(solution)/shard_map/all_to_all | solution.py:493
  215.6 1.1 copy-start.6
  216.8 49.9 %all-to-all-start.4 = ((bf16[8,128,768]{2,1,0:T(8,128)(2,1)}), bf16[8,128,768]{2,1,0:T(8,128)(2,1)S(1)}, u32[]{:S(2)}, u32[]{:S(2)}) async-start(bf16[8,128,768]{2,1,0:T(8,128)(2,1)} %bitcast.32), calls=%async_computation.4 | async-start | bytes 3145728 | tf_op jit(solution)/shard_map/all_to_all | solution.py:493
  266.7 1.1 copy-start.4
  267.8 42.9 %all-to-all-start.7 = ((bf16[8,128,768]{2,1,0:T(8,128)(2,1)}), bf16[8,128,768]{2,1,0:T(8,128)(2,1)S(1)}, u32[]{:S(2)}, u32[]{:S(2)}) async-start(bf16[8,128,768]{2,1,0:T(8,128)(2,1)} %bitcast.35), calls=%async_computation.7 | async-start | bytes 3145728 | tf_op jit(solution)/shard_map/all_to_all | solution.py:493
  272.9 318.0 %all-reduce.8.cloned.1.call-start = ((), (), s32[]{:S(2)}) async-start(), calls=%async_computation.16 | async-start | bytes 9437184 | tf_op jit(solution)/shard_map/psum | solution.py:577
  310.7 1.1 copy-start.7
  373.5 232.3 %reduce-scatter.17.cloned.1.call-start = ((), (), s32[]{:S(2)}) async-start(), calls=%async_computation.14 | async-start | bytes 5898240
  374.1 231.7 %reduce-scatter.19.cloned.1.call-start = ((), (), s32[]{:S(2)}) async-start(), calls=%async_computation.15 | async-start | bytes 5898240
  374.7 235.3 %reduce-scatter.13.cloned.1.call-start = ((), (), s32[]{:S(2)}) async-start(), calls=%async_computation.12 | async-start | bytes 5898240
  375.2 253.7 %reduce-scatter.15.cloned.1.call-start = ((), (), s32[]{:S(2)}) async-start(), calls=%async_computation.13 | async-start | bytes 5898240
  375.3 1.4 copy-start.1
  434.5 3.9 copy-start.8
  434.5 3.9 copy-start.9
  434.5 162.7 %all-to-all-start.5 = ((bf16[8,128,768]{2,1,0:T(8,128)(2,1)}), bf16[8,128,768]{2,1,0:T(8,128)(2,1)S(1)}, u32[]{:S(2)}, u32[]{:S(2)}) async-start(bf16[8,128,768]{2,1,0:T(8,128)(2,1)} %bitcast.12), calls=%async_computation.5 | async-start | bytes 3145728 | tf_op jit(solution)/shard_map/all_to_all | solution.py:493
  438.5 10.3 %copy-start.16 = (f32[1,768]{1,0:T(1,128)S(1)}, f32[1,768]{1,0:T(1,128)}, u32[]{:S(2)}) copy-start(f32[1,768]{1,0:T(1,128)} %get-tuple-element.95) | copy-start | bytes 9220
  438.5 10.3 %copy-start.13 = (f32[6,2,2,128]{3,2,1,0:T(2,128)S(1)}, f32[6,2,2,128]{3,2,1,0:T(2,128)}, u32[]{:S(2)}) copy-start(f32[6,2,2,128]{3,2,1,0:T(2,128)} %get-tuple-element.99) | copy-start | bytes 36868
  438.5 10.4 %copy-start.12 = (f32[6,2,512]{2,1,0:T(2,128)S(1)}, f32[6,2,512]{2,1,0:T(2,128)}, u32[]{:S(2)}) copy-start(f32[6,2,512]{2,1,0:T(2,128)} %get-tuple-element.98) | copy-start | bytes 73732
  590.9 3.2 copy-start
  597.2 1.1 copy-start.2
Sparse Core Ops, SparseCore 0:
  373.6 217.2 all-reduce.7
Sparse Core Ops, SparseCore 1:
  377.2 60.4 reduce-scatter.16
  440.8 62.2 reduce-scatter.18
  506.8 61.6 reduce-scatter.12
  571.7 57.2 reduce-scatter.14

commit v2 on v1

--- a/solution.py
+++ b/solution.py
@@ -60,7 +60,7 @@
     return jax.ShapeDtypeStruct(shape, kind)
 
 
-def call(kernel, name, grid, in_specs, out_specs, out_shape, scratch=(), flops=0, moved=0, transcendentals=0):
+def call(kernel, name, grid, in_specs, out_specs, out_shape, scratch=(), flops=0, moved=0, transcendentals=0, **params):
     return pl.pallas_call(
         kernel,
         grid=grid,
@@ -68,7 +68,7 @@
         out_specs=out_specs,
         out_shape=out_shape,
         scratch_shapes=list(scratch),
-        compiler_params=pltpu.CompilerParams(vmem_limit_bytes=BIG),
+        compiler_params=pltpu.CompilerParams(vmem_limit_bytes=BIG, **params),
         cost_estimate=pl.CostEstimate(flops=int(flops), bytes_accessed=int(moved), transcendentals=int(transcendentals)),
         name=name,
     )
@@ -99,12 +99,13 @@
     return dot(hot, values).astype(BF)
 
 
-def cotangent_kernel(local, len_ref, srow_ref, cot_ref, *out_refs):
-    L = cot_ref.shape[0]
+def cotangent_kernel(local, len_ref, srow_ref, cot_ref, out_ref):
+    L, D = cot_ref.shape
+    peers, _, most, _ = out_ref.shape
     live = iota((L, 1), 0) < len_ref[0]
     values = jnp.where(live, cot_ref[...].astype(F32), 0.0).astype(BF)
     for e in range(local):
-        out_refs[e][...] = dispatch_rows(srow_ref[e:e + 1, :], values, out_refs[e].shape[0])
+        out_ref[:, e] = dispatch_rows(srow_ref[e:e + 1, :], values, peers * most).reshape(peers, most, D)
 
 
 def rms_scale(v):
@@ -149,7 +150,7 @@
         probs = ex / jnp.sum(ex, axis=1, keepdims=True)
         gate = jnp.sum(probs * hot_ref[...], axis=1, keepdims=True)
         gate_s[...] = jnp.broadcast_to(gate, gate_s.shape)
-        gr_s[...] = (gate * g_ref[...].astype(F32)).astype(BF)
+        gr_s[...] = (gate * g_ref[:, 0].reshape(h.shape).astype(F32)).astype(BF)
 
     w1 = w1_ref[0]
     w2 = w2_ref[0]
@@ -187,13 +188,13 @@
         rows = rows_s[...].astype(BF).astype(F32)
         gate = gate_s[:, :1]
         rows_ref[...] = (gate * rows).astype(BF)
-        grad_gate = jnp.sum(rows * g_ref[...].astype(F32), axis=1, keepdims=True)
+        grad_gate = jnp.sum(rows * g_ref[:, 0].reshape(rows.shape).astype(F32), axis=1, keepdims=True)
         logits = dot(h_ref[...], wr_ref[...])
         top = jnp.max(logits, axis=1, keepdims=True)
         ex = jnp.exp(logits - top)
         probs = ex / jnp.sum(ex, axis=1, keepdims=True)
         gl = (grad_gate * gate * (hot_ref[...] - probs)).astype(BF)
-        dr_ref[...] = dot(ht_s[...], gl)
+        dr_ref[...] = dot_tn(gl, h_ref[...])
         back_ref[...] = (sent_s[...] + dot_nt(gl, wr_ref[...])).astype(BF)
 
 
@@ -204,9 +205,9 @@
     E = router.shape[1]
     return call(
         expert_kernel, "experts", (parts,),
-        [whole(1, E), whole(S, D), whole(S, D), pl.BlockSpec((1, D, FT), lambda f: (e, 0, f)), pl.BlockSpec((1, FT, D), lambda f: (e, f, 0)), whole(D, E)],
-        [whole(S, D), whole(S, D), pl.BlockSpec((1, D, FT), lambda f: (f, 0, 0)), pl.BlockSpec((1, FT, D), lambda f: (f, 0, 0)), whole(D, E)],
-        [struct((S, D), BF), struct((S, D), BF), struct((parts, D, FT), BF), struct((parts, FT, D), BF), struct((D, E), F32)],
+        [whole(1, E), whole(S, D), pl.BlockSpec((g.shape[0], 1, g.shape[2], D), lambda f: (0, e, 0, 0)), pl.BlockSpec((1, D, FT), lambda f: (e, 0, f)), pl.BlockSpec((1, FT, D), lambda f: (e, f, 0)), whole(D, E)],
+        [whole(S, D), whole(S, D), pl.BlockSpec((1, D, FT), lambda f: (f, 0, 0)), pl.BlockSpec((1, FT, D), lambda f: (f, 0, 0)), whole(E, D)],
+        [struct((S, D), BF), struct((S, D), BF), struct((parts, D, FT), BF), struct((parts, FT, D), BF), struct((E, D), F32)],
         [pltpu.VMEM((D, S), BF), pltpu.VMEM((S, D), BF), pltpu.VMEM((S, 128), F32), pltpu.VMEM((S, FT), BF), pltpu.VMEM((S, FT), BF), pltpu.VMEM((S, D), F32), pltpu.VMEM((S, D), F32)],
         flops=12 * S * D * FF, moved=8 * D * FF + 8 * S * D, transcendentals=S * FF,
     )(hot, h, g, first, second, router)
@@ -225,7 +226,7 @@
 
 def combine_kernel(local, len_ref, scol_ref, *refs):
     backs = refs[:local]
-    middle_ref, cot_ref, o_ref, inv_ref, wo_ref, gain_ref, gm_ref, do_ref, dwo_ref, gain_out, acc_s, gain_s = refs[local:]
+    middle_ref, cot_ref, inv_ref, wo_ref, gain_ref, gm_ref, gb_ref, do_ref, gain_out = refs[local:]
     r = pl.program_id(0)
     scol = scol_ref[...]
     gh = sum(dot(combine_hot(scol, b.shape[0], e), b[...]) for e, b in enumerate(backs))
@@ -235,71 +236,192 @@
     gm = jnp.where(live, cot_ref[...].astype(F32), 0.0) + gv
     gm_ref[...] = gm
     gb = gm.astype(BF)
+    gb_ref[...] = gb
     do_ref[...] = (dot_nt(gb, wo_ref[...]) * inv_ref[...]).astype(BF)
-    dw = dot_tn(o_ref[...], gb)
     gs = jnp.sum(gg, axis=0, keepdims=True)
 
     @pl.when(r == 0)
     def _():
-        acc_s[...] = dw
-        gain_s[...] = gs
+        gain_out[...] = gs
 
     @pl.when(r > 0)
     def _():
-        acc_s[...] += dw
-        gain_s[...] += gs
-
-    @pl.when(r == pl.num_programs(0) - 1)
-    def _():
-        dwo_ref[...] = acc_s[...].astype(BF)
-        gain_out[...] = gain_s[...]
-
-
-def weights_kernel(h_ref, dq_ref, dk_ref, dv_ref, out_ref, acc_s):
+        gain_out[...] += gs
+
+
+def weights_kernel(h_ref, o_ref, d_ref, gb_ref, out_ref, ht_s):
+    n = pl.program_id(0)
+
+    @pl.when(n == 0)
+    def _():
+        ht_s[...] = h_ref[...].T
+
+    @pl.when(n < 3)
+    def _():
+        out_ref[0] = dot(ht_s[...], d_ref[0]).astype(BF)
+
+    @pl.when(n == 3)
+    def _():
+        out_ref[0] = dot_tn(o_ref[...], gb_ref[...]).astype(BF)
+
+
+def bit_orders():
+    def bits(axis):
+        return [(axis, 1 << n) for n in range(lax.axis_size(axis).bit_length() - 1)]
+    dp, ex = bits("dp"), bits("expert")
+    return [ex[:1] + dp + ex[1:], ex[:1] + dp[::-1] + ex[1:]]
+
+
+def neighbour(axis, mask):
+    me = lax.axis_index(axis)
+    bit = (me // mask) % 2
+    return bit, {axis: me + mask * (1 - 2 * bit)}
+
+
+def add_rows(acc, start, recv, offset, rows):
+    step = 48
+
+    def one(i, _):
+        to = pl.ds(pl.multiple_of(start + i * step, 16), step)
+        acc[to, :] = (acc[to, :].astype(F32) + recv[pl.ds(pl.multiple_of(offset + i * step, 16), step), :].astype(F32)).astype(acc.dtype)
+        return 0
+
+    lax.fori_loop(0, rows // step, one, 0)
+
+
+def halving_stages(order, base, rows, acc, recv, landing, out, send_sem, recv_sem, sem0):
+    stages = []
+    start, n, offset, sem = base, rows, landing, sem0
+    kept = []
+
+    def transfer(src, dst, who, sem):
+        return pltpu.make_async_remote_copy(src_ref=src, dst_ref=dst, send_sem=send_sem.at[sem], recv_sem=recv_sem.at[sem],
+                                            device_id=who, device_id_type=pl.DeviceIdType.MESH)
+
+    for axis, mask in order:
+        bit, who = neighbour(axis, mask)
+        halve = n % 96 == 0
+        m = n // 2 if halve else n
+        keep = start + bit * m if halve else start
+        give = start + (1 - bit) * m if halve else start
+        copy = transfer(acc.at[pl.ds(pl.multiple_of(give, 16), m)], recv.at[pl.ds(offset, m)], who, sem)
+
+        def finish(copy=copy, keep=keep, offset=offset, m=m):
+            copy.wait()
+            add_rows(acc, keep, recv, offset, m)
+
+        stages.append((copy.start, finish))
+        if halve:
+            kept.append((axis, mask, keep, m))
+        start, n = keep, m
+        offset += m
+        sem += 1
+    first = True
+    for axis, mask, at, m in kept[::-1]:
+        bit, who = neighbour(axis, mask)
+        here = pl.ds(pl.multiple_of(at, 16), m)
+        copy = transfer(out.at[here], out.at[here], who, sem)
+
+        def begin(copy=copy, here=here, first=first):
+            if first:
+                out[here, :] = acc[here, :]
+            copy.start()
+
+        stages.append((begin, copy.wait))
+        first = False
+        sem += 1
+    return stages
+
+
+def exchange_stages(order, acc, recv, send_sem, recv_sem, sem0):
+    stages = []
+    for n, (axis, mask) in enumerate(order):
+        bit, who = neighbour(axis, mask)
+        copy = pltpu.make_async_remote_copy(src_ref=acc.at[n], dst_ref=recv.at[n], send_sem=send_sem.at[sem0 + n],
+                                            recv_sem=recv_sem.at[sem0 + n], device_id=who, device_id_type=pl.DeviceIdType.MESH)
+
+        def finish(copy=copy, n=n):
+            copy.wait()
+            acc[n + 1] = acc[n] + recv[n]
+
+        stages.append((copy.start, finish))
+    return stages
+
+
+def last_kernel(local, len_ref, scol_ref, *refs):
+    rows = refs[:local]
+    (middle_ref, x_ref, gain_ref, d_ref, wq_ref, wk_ref, wv_ref, gm_ref, dw_ref, small_ref,
+     mixed_ref, token_ref, sums_ref, small_out, acc, recv, out, sacc, srecv, gain_s, send_sem, recv_sem, local_sem) = refs[local:]
     r = pl.program_id(0)
-    D = h_ref.shape[1]
-    h = h_ref[...]
-    for n, ref in enumerate((dq_ref, dk_ref, dv_ref)):
-        dw = dot_tn(h, ref[...])
-        sl = slice(n * D, (n + 1) * D)
-
-        @pl.when(r == 0)
-        def _():
-            acc_s[:, sl] = dw
-
-        @pl.when(r > 0)
-        def _():
-            acc_s[:, sl] += dw
-
-    @pl.when(r == pl.num_programs(0) - 1)
-    def _():
-        out_ref[...] = acc_s[...].astype(BF)
-
-
-def tokens_kernel(x_ref, gain_ref, dq_ref, dk_ref, dv_ref, wq_ref, wk_ref, wv_ref, gm_ref, out_ref, gain_out):
-    r = pl.program_id(0)
-    gh = dot_nt(dq_ref[...], wq_ref[...]) + dot_nt(dk_ref[...], wk_ref[...]) + dot_nt(dv_ref[...], wv_ref[...])
+    steps = pl.num_programs(0)
+    orders = bit_orders()
+    total = acc.shape[0]
+    half = total // 2
+    parts = [halving_stages(order, n * half, half, acc, recv, n * (recv.shape[0] // 2), out, send_sem, recv_sem, 2 * len(order) * n) for n, order in enumerate(orders)]
+    smalls = exchange_stages(orders[0], sacc, srecv, send_sem, recv_sem, 4 * len(orders[0]))
+    n_rs = len(orders[0])
+
+    @pl.when(r == 0)
+    def _():
+        barrier = pltpu.get_barrier_semaphore()
+        for axis, mask in orders[0]:
+            pl.semaphore_signal(barrier, inc=1, device_id=neighbour(axis, mask)[1], device_id_type=pl.DeviceIdType.MESH)
+        load = pltpu.make_async_copy(dw_ref, acc, local_sem)
+        load.start()
+        load.wait()
+        pl.semaphore_wait(barrier, len(orders[0]))
+        for part in parts:
+            part[0][0]()
+
+    for s in range(1, n_rs):
+        @pl.when(r == s)
+        def _(s=s):
+            for part in parts:
+                part[s - 1][1]()
+                part[s][0]()
+
+    gh = dot_nt(d_ref[0], wq_ref[...]) + dot_nt(d_ref[1], wk_ref[...]) + dot_nt(d_ref[2], wv_ref[...])
     gv, gg = norm_back(x_ref[...].astype(F32), gain_ref[...], gh)
-    out_ref[...] = (gm_ref[...] + gv).astype(BF)
+    token_ref[...] = (gm_ref[...] + gv).astype(BF)
     gs = jnp.sum(gg, axis=0, keepdims=True)
-
-    @pl.when(r == 0)
-    def _():
-        gain_out[...] = gs
-
-    @pl.when(r > 0)
-    def _():
-        gain_out[...] += gs
-
-
-def mixed_kernel(local, len_ref, scol_ref, *refs):
-    rows = refs[:local]
-    middle_ref, out_ref = refs[local:]
-    r = pl.program_id(0)
+    T = x_ref.shape[0]
     scol = scol_ref[...]
     got = sum(dot(combine_hot(scol, b.shape[0], e), b[...]) for e, b in enumerate(rows))
-    live = iota((RB, 1), 0) + r * RB < len_ref[0]
-    out_ref[...] = jnp.where(live, middle_ref[...] + got, 0.0).astype(BF)
+    live = iota((T, 1), 0) + r * T < len_ref[0]
+    mixed_ref[...] = jnp.where(live, middle_ref[...] + got, 0.0).astype(BF)
+
+    @pl.when(r == 0)
+    def _():
+        gain_s[0:1] = gs
+
+    @pl.when(r > 0)
+    def _():
+        gain_s[0:1] += gs
+
+    @pl.when(r == steps - 1)
+    def _():
+        sacc[0] = small_ref[...]
+        sacc[0, 0:1] = gain_s[0:1]
+        smalls[0][0]()
+        done = 0
+        for s in range(n_rs, max(len(part) for part in parts) + 1):
+            for part in parts:
+                if s <= len(part):
+                    part[s - 1][1]()
+                if s < len(part):
+                    part[s][0]()
+            if done < len(smalls):
+                smalls[done][1]()
+                done += 1
+                if done < len(smalls):
+                    smalls[done][0]()
+        while done < len(smalls):
+            smalls[done][1]()
+            done += 1
+            if done < len(smalls):
+                smalls[done][0]()
+        sums_ref[...] = out[...]
+        small_out[...] = sacc[len(smalls)]
 
 
 def near_bias(w_row):
@@ -384,7 +506,7 @@
     )(lengths, far, qkv, qkv, qkv, w)
 
 
-def attn_bwd_kernel(q_ref, k_ref, v_ref, do_ref, o_ref, p_ref, dq_ref, dk_ref, dv_ref, near_ref, blk_ref):
+def attn_bwd_kernel(q_ref, k_ref, v_ref, do_ref, o_ref, p_ref, d_ref, near_ref, blk_ref):
     L = q_ref.shape[0]
     nb = L // SUB
     q = q_ref[...]
@@ -452,9 +574,9 @@
             full = jnp.where((line & step) > 0, pltpu.roll(full, 512 - step, 1), full)
         diag = jnp.sum(full, axis=0, keepdims=True)
         near_ref[0, a:a + 1, :] = diag
-    dq_ref[...] = jnp.where(lane < 64, dqs[0], dqs[1]).astype(BF)
-    dk_ref[...] = dk.astype(BF)
-    dv_ref[...] = dv.astype(BF)
+    d_ref[0] = jnp.where(lane < 64, dqs[0], dqs[1]).astype(BF)
+    d_ref[1] = dk.astype(BF)
+    d_ref[2] = dv.astype(BF)
 
 
 def attn_bwd(qkv, do, o, p):
@@ -466,8 +588,8 @@
         attn_bwd_kernel,
         grid=(pairs,),
         in_specs=[blk(0), blk(pairs), blk(2 * pairs), blk(0), blk(0), pl.BlockSpec((2, L, L), lambda i: (i, 0, 0))],
-        out_specs=[blk(0), blk(0), blk(0), pl.BlockSpec((1, 2, 512), lambda i: (i, 0, 0)), pl.BlockSpec((1, 2, 2, 128), lambda i: (i, 0, 0, 0))],
-        out_shape=[jax.ShapeDtypeStruct((L, D), BF)] * 3 + [jax.ShapeDtypeStruct((pairs, 2, 512), F32), jax.ShapeDtypeStruct((pairs, 2, 2, 128), F32)],
+        out_specs=[pl.BlockSpec((3, L, 128), lambda i: (0, 0, i)), pl.BlockSpec((1, 2, 512), lambda i: (i, 0, 0)), pl.BlockSpec((1, 2, 2, 128), lambda i: (i, 0, 0, 0))],
+        out_shape=[jax.ShapeDtypeStruct((3, L, D), BF), jax.ShapeDtypeStruct((pairs, 2, 512), F32), jax.ShapeDtypeStruct((pairs, 2, 2, 128), F32)],
         compiler_params=pltpu.CompilerParams(vmem_limit_bytes=BIG),
         cost_estimate=pl.CostEstimate(flops=8 * 2 * pairs * L * L * 256, bytes_accessed=2 * pairs * L * L * 2 + 12 * L * D, transcendentals=0),
         name="attention_backward",
@@ -490,8 +612,7 @@
     gain_2 = gain_two[None, :]
 
     def exchange(values):
-        moved = lax.all_to_all(values.reshape(peers, most, D), "expert", split_axis=0, concat_axis=0, tiled=True)
-        return moved.reshape(S, D)
+        return lax.all_to_all(values, "expert", split_axis=0, concat_axis=0, tiled=True)
 
     srow, scol = call(
         functools.partial(slots_kernel, local, most, experts), "slots", (1,),
@@ -500,10 +621,10 @@
     )(routes.reshape(1, L), routes)
     g_sent = call(
         functools.partial(cotangent_kernel, local), "dispatch_cotangent", (1,),
-        [SMEM, whole(local, L), whole(L, D)], [whole(S, D)] * local, [struct((S, D), BF)] * local,
+        [SMEM, whole(local, L), whole(L, D)], whole(peers, local, most, D), struct((peers, local, most, D), BF),
         flops=2 * local * S * L * D, moved=2 * (1 + local) * S * D,
     )(lengths, srow, cotangent)
-    g_got = [exchange(v) for v in g_sent]
+    g_got = exchange(g_sent)
 
     h_one, qkv = call(
         project_kernel, "project", (steps,),
@@ -530,63 +651,68 @@
             functools.partial(dispatch_kernel, e), "dispatch", (1,),
             [whole(local, L), whole(L, D)], whole(S, D), struct((S, D), BF), flops=2 * S * L * D, moved=4 * S * D,
         )(srow, h_two)
-        h_got.append(exchange(sent))
+        h_got.append(exchange(sent.reshape(peers, most, D)).reshape(S, D))
 
     runs = []
     for e in range(local):
         hot = (jnp.arange(experts, dtype=I32) == me * local + e).astype(F32)[None, :]
-        runs.append(experts_run(e, n_dp, hot, h_got[e], g_got[e], expert_in, expert_out, router_weight))
-    backs = [exchange(run[1]) for run in runs]
+        runs.append(experts_run(e, n_dp, hot, h_got[e], g_got, expert_in, expert_out, router_weight))
+    backs = [exchange(run[1].reshape(peers, most, D)).reshape(S, D) for run in runs]
     *rows_sent, backs[0] = lax.optimization_barrier((*[run[0] for run in runs], backs[0]))
-    rows_got = [exchange(v) for v in rows_sent]
+    rows_got = [exchange(v.reshape(peers, most, D)).reshape(S, D) for v in rows_sent]
     d_first = [lax.psum_scatter(run[2], "dp", scatter_dimension=0, tiled=True) for run in runs]
     d_second = [lax.psum_scatter(run[3], "dp", scatter_dimension=0, tiled=True) for run in runs]
     d_router = sum(run[4] for run in runs)
 
-    gm, do, d_out, d_gain_2 = call(
+    gm, gb, do, d_gain_2 = call(
         functools.partial(combine_kernel, local), "combine", (steps,),
-        [SMEM, rows_of(128)] + [whole(S, D)] * local + [rows_of(D)] * 4 + [whole(D, D), whole(1, D)],
-        [rows_of(D), rows_of(D), whole(D, D), whole(1, D)],
-        [struct((L, D), F32), struct((L, D), BF), struct((D, D), BF), struct((1, D), F32)],
-        [pltpu.VMEM((D, D), F32), pltpu.VMEM((1, D), F32)],
-        flops=2 * local * S * L * D + 4 * L * D * D, moved=4 * D * D + 20 * L * D,
-    )(lengths, scol, *backs, middle, cotangent, o, inv, out_weight, gain_2)
-    dq, dk, dv, near_sums, far_sums = attn_bwd(qkv, do, o, p)
-    d_qkv = call(
-        weights_kernel, "projection_gradients", (steps,),
-        [rows_of(D)] * 4, whole(D, 3 * D), struct((D, 3 * D), BF), [pltpu.VMEM((D, 3 * D), F32)],
-        flops=6 * L * D * D, moved=6 * D * D + 8 * L * D,
-    )(h_one, dq, dk, dv)
-    grad_tokens, d_gain_1 = call(
-        tokens_kernel, "token_gradients", (steps,),
-        [rows_of(D), whole(1, D)] + [rows_of(D)] * 3 + [whole(D, D)] * 3 + [rows_of(D)],
-        [rows_of(D), whole(1, D)], [struct((L, D), BF), struct((1, D), F32)],
-        flops=6 * L * D * D, moved=6 * D * D + 14 * L * D,
-    )(tokens, gain_1, dq, dk, dv, query_weight, key_weight, value_weight, gm)
+        [SMEM, rows_of(128)] + [whole(S, D)] * local + [rows_of(D)] * 3 + [whole(D, D), whole(1, D)],
+        [rows_of(D), rows_of(D), rows_of(D), whole(1, D)],
+        [struct((L, D), F32), struct((L, D), BF), struct((L, D), BF), struct((1, D), F32)],
+        flops=2 * local * S * L * D + 2 * L * D * D, moved=2 * D * D + 20 * L * D,
+    )(lengths, scol, *backs, middle, cotangent, inv, out_weight, gain_2)
+    d_first[0], d_second[0], do = lax.optimization_barrier((d_first[0], d_second[0], do))
+    d_heads, near_sums, far_sums = attn_bwd(qkv, do, o, p)
+    d_heads, rows_got[0] = lax.optimization_barrier((d_heads, rows_got[0]))
+    d_weights = call(
+        weights_kernel, "weight_gradients", (4,),
+        [whole(L, D), whole(L, D), pl.BlockSpec((1, L, D), lambda n: (jnp.minimum(n, 2), 0, 0)), whole(L, D)],
+        pl.BlockSpec((1, D, D), lambda n: (n, 0, 0)), struct((4, D, D), BF), [pltpu.VMEM((D, L), BF)],
+        flops=8 * L * D * D, moved=8 * D * D + 12 * L * D,
+    )(h_one, o, d_heads, gb)
     d_table = jnp.dot(near_sums.reshape(heads, WIDE), hot_near.T, precision=HIGHEST).T
     far_sums = jnp.sum(far_sums.reshape(heads, 2, 128), axis=2)
     d_table = d_table.at[edge - 1].add(far_sums[:, 0]).at[buckets - 1].add(far_sums[:, 1])
-    mixed = call(
-        functools.partial(mixed_kernel, local), "mixed", (steps,),
-        [SMEM, rows_of(128)] + [whole(S, D)] * local + [rows_of(D)], rows_of(D), struct((L, D), BF),
-        flops=2 * local * S * L * D, moved=10 * S * D,
-    )(lengths, scol, *rows_got, middle)
-
-    both = ("dp", "expert")
-    d_out = lax.psum(d_out, both).astype(F32)
-    d_qkv = lax.psum(d_qkv, both).astype(F32)
-    d_gain_1, d_gain_2, d_table, d_router = lax.psum((d_gain_1[0], d_gain_2[0], d_table, d_router), both)
+    d_table = jnp.pad(d_table.reshape(1, buckets * heads), ((0, 5), (0, D - buckets * heads)))
+    small = jnp.concatenate([jnp.zeros((1, D), F32), d_gain_2, d_table, d_router], axis=0)
+    T = L // 8
+    orders = (n_dp * peers).bit_length() - 1
+    part = pl.BlockSpec((T, D), lambda r: (r, 0))
+    sems = 5 * orders
+    mixed, grad_tokens, sums, small = call(
+        functools.partial(last_kernel, local), "last", (L // T,),
+        [SMEM, pl.BlockSpec((T, 128), lambda r: (r, 0))] + [whole(S, D)] * local
+        + [part, part, whole(1, D), pl.BlockSpec((3, T, D), lambda r: (0, r, 0))] + [whole(D, D)] * 3
+        + [part, pl.BlockSpec(memory_space=pl.ANY), whole(*small.shape)],
+        [part, part, whole(4 * D, D), whole(*small.shape)],
+        [struct((L, D), BF), struct((L, D), BF), struct((4 * D, D), BF), struct(small.shape, F32)],
+        [pltpu.VMEM((4 * D, D), BF), pltpu.VMEM((4 * D + 96 * orders, D), BF), pltpu.VMEM((4 * D, D), BF)] + [pltpu.VMEM((orders + 1, *small.shape), F32), pltpu.VMEM((orders, *small.shape), F32), pltpu.VMEM((8, D), F32),
+         pltpu.SemaphoreType.DMA((sems,)), pltpu.SemaphoreType.DMA((sems,)), pltpu.SemaphoreType.DMA],
+        flops=6 * L * D * D + 2 * local * S * L * D, moved=6 * D * D + 24 * L * D, collective_id=1, has_side_effects=True,
+    )(lengths, scol, *rows_got, middle, tokens, gain_1, d_heads, query_weight, key_weight, value_weight, gm, d_weights.reshape(4 * D, D), small)
+
+    sums = sums.astype(F32)
     return (
         mixed,
         grad_tokens,
-        d_gain_1,
-        d_gain_2,
-        d_qkv[:, :D],
-        d_qkv[:, D:2 * D],
-        d_qkv[:, 2 * D:],
-        d_out,
-        d_table,
-        d_router,
+        small[0],
+        small[1],
+        sums[:D],
+        sums[D:2 * D],
+        sums[2 * D:3 * D],
+        sums[3 * D:],
+        small[2, :buckets * heads].reshape(buckets, heads),
+        small[8:].T,
         jnp.concatenate(d_first, axis=0).astype(F32),
         jnp.concatenate(d_second, axis=0).astype(F32),
     )

time: 646 us -> 630 us (0.975)
  blocking collectives: 160 us -> 41 us
  Pallas kernels: 231 us -> 301 us
  waiting for transfers between devices: 175 us -> 201 us
  local copies, waits for them, and re-layouts: 16.7 us -> 26.4 us
    all_to_all x6, waiting for transfers between devices: 70.9 us -> 200 us  [exchange(): lax.all_to_all(values, 'expert', split_axis=0, concat_axis=0, tiled=True)]
    psum x1 -> x0, waiting for transfers between devices: 82.4 us -> none  [body(): d_qkv = lax.psum(d_qkv, both).astype(F32)]
    pallas_call x5 -> x4, Pallas kernels: 118 us -> 188 us  [the longest x2 88.7 us: experts_run(): call(expert_kernel, 'experts', (parts,), [whole(1, E), whole(S, D), pl.Bl...]
    all_to_all x2 -> x1, blocking collectives: 102 us -> 41 us  [exchange(): lax.all_to_all(values, 'expert', split_axis=0, concat_axis=0, tiled=True)]
    psum x1 -> x0, blocking collectives: 57.8 us -> none  [body(): lax.psum((d_gain_1[0], d_gain_2[0], d_table, d_router), both)]
    unnamed x9 -> x6, waiting for transfers between devices: 21.3 us -> 1.25 us
  transfers between devices with their start and end apart: 11 -> 10, of which waited for: 4 -> 5; matrix products, arithmetic and copies ran while one was open for 3% -> 3% of each run, Pallas kernels for 25% -> 33%
where the time goes in v2:
time: 630 us; the launch traced here: 622 us
  Pallas kernels  301 us (48%)
  waiting for transfers between devices  201 us (32%)
  blocking collectives  41 us (7%)
  local copies, waits for them, and re-layouts  26.4 us (4%)
  starting transfers between devices  25.4 us (4%)
  between operations  14.9 us (2%)
  other arithmetic  11.1 us (2%)
    all_to_all x6, waiting for transfers between devices, exchange(): lax.all_to_all(values, 'expert', split_axis=0, concat_axis=0, tiled=True)  200 us
    pallas_call x2, Pallas kernels, experts_run(): call(expert_kernel, 'experts', (parts,), [whole(1, E), whole(S, D), pl.Bl...  88.7 us
    pallas_call x1, Pallas kernels, body(): call(functools.partial(last_kernel, local), 'last', (L // T,), [SMEM, pl....  88.4 us
    all_to_all x1, blocking collectives, exchange(): lax.all_to_all(values, 'expert', split_axis=0, concat_axis=0, tiled=True)  41 us
    pallas_call x1, Pallas kernels, attn_bwd(): pl.pallas_call(attn_bwd_kernel, grid=(pairs,), in_specs=[blk(0), blk(pair...  35.5 us
    pallas_call x1, Pallas kernels, attn_fwd(): pl.pallas_call(attn_fwd_kernel, grid=(pairs,), in_specs=[SMEM, SMEM, blk(...  31.6 us
    all_to_all x6, starting transfers between devices, exchange(): lax.all_to_all(values, 'expert', split_axis=0, concat_axis=0, tiled=True)  25.1 us
    pallas_call x1, Pallas kernels, body(): call(functools.partial(combine_kernel, local), 'combine', (steps,), [SMEM...  13.4 us
  transfers between devices with their start and end apart: 10, of which 5 were waited for; matrix products, arithmetic and copies ran while one was open for 3% of the time, Pallas kernels for 33%

profile of v2, /device:TPU:0, one launch (start us, length us, event | category | flops | bytes accessed | tf_op | source)
XLA Modules:
  0.0 621.6 jit_solution(12857123207892492977)
XLA Ops:
  7.8 1.3 broadcast_in_dim.6.gain_ref.refs_4_
  9.1 1.3 broadcast_in_dim.14.gain_ref.refs_6_
  10.4 0.8 fusion.11
  11.4 0.8 convolution_bitcast_fusion
  12.2 0.6 reshape.185.w_ref
  12.9 1.7 copy.44.col_ref
  14.6 0.6 pad_maximum_fusion.far_ref
  15.2 4.0 slots.1
  19.1 8.0 %project.1 = (bf16[1024,768]{1,0:T(8,128)(2,1)}, bf16[1024,2304]{1,0:T(8,128)(2,1)}) custom-call(bf16[1024,768]{1,0:T(8,128)(2,1)} %refs_3_.3, f32[1,768]{1,0:T(1,128)} %broadcast_in_dim.6.gain_ref.refs_4_, bf16[768,768]{1,0:T(8,128)(2,1)} %refs_6_.1, bf16[768,768]{1,0:T(8,128)(2,1)} %refs_7_.1, bf16[768,768]{1,0:T(8,128)(2,1)} %refs_8_.1), custom_call_target="tpu_custom_call" | custom-call | flops 3623878656 | bytes 11403264 | tf_op jit(solution)/shard_map/project/pallas_call | solution.py:629
  27.1 31.6 %attention_forward.1 = (bf16[1024,768]{1,0:T(8,128)(2,1)}, f32[1024,768]{1,0:T(8,128)}, bf16[12,1024,1024]{2,1,0:T(8,128)(2,1)}) custom-call(s32[1]{0:T(128)S(6)} %copy.63.len_ref, f32[2,12]{1,0:T(2,128)} %pad_maximum_fusion.far_ref, bf16[1024,2304]{1,0:T(8,128)(2,1)} %get-tuple-element.75.q_ref.k_ref.v_ref, ...), custom_call_target="tpu_custom_call" | custom-call | flops 12884901888 | bytes 34603008 | tf_op jit(solution)/shard_map/attention_forward/pallas_call | solution.py:497
  58.7 5.7 middle.1
  64.4 4.4 dispatch.2
  68.8 6.8 %all-to-all-start = ((bf16[8,128,768]{2,1,0:T(8,128)(2,1)}), bf16[8,128,768]{2,1,0:T(8,128)(2,1)S(1)}, u32[]{:S(2)}, u32[]{:S(2)}) async-start(bf16[8,128,768]{2,1,0:T(8,128)(2,1)} %bitcast.32), calls=%async_computation | async-start | bytes 3145728 | tf_op jit(solution)/shard_map/all_to_all | solution.py:615
  75.6 6.5 %dispatch_cotangent.1 = bf16[8,2,128,768]{3,2,1,0:T(8,128)(2,1)} custom-call(s32[1]{0:T(128)S(6)} %copy.63.len_ref, s32[2,1024]{1,0:T(2,128)} %get-tuple-element.76.srow_ref, bf16[1024,768]{1,0:T(8,128)(2,1)} %refs_3_.2), custom_call_target="tpu_custom_call" | custom-call | flops 3221225472 | bytes 4718592 | tf_op jit(solution)/shard_map/dispatch_cotangent/pallas_call | solution.py:622
  82.1 31.3 %all-to-all-done = bf16[8,128,768]{2,1,0:T(8,128)(2,1)S(1)} async-done(((bf16[8,128,768]{2,1,0:T(8,128)(2,1)}), bf16[8,128,768]{2,1,0:T(8,128)(2,1)S(1)}, u32[]{:S(2)}, u32[]{:S(2)}) %all-to-all-start) | async-done | bytes 1572896 | tf_op jit(solution)/shard_map/all_to_all | solution.py:615
  113.4 1.1 copy-done.8
  114.6 3.7 all-to-all-start.1
  118.3 0.8 copy.47.wr_ref
  119.1 0.5 compare_convert_fusion.1.hot_ref
  119.6 70.0 %all-to-all-done.1.g_ref = bf16[8,2,128,768]{3,2,1,0:T(8,128)(2,1)S(1)} async-done(((bf16[8,2,128,768]{3,2,1,0:T(8,128)(2,1)}), bf16[8,2,128,768]{3,2,1,0:T(8,128)(2,1)S(1)}, u32[]{:S(2)}, u32[]{:S(2)}) %all-to-all-start.1) | async-done | bytes 3145760 | tf_op jit(solution)/shard_map/all_to_all | solution.py:615
  189.7 1.7 copy-done.1
  191.3 44.3 %experts.2 = (bf16[1024,768]{1,0:T(8,128)(2,1)}, bf16[1024,768]{1,0:T(8,128)(2,1)}, bf16[4,768,768]{2,1,0:T(8,128)(2,1)}, bf16[4,768,768]{2,1,0:T(8,128)(2,1)}, f32[16,768]{1,0:T(8,128)}) custom-call(f32[1,16]{1,0:T(1,128)} %compare_convert_fusion.1.hot_ref, bf16[1024,768]{1,0:T(8,128)(2,1)} %bitcast.29, bf16[8,2,128,768]{3,2,1,0:T(8,128)(2,1)} %copy-done.1, ...), custom_call_target="tpu_custom_call" | custom-call | flops 28991029248 | bytes 25165824 | tf_op jit(solution)/shard_map/experts/pallas_call | solution.py:206
  235.7 0.7 reduce-scatter.15.cloned.1.call-update
  236.4 4.4 dispatch.3
  240.7 3.6 all-to-all-start.2
  244.3 0.2 reduce-scatter.17.cloned.1.call-start
  244.6 0.5 compare_convert_fusion.hot_ref
  245.1 37.0 %all-to-all-done.2 = bf16[8,128,768]{2,1,0:T(8,128)(2,1)S(1)} async-done(((bf16[8,128,768]{2,1,0:T(8,128)(2,1)}), bf16[8,128,768]{2,1,0:T(8,128)(2,1)S(1)}, u32[]{:S(2)}, u32[]{:S(2)}) %all-to-all-start.2) | async-done | bytes 1572896 | tf_op jit(solution)/shard_map/all_to_all | solution.py:615
  282.1 1.1 copy-done.9
  283.2 44.4 %experts.3 = (bf16[1024,768]{1,0:T(8,128)(2,1)}, bf16[1024,768]{1,0:T(8,128)(2,1)}, bf16[4,768,768]{2,1,0:T(8,128)(2,1)}, bf16[4,768,768]{2,1,0:T(8,128)(2,1)}, f32[16,768]{1,0:T(8,128)}) custom-call(f32[1,16]{1,0:T(1,128)} %compare_convert_fusion.hot_ref, bf16[1024,768]{1,0:T(8,128)(2,1)} %bitcast.30, bf16[8,2,128,768]{3,2,1,0:T(8,128)(2,1)} %copy-done.1, ...), custom_call_target="tpu_custom_call" | custom-call | flops 28991029248 | bytes 25165824 | tf_op jit(solution)/shard_map/experts/pallas_call | solution.py:206
  327.7 1.4 copy-done.4
  329.0 41.0 %all_to_all.35 = bf16[8,128,768]{2,1,0:T(8,128)(2,1)} all-to-all(bf16[8,128,768]{2,1,0:T(8,128)(2,1)S(1)} %bitcast.26), channel_id=1, replica_groups=mesh['dp'=4,'expert'=8] {'expert'}, dimensions={0} | all-to-all | bytes 3145728 | tf_op jit(solution)/shard_map/all_to_all | solution.py:615
  370.0 3.6 all-to-all-start.4
  373.6 0.5 reduce-scatter.19.cloned.1.call-update
  374.2 37.1 %all-to-all-done.4 = bf16[8,128,768]{2,1,0:T(8,128)(2,1)S(1)} async-done(((bf16[8,128,768]{2,1,0:T(8,128)(2,1)}), bf16[8,128,768]{2,1,0:T(8,128)(2,1)S(1)}, u32[]{:S(2)}, u32[]{:S(2)}) %all-to-all-start.4) | async-done | bytes 1572896 | tf_op jit(solution)/shard_map/all_to_all | solution.py:615
  411.3 3.8 all-to-all-start.5
  415.2 13.4 %combine.1 = (f32[1024,768]{1,0:T(8,128)}, bf16[1024,768]{1,0:T(8,128)(2,1)}, bf16[1024,768]{1,0:T(8,128)(2,1)}, f32[1,768]{1,0:T(1,128)}) custom-call(s32[1]{0:T(128)S(6)} %copy.63.len_ref, s32[1024,128]{1,0:T(8,128)} %get-tuple-element.74.scol_ref, bf16[1024,768]{1,0:T(8,128)(2,1)} %bitcast.27, bf16[1024,768]{1,0:T(8,128)(2,1)} %bitcast.28, ...), custom_call_target="tpu_custom_call" | custom-call | flops 4429185024 | bytes 16908288 | tf_op jit(solution)/shard_map/combine/pallas_call | solution.py:667
  428.7 24.2 %all-to-all-done.5 = bf16[8,128,768]{2,1,0:T(8,128)(2,1)S(1)} async-done(((bf16[8,128,768]{2,1,0:T(8,128)(2,1)}), bf16[8,128,768]{2,1,0:T(8,128)(2,1)S(1)}, u32[]{:S(2)}, u32[]{:S(2)}) %all-to-all-start.5) | async-done | bytes 1572896 | tf_op jit(solution)/shard_map/all_to_all | solution.py:615
  452.9 3.6 all-to-all-start.6
  456.5 35.5 %attention_backward.1 = (bf16[3,1024,768]{2,1,0:T(8,128)(2,1)}, f32[6,2,512]{2,1,0:T(2,128)}, f32[6,2,2,128]{3,2,1,0:T(2,128)}) custom-call(bf16[1024,2304]{1,0:T(8,128)(2,1)} %get-tuple-element.75.q_ref.k_ref.v_ref, bf16[1024,2304]{1,0:T(8,128)(2,1)} %get-tuple-element.75.q_ref.k_ref.v_ref, bf16[1024,2304]{1,0:T(8,128)(2,1)} %get-tuple-element.75.q_ref.k_ref.v_ref, ...), custom_call_target="tpu_custom_call" | custom-call | flops 25769803776 | bytes 34603008 | tf_op jit(solution)/shard_map/attention_backward/pallas_call | solution.py:587
  492.0 0.8 reduce_sum.11
  492.9 0.1 copy.58
  493.1 0.1 copy.50
  493.2 0.1 copy.51
  493.3 0.8 reshape.199
  494.1 0.1 fusion.2
  494.3 0.1 scatter-add.6
  494.5 0.3 scatter-add.9
  494.9 0.1 reshape.202
  495.0 0.7 fusion.refs_11_
  495.7 10.4 %weight_gradients.1 = bf16[4,768,768]{2,1,0:T(8,128)(2,1)} custom-call(bf16[1024,768]{1,0:T(8,128)(2,1)} %get-tuple-element.97.h_ref, bf16[1024,768]{1,0:T(8,128)(2,1)} %get-tuple-element.77.o_ref, bf16[3,1024,768]{2,1,0:T(8,128)(2,1)} %get-tuple-element.95.d_ref.refs_5_, bf16[1024,768]{1,0:T(8,128)(2,1)} %get-tuple-element.98.gb_ref), custom_call_target="tpu_custom_call" | custom-call | flops 4831838208 | bytes 14155776 | tf_op jit(solution)/shard_map/weight_gradients/pallas_call | solution.py:677
  506.2 1.1 copy-done.3
  507.3 88.4 %last.1 = (bf16[1024,768]{1,0:T(8,128)(2,1)}, bf16[1024,768]{1,0:T(8,128)(2,1)}, bf16[3072,768]{1,0:T(8,128)(2,1)}, f32[24,768]{1,0:T(8,128)}) custom-call(s32[1]{0:T(128)S(6)} %copy.63.len_ref, s32[1024,128]{1,0:T(8,128)} %get-tuple-element.74.scol_ref, bf16[1024,768]{1,0:T(8,128)(2,1)} %bitcast.24, bf16[1024,768]{1,0:T(8,128)(2,1)} %bitcast.25, ...), custom_call_target="tpu_custom_call" | custom-call | flops 6845104128 | bytes 22413312 | tf_op jit(solution)/shard_map/last/pallas_call | solution.py:692
  595.7 0.7 slice_reduce_fusion.2
  596.4 0.1 reshape_squeeze.3
  596.5 0.7 copy.53
  597.2 1.4 slice_reduce_fusion
  598.7 1.4 slice_bitcast_fusion
  600.1 3.9 maximum_convert_fusion
  604.0 3.8 fusion.9
  607.8 3.9 maximum_convert_fusion.1
  611.7 1.1 copy.64
  612.9 0.8 copy-done.5
  613.7 1.1 copy.65
  (47 shorter events, 0.9 us)
Async XLA Ops:
  68.8 44.6 %all-to-all-start = ((bf16[8,128,768]{2,1,0:T(8,128)(2,1)}), bf16[8,128,768]{2,1,0:T(8,128)(2,1)S(1)}, u32[]{:S(2)}, u32[]{:S(2)}) async-start(bf16[8,128,768]{2,1,0:T(8,128)(2,1)} %bitcast.32), calls=%async_computation | async-start | bytes 3145728 | tf_op jit(solution)/shard_map/all_to_all | solution.py:615
  82.1 36.1 %copy-start.14 = (bf16[768,16]{0,1:T(8,128)(2,1)S(1)}, bf16[768,16]{0,1:T(8,128)(2,1)}, u32[]{:S(2)}) copy-start(bf16[768,16]{0,1:T(8,128)(2,1)} %param.27) | copy-start | bytes 73732
  113.4 1.1 copy-start.8
  114.6 75.1 %all-to-all-start.1 = ((bf16[8,2,128,768]{3,2,1,0:T(8,128)(2,1)}), bf16[8,2,128,768]{3,2,1,0:T(8,128)(2,1)S(1)}, u32[]{:S(2)}, u32[]{:S(2)}) async-start(bf16[8,2,128,768]{3,2,1,0:T(8,128)(2,1)} %dispatch_cotangent.1), calls=%async_computation.1 | async-start | bytes 6291456 | tf_op jit(solution)/shard_map/all_to_all | solution.py:615
  118.2 310.4 %reduce-scatter.13.cloned.1.call-start = ((), (), s32[]{:S(2)}) async-start(), calls=%async_computation.11 | async-start | bytes 5898240
  189.7 1.7 copy-start.1
  235.6 193.1 %reduce-scatter.15.cloned.1.call-start = ((), (), s32[]{:S(2)}) async-start(), calls=%async_computation.12 | async-start | bytes 5898240
  240.7 41.3 %all-to-all-start.2 = ((bf16[8,128,768]{2,1,0:T(8,128)(2,1)}), bf16[8,128,768]{2,1,0:T(8,128)(2,1)S(1)}, u32[]{:S(2)}, u32[]{:S(2)}) async-start(bf16[8,128,768]{2,1,0:T(8,128)(2,1)} %bitcast.31), calls=%async_computation.2 | async-start | bytes 3145728 | tf_op jit(solution)/shard_map/all_to_all | solution.py:615
  244.3 355.7 %reduce-scatter.17.cloned.1.call-start = ((), (), s32[]{:S(2)}) async-start(), calls=%async_computation.13 | async-start | bytes 5898240
  282.1 1.1 copy-start.9
  327.6 1.4 copy-start.4
  370.0 41.3 %all-to-all-start.4 = ((bf16[8,128,768]{2,1,0:T(8,128)(2,1)}), bf16[8,128,768]{2,1,0:T(8,128)(2,1)S(1)}, u32[]{:S(2)}, u32[]{:S(2)}) async-start(bf16[8,128,768]{2,1,0:T(8,128)(2,1)} %bitcast.8), calls=%async_computation.4 | async-start | bytes 3145728 | tf_op jit(solution)/shard_map/all_to_all | solution.py:615
  373.6 234.2 %reduce-scatter.19.cloned.1.call-start = ((), (), s32[]{:S(2)}) async-start(), calls=%async_computation.14 | async-start | bytes 5898240
  374.2 41.0 %copy-start.12 = (f32[16,768]{1,0:T(8,128)S(1)}, f32[16,768]{1,0:T(8,128)}, u32[]{:S(2)}) copy-start(f32[16,768]{1,0:T(8,128)} %get-tuple-element.102) | copy-start | bytes 147460
  374.2 41.0 %copy-start.13 = (f32[16,768]{1,0:T(8,128)S(1)}, f32[16,768]{1,0:T(8,128)}, u32[]{:S(2)}) copy-start(f32[16,768]{1,0:T(8,128)} %get-tuple-element.103) | copy-start | bytes 147460
  411.3 3.9 copy-start.7
  411.3 41.5 %all-to-all-start.5 = ((bf16[8,128,768]{2,1,0:T(8,128)(2,1)}), bf16[8,128,768]{2,1,0:T(8,128)(2,1)S(1)}, u32[]{:S(2)}, u32[]{:S(2)}) async-start(bf16[8,128,768]{2,1,0:T(8,128)(2,1)} %bitcast.10), calls=%async_computation.5 | async-start | bytes 3145728 | tf_op jit(solution)/shard_map/all_to_all | solution.py:615
  452.9 39.1 %copy-start.2 = (bf16[8,128,768]{2,1,0:T(8,128)(2,1)}, bf16[8,128,768]{2,1,0:T(8,128)(2,1)S(1)}, u32[]{:S(2)}) copy-start(bf16[8,128,768]{2,1,0:T(8,128)(2,1)S(1)} %all-to-all-done.5) | copy-start | bytes 4718596
  452.9 53.3 %all-to-all-start.6 = ((bf16[8,128,768]{2,1,0:T(8,128)(2,1)}), bf16[8,128,768]{2,1,0:T(8,128)(2,1)S(1)}, u32[]{:S(2)}, u32[]{:S(2)}) async-start(bf16[8,128,768]{2,1,0:T(8,128)(2,1)} %bitcast.12), calls=%async_computation.6 | async-start | bytes 3145728 | tf_op jit(solution)/shard_map/all_to_all | solution.py:615
  456.5 38.5 %copy-start.15 = (f32[1,768]{1,0:T(1,128)S(1)}, f32[1,768]{1,0:T(1,128)}, u32[]{:S(2)}) copy-start(f32[1,768]{1,0:T(1,128)} %get-tuple-element.99) | copy-start | bytes 9220
  506.2 1.1 copy-start.3
  507.3 92.8 %copy-start.11 = (bf16[1,768,768]{2,1,0:T(8,128)(2,1)S(1)}, bf16[1,768,768]{2,1,0:T(8,128)(2,1)}, u32[]{:S(2)}) copy-start(bf16[1,768,768]{2,1,0:T(8,128)(2,1)} %reduce-scatter.13.cloned.1.call-done) | copy-start | bytes 3538948
  600.1 3.9 copy-start
  604.0 3.8 copy-start.10
  607.8 3.9 copy-start.6
  611.7 2.0 copy-start.5
Sparse Core Ops, SparseCore 0:
  235.8 55.9 reduce-scatter.12
  294.8 57.0 reduce-scatter.14
  354.9 57.0 reduce-scatter.16
  414.9 57.1 reduce-scatter.18

commit v3 on v2

--- a/solution.py
+++ b/solution.py
@@ -60,7 +60,7 @@
     return jax.ShapeDtypeStruct(shape, kind)
 
 
-def call(kernel, name, grid, in_specs, out_specs, out_shape, scratch=(), flops=0, moved=0, transcendentals=0, **params):
+def call(kernel, name, grid, in_specs, out_specs, out_shape, scratch=(), flops=0, moved=0, transcendentals=0, vmem=BIG, **params):
     return pl.pallas_call(
         kernel,
         grid=grid,
@@ -68,7 +68,7 @@
         out_specs=out_specs,
         out_shape=out_shape,
         scratch_shapes=list(scratch),
-        compiler_params=pltpu.CompilerParams(vmem_limit_bytes=BIG, **params),
+        compiler_params=pltpu.CompilerParams(vmem_limit_bytes=vmem, **params),
         cost_estimate=pl.CostEstimate(flops=int(flops), bytes_accessed=int(moved), transcendentals=int(transcendentals)),
         name=name,
     )
@@ -130,87 +130,206 @@
     h_ref[...] = jnp.where(live, h, 0.0).astype(BF)
 
 
-def dispatch_kernel(e, srow_ref, h_ref, out_ref):
-    out_ref[...] = dispatch_rows(srow_ref[e:e + 1, :], h_ref[...], out_ref.shape[0])
-
-
-def expert_kernel(hot_ref, h_ref, g_ref, w1_ref, w2_ref, wr_ref, rows_ref, back_ref, d1_ref, d2_ref, dr_ref,
-                  ht_s, gr_s, gate_s, act_s, gp_s, rows_s, sent_s):
-    f = pl.program_id(0)
-    last = pl.num_programs(0) - 1
-    S = h_ref.shape[0]
+def dp_partners(me):
+    first, second = me % 2, me // 2
+    return me + 1 - 2 * first, me + 2 - 4 * second, 3 - me
+
+
+def remote(src, dst, send_sem, recv_sem, who):
+    return pltpu.make_async_remote_copy(src_ref=src, dst_ref=dst, send_sem=send_sem, recv_sem=recv_sem, device_id=who,
+                                        device_id_type=pl.DeviceIdType.MESH)
+
+
+class Exchange:
+    def __init__(self, src, dst, send_sems, recv_sems, own_sem):
+        self.me = lax.axis_index("expert")
+        self.n = lax.axis_size("expert")
+        self.src, self.dst, self.send, self.recv, self.own = src, dst, send_sems, recv_sems, own_sem
+
+    def copy(self, k):
+        to = lax.rem(self.me + k, self.n)
+        return remote(self.src(to), self.dst(self.me), self.send.at[k], self.recv.at[k], {"expert": to})
+
+    def mine(self):
+        return pltpu.make_async_copy(self.src(self.me), self.dst(self.me), self.own)
+
+    def each(self, what):
+        def one(k, _):
+            what(self.copy(k))
+            return 0
+
+        lax.fori_loop(1, self.n, one, 0)
+
+    def start(self):
+        self.each(lambda c: c.start())
+        self.mine().start()
+
+    def wait(self):
+        self.each(lambda c: c.wait())
+        self.mine().wait()
+
+
+def greet(who):
+    barrier = pltpu.get_barrier_semaphore()
+    for device in who:
+        pl.semaphore_signal(barrier, inc=1, device_id=device, device_id_type=pl.DeviceIdType.MESH)
+    me, n = lax.axis_index("expert"), lax.axis_size("expert")
+
+    def one(k, _):
+        pl.semaphore_signal(barrier, inc=1, device_id={"expert": lax.rem(me + k, n)}, device_id_type=pl.DeviceIdType.MESH)
+        return 0
+
+    lax.fori_loop(1, n, one, 0)
+    pl.semaphore_wait(barrier, len(who) + n - 1)
+
+
+def router(h, wr):
+    logits = dot(h, wr)
+    ex = jnp.exp(logits - jnp.max(logits, axis=1, keepdims=True))
+    return ex / jnp.sum(ex, axis=1, keepdims=True)
+
+
+def experts_kernel(srow_ref, hot_ref, h_ref, g_ref, w1_ref, w2_ref, wr_ref,
+                   rows_ref, back0_ref, back1_ref, d_ref, part_ref, dr_ref,
+                   send_s, land_s, ht_s, gr_s, gate_s, act_s, gp_s, rows_s, sent_s, stage_s,
+                   h_send, h_recv, h_own, b_send, b_recv, b_own, d_local, r_send, r_recv):
+    step = pl.program_id(0)
+    e = step // 8
+    f = step % 8
+    _, peers, most, D = land_s.shape
+    S = peers * most
+    group = RB // most
+    me_dp = lax.axis_index("dp")
+    by_x, by_y, by_xy = dp_partners(me_dp)
+    backs = (back0_ref, back1_ref)
+
+    def block(buffer, which):
+        return lambda j: buffer.at[which, pl.ds(pl.multiple_of(j * most, 16), most)]
+
+    h_moves = [Exchange(block(send_s, n), lambda j, n=n: land_s.at[n, j], h_send.at[n], h_recv.at[n], h_own.at[n]) for n in range(2)]
+    b_moves = [Exchange(block(send_s, n), lambda j, n=n: backs[n].at[j], b_send.at[n], b_recv.at[n], b_own.at[n]) for n in range(2)]
+    order = (by_xy, by_x, by_y, me_dp)
+
+    def store(n, t):
+        return [pltpu.make_async_copy(stage_s.at[t % 2, m], d_ref.at[n, m, order[t]], d_local.at[t % 2, m]) for m in range(2)]
+
+    def first_stage(n, m, k, sem):
+        tile = (by_xy, (by_x, by_y)[m])[k]
+        return remote(d_ref.at[n, m, tile], part_ref.at[n, m, k], r_send.at[sem], r_recv.at[sem], {"dp": (by_x, by_y)[m]})
+
+    early = [first_stage(0, 0, 0, 0), first_stage(0, 1, 0, 1), first_stage(0, 0, 1, 2), first_stage(0, 1, 1, 3), first_stage(1, 0, 0, 4), first_stage(1, 1, 0, 5)]
+
+    @pl.when(step == 0)
+    def _():
+        send_s[0] = dispatch_rows(srow_ref[0:1, :], h_ref[...], S)
+        greet([{"dp": by_x}, {"dp": by_y}])
+        h_moves[0].start()
+        send_s[1] = dispatch_rows(srow_ref[1:2, :], h_ref[...], S)
+        h_moves[0].wait()
+        h_moves[1].start()
+
+    @pl.when(step == 8)
+    def _():
+        h_moves[1].wait()
 
     @pl.when(f == 0)
     def _():
-        h = h_ref[...]
-        ht_s[...] = h.T
-        logits = dot(h, wr_ref[...])
-        top = jnp.max(logits, axis=1, keepdims=True)
-        ex = jnp.exp(logits - top)
-        probs = ex / jnp.sum(ex, axis=1, keepdims=True)
-        gate = jnp.sum(probs * hot_ref[...], axis=1, keepdims=True)
+        h = land_s[e].reshape(S, D)
+        gate = jnp.sum(router(h, wr_ref[...]) * hot_ref[e], axis=1, keepdims=True)
         gate_s[...] = jnp.broadcast_to(gate, gate_s.shape)
-        gr_s[...] = (gate * g_ref[:, 0].reshape(h.shape).astype(F32)).astype(BF)
-
-    w1 = w1_ref[0]
-    w2 = w2_ref[0]
-    for c in range(S // RB):
-        sl = slice(c * RB, (c + 1) * RB)
-        v = dot(h_ref[sl], w1)
-        ga = dot_nt(gr_s[sl], w2)
-        v2 = v * v
-        t = jnp.tanh(v * (GELU_C + (GELU_C * GELU_A) * v2))
-        half = 0.5 + 0.5 * t
-        act = v * half
-        slope = half + 2.0 * act * (1.0 - half) * (GELU_C + (3.0 * GELU_C * GELU_A) * v2)
-        actb = act.astype(BF)
-        gpre = (ga * slope).astype(BF)
-        act_s[sl] = actb
-        gp_s[sl] = gpre
-        r = dot(actb, w2)
-        s = dot_nt(gpre, w1)
-
-        @pl.when(f == 0)
-        def _():
-            rows_s[sl] = r
-            sent_s[sl] = s
-
-        @pl.when(f > 0)
-        def _():
-            rows_s[sl] += r
-            sent_s[sl] += s
-
-    d1_ref[0] = dot(ht_s[...], gp_s[...]).astype(BF)
-    d2_ref[0] = dot_tn(act_s[...], gr_s[...]).astype(BF)
-
-    @pl.when(f == last)
+        gr_s[...] = (gate * g_ref[:, 0].reshape(S, D).astype(F32)).astype(BF)
+        rows_s[...] = jnp.zeros_like(rows_s)
+        sent_s[...] = jnp.zeros_like(sent_s)
+
+    @pl.when(f < 4)
+    def _():
+        w1 = w1_ref[0]
+        w2 = w2_ref[0]
+        for c in range(S // RB):
+            sl = slice(c * RB, (c + 1) * RB)
+            v = dot(land_s[e, c * group:(c + 1) * group].reshape(RB, D), w1)
+            ga = dot_nt(gr_s[sl], w2)
+            v2 = v * v
+            t = jnp.tanh(v * (GELU_C + (GELU_C * GELU_A) * v2))
+            half = 0.5 + 0.5 * t
+            act = v * half
+            slope = half + 2.0 * act * (1.0 - half) * (GELU_C + (3.0 * GELU_C * GELU_A) * v2)
+            actb = act.astype(BF)
+            gpre = (ga * slope).astype(BF)
+            act_s[f, sl] = actb
+            gp_s[f, sl] = gpre
+            rows_s[sl] += dot(actb, w2)
+            sent_s[sl] += dot_nt(gpre, w1)
+
+    @pl.when(f == 3)
     def _():
         rows = rows_s[...].astype(BF).astype(F32)
         gate = gate_s[:, :1]
-        rows_ref[...] = (gate * rows).astype(BF)
-        grad_gate = jnp.sum(rows * g_ref[:, 0].reshape(rows.shape).astype(F32), axis=1, keepdims=True)
-        logits = dot(h_ref[...], wr_ref[...])
-        top = jnp.max(logits, axis=1, keepdims=True)
-        ex = jnp.exp(logits - top)
-        probs = ex / jnp.sum(ex, axis=1, keepdims=True)
-        gl = (grad_gate * gate * (hot_ref[...] - probs)).astype(BF)
-        dr_ref[...] = dot_tn(gl, h_ref[...])
-        back_ref[...] = (sent_s[...] + dot_nt(gl, wr_ref[...])).astype(BF)
-
-
-def experts_run(e, parts, hot, h, g, first, second, router):
-    S, D = h.shape
-    FF = first.shape[2]
-    FT = FF // parts
-    E = router.shape[1]
-    return call(
-        expert_kernel, "experts", (parts,),
-        [whole(1, E), whole(S, D), pl.BlockSpec((g.shape[0], 1, g.shape[2], D), lambda f: (0, e, 0, 0)), pl.BlockSpec((1, D, FT), lambda f: (e, 0, f)), pl.BlockSpec((1, FT, D), lambda f: (e, f, 0)), whole(D, E)],
-        [whole(S, D), whole(S, D), pl.BlockSpec((1, D, FT), lambda f: (f, 0, 0)), pl.BlockSpec((1, FT, D), lambda f: (f, 0, 0)), whole(E, D)],
-        [struct((S, D), BF), struct((S, D), BF), struct((parts, D, FT), BF), struct((parts, FT, D), BF), struct((E, D), F32)],
-        [pltpu.VMEM((D, S), BF), pltpu.VMEM((S, D), BF), pltpu.VMEM((S, 128), F32), pltpu.VMEM((S, FT), BF), pltpu.VMEM((S, FT), BF), pltpu.VMEM((S, D), F32), pltpu.VMEM((S, D), F32)],
-        flops=12 * S * D * FF, moved=8 * D * FF + 8 * S * D, transcendentals=S * FF,
-    )(hot, h, g, first, second, router)
+        rows_ref[0] = (gate * rows).astype(BF)
+        grad_gate = jnp.sum(rows * g_ref[:, 0].reshape(S, D).astype(F32), axis=1, keepdims=True)
+        h = land_s[e].reshape(S, D)
+        gl = (grad_gate * gate * (hot_ref[e] - router(h, wr_ref[...]))).astype(BF)
+        send_s[e] = (sent_s[...] + dot_nt(gl, wr_ref[...])).astype(BF)
+        dr = dot_tn(gl, h)
+
+        @pl.when(e == 0)
+        def _():
+            dr_ref[...] = dr
+
+        @pl.when(e > 0)
+        def _():
+            dr_ref[...] += dr
+
+    for n in range(2):
+        @pl.when(step == 8 * n + 3)
+        def _(n=n):
+            b_moves[n].start()
+
+    @pl.when(f == 4)
+    def _():
+        ht_s[...] = land_s[e].reshape(S, D).T
+
+    for n in range(2):
+        for t in range(4):
+            @pl.when(step == 8 * n + 4 + t)
+            def _(n=n, t=t):
+                if t >= 1:
+                    for c in store(n, t - 1):
+                        c.wait()
+                if n == 0 and t == 1:
+                    early[0].start()
+                    early[1].start()
+                if n == 0 and t == 2:
+                    early[2].start()
+                if n == 0 and t == 3:
+                    early[3].start()
+                if n == 1 and t == 1:
+                    early[4].start()
+                    early[5].start()
+
+    @pl.when(f >= 4)
+    def _():
+        tile = jnp.where(f == 4, by_xy, jnp.where(f == 5, by_x, jnp.where(f == 6, by_y, me_dp)))
+        slot = f % 2
+        stage_s[slot, 0] = dot(ht_s[...], gp_s[tile]).astype(BF)
+        stage_s[slot, 1] = dot_tn(act_s[tile], gr_s[...]).astype(BF)
+
+    for n in range(2):
+        for t in range(4):
+            @pl.when(step == 8 * n + 4 + t)
+            def _(n=n, t=t):
+                for c in store(n, t):
+                    c.start()
+                if t == 3:
+                    for c in store(n, t):
+                        c.wait()
+
+    @pl.when(step == 15)
+    def _():
+        for n in range(2):
+            b_moves[n].wait()
+        for c in early:
+            c.wait()
 
 
 def norm_back(v, gain, upstream):
@@ -348,10 +467,8 @@
     return stages
 
 
-def last_kernel(local, len_ref, scol_ref, *refs):
-    rows = refs[:local]
-    (middle_ref, x_ref, gain_ref, d_ref, wq_ref, wk_ref, wv_ref, gm_ref, dw_ref, small_ref,
-     mixed_ref, token_ref, sums_ref, small_out, acc, recv, out, sacc, srecv, gain_s, send_sem, recv_sem, local_sem) = refs[local:]
+def last_kernel(x_ref, gain_ref, d_ref, wq_ref, wk_ref, wv_ref, gm_ref, dw_ref, small_ref,
+                token_ref, sums_ref, small_out, acc, recv, out, sacc, srecv, gain_s, send_sem, recv_sem, local_sem):
     r = pl.program_id(0)
     steps = pl.num_programs(0)
     orders = bit_orders()
@@ -384,11 +501,6 @@
     gv, gg = norm_back(x_ref[...].astype(F32), gain_ref[...], gh)
     token_ref[...] = (gm_ref[...] + gv).astype(BF)
     gs = jnp.sum(gg, axis=0, keepdims=True)
-    T = x_ref.shape[0]
-    scol = scol_ref[...]
-    got = sum(dot(combine_hot(scol, b.shape[0], e), b[...]) for e, b in enumerate(rows))
-    live = iota((T, 1), 0) + r * T < len_ref[0]
-    mixed_ref[...] = jnp.where(live, middle_ref[...] + got, 0.0).astype(BF)
 
     @pl.when(r == 0)
     def _():
@@ -422,6 +534,16 @@
                 smalls[done][0]()
         sums_ref[...] = out[...]
         small_out[...] = sacc[len(smalls)]
+
+
+def mixed_kernel(local, len_ref, scol_ref, *refs):
+    rows = refs[:local]
+    middle_ref, out_ref = refs[local:]
+    r = pl.program_id(0)
+    scol = scol_ref[...]
+    got = sum(dot(combine_hot(scol, b.shape[0], e), b[...]) for e, b in enumerate(rows))
+    live = iota((RB, 1), 0) + r * RB < len_ref[0]
+    out_ref[...] = jnp.where(live, middle_ref[...] + got, 0.0).astype(BF)
 
 
 def near_bias(w_row):
@@ -624,6 +746,7 @@
         [SMEM, whole(local, L), whole(L, D)], whole(peers, local, most, D), struct((peers, local, most, D), BF),
         flops=2 * local * S * L * D, moved=2 * (1 + local) * S * D,
     )(lengths, srow, cotangent)
+    g_sent, tokens = lax.optimization_barrier((g_sent, tokens))
     g_got = exchange(g_sent)
 
     h_one, qkv = call(
@@ -645,24 +768,24 @@
         [SMEM, rows_of(D), rows_of(D), whole(D, D), whole(1, D)], [rows_of(D), rows_of(D)],
         [struct((L, D), F32), struct((L, D), BF)], flops=2 * L * D * D, moved=2 * D * D + 10 * L * D,
     )(lengths, tokens, o, out_weight, gain_2)
-    h_got = []
-    for e in range(local):
-        sent = call(
-            functools.partial(dispatch_kernel, e), "dispatch", (1,),
-            [whole(local, L), whole(L, D)], whole(S, D), struct((S, D), BF), flops=2 * S * L * D, moved=4 * S * D,
-        )(srow, h_two)
-        h_got.append(exchange(sent.reshape(peers, most, D)).reshape(S, D))
-
-    runs = []
-    for e in range(local):
-        hot = (jnp.arange(experts, dtype=I32) == me * local + e).astype(F32)[None, :]
-        runs.append(experts_run(e, n_dp, hot, h_got[e], g_got, expert_in, expert_out, router_weight))
-    backs = [exchange(run[1].reshape(peers, most, D)).reshape(S, D) for run in runs]
-    *rows_sent, backs[0] = lax.optimization_barrier((*[run[0] for run in runs], backs[0]))
-    rows_got = [exchange(v.reshape(peers, most, D)).reshape(S, D) for v in rows_sent]
-    d_first = [lax.psum_scatter(run[2], "dp", scatter_dimension=0, tiled=True) for run in runs]
-    d_second = [lax.psum_scatter(run[3], "dp", scatter_dimension=0, tiled=True) for run in runs]
-    d_router = sum(run[4] for run in runs)
+    FF = expert_in.shape[2]
+    FT = FF // 4
+    hot = (jnp.arange(experts, dtype=I32)[None, :] == me * local + jnp.arange(local, dtype=I32)[:, None]).astype(F32)[:, None, :]
+    anywhere = pl.BlockSpec(memory_space=pl.ANY)
+    dma = pltpu.SemaphoreType.DMA
+    rows_sent, *backs, d_tiles, d_parts, d_router = call(
+        experts_kernel, "experts", (16,),
+        [whole(local, L), whole(local, 1, experts), whole(L, D), pl.BlockSpec((peers, 1, most, D), lambda s: (0, s // 8, 0, 0)),
+         pl.BlockSpec((1, D, FT), lambda s: (s // 8, 0, jnp.minimum(s % 8, 3))), pl.BlockSpec((1, FT, D), lambda s: (s // 8, jnp.minimum(s % 8, 3), 0)), whole(D, experts)],
+        [pl.BlockSpec((1, S, D), lambda s: (s // 8, 0, 0)), anywhere, anywhere, anywhere, anywhere, whole(experts, D)],
+        [struct((2, S, D), BF), struct((peers, most, D), BF), struct((peers, most, D), BF), struct((2, 2, 4, D, D), BF), struct((2, 2, 2, D, D), BF), struct((experts, D), F32)],
+        [pltpu.VMEM((2, S, D), BF), pltpu.VMEM((2, peers, most, D), BF), pltpu.VMEM((D, S), BF), pltpu.VMEM((S, D), BF), pltpu.VMEM((S, 128), F32),
+         pltpu.VMEM((4, S, FT), BF), pltpu.VMEM((4, S, FT), BF), pltpu.VMEM((S, D), F32), pltpu.VMEM((S, D), F32), pltpu.VMEM((2, 2, D, D), BF),
+         dma((2, peers)), dma((2, peers)), dma((2,)), dma((2, peers)), dma((2, peers)), dma((2,)), dma((2, 2)), dma((6,)), dma((6,))],
+        flops=24 * S * D * FF, moved=24 * D * FF + 16 * S * D, transcendentals=2 * S * FF, vmem=62 * 2**20, collective_id=2, has_side_effects=True,
+    )(srow, hot, h_two, g_got, expert_in, expert_out, router_weight)
+    backs = [b.reshape(S, D) for b in backs]
+    rows_got = [exchange(rows_sent[e].reshape(peers, most, D)).reshape(S, D) for e in range(local)]
 
     gm, gb, do, d_gain_2 = call(
         functools.partial(combine_kernel, local), "combine", (steps,),
@@ -671,7 +794,6 @@
         [struct((L, D), F32), struct((L, D), BF), struct((L, D), BF), struct((1, D), F32)],
         flops=2 * local * S * L * D + 2 * L * D * D, moved=2 * D * D + 20 * L * D,
     )(lengths, scol, *backs, middle, cotangent, inv, out_weight, gain_2)
-    d_first[0], d_second[0], do = lax.optimization_barrier((d_first[0], d_second[0], do))
     d_heads, near_sums, far_sums = attn_bwd(qkv, do, o, p)
     d_heads, rows_got[0] = lax.optimization_barrier((d_heads, rows_got[0]))
     d_weights = call(
@@ -689,17 +811,22 @@
     orders = (n_dp * peers).bit_length() - 1
     part = pl.BlockSpec((T, D), lambda r: (r, 0))
     sems = 5 * orders
-    mixed, grad_tokens, sums, small = call(
-        functools.partial(last_kernel, local), "last", (L // T,),
-        [SMEM, pl.BlockSpec((T, 128), lambda r: (r, 0))] + [whole(S, D)] * local
-        + [part, part, whole(1, D), pl.BlockSpec((3, T, D), lambda r: (0, r, 0))] + [whole(D, D)] * 3
+    grad_tokens, sums, small = call(
+        last_kernel, "last", (L // T,),
+        [part, whole(1, D), pl.BlockSpec((3, T, D), lambda r: (0, r, 0))] + [whole(D, D)] * 3
         + [part, pl.BlockSpec(memory_space=pl.ANY), whole(*small.shape)],
-        [part, part, whole(4 * D, D), whole(*small.shape)],
-        [struct((L, D), BF), struct((L, D), BF), struct((4 * D, D), BF), struct(small.shape, F32)],
-        [pltpu.VMEM((4 * D, D), BF), pltpu.VMEM((4 * D + 96 * orders, D), BF), pltpu.VMEM((4 * D, D), BF)] + [pltpu.VMEM((orders + 1, *small.shape), F32), pltpu.VMEM((orders, *small.shape), F32), pltpu.VMEM((8, D), F32),
-         pltpu.SemaphoreType.DMA((sems,)), pltpu.SemaphoreType.DMA((sems,)), pltpu.SemaphoreType.DMA],
-        flops=6 * L * D * D + 2 * local * S * L * D, moved=6 * D * D + 24 * L * D, collective_id=1, has_side_effects=True,
-    )(lengths, scol, *rows_got, middle, tokens, gain_1, d_heads, query_weight, key_weight, value_weight, gm, d_weights.reshape(4 * D, D), small)
+        [part, whole(4 * D, D), whole(*small.shape)],
+        [struct((L, D), BF), struct((4 * D, D), BF), struct(small.shape, F32)],
+        [pltpu.VMEM((4 * D, D), BF), pltpu.VMEM((4 * D + 96 * orders, D), BF), pltpu.VMEM((4 * D, D), BF)]
+        + [pltpu.VMEM((orders + 1, *small.shape), F32), pltpu.VMEM((orders, *small.shape), F32), pltpu.VMEM((8, D), F32),
+           pltpu.SemaphoreType.DMA((sems,)), pltpu.SemaphoreType.DMA((sems,)), pltpu.SemaphoreType.DMA],
+        flops=6 * L * D * D, moved=6 * D * D + 20 * L * D, collective_id=1, has_side_effects=True,
+    )(tokens, gain_1, d_heads, query_weight, key_weight, value_weight, gm, d_weights.reshape(4 * D, D), small)
+    mixed = call(
+        functools.partial(mixed_kernel, local), "mixed", (steps,),
+        [SMEM, rows_of(128)] + [whole(S, D)] * local + [rows_of(D)], rows_of(D), struct((L, D), BF),
+        flops=2 * local * S * L * D, moved=10 * S * D,
+    )(lengths, scol, *rows_got, middle)
 
     sums = sums.astype(F32)
     return (
@@ -713,8 +840,8 @@
         sums[3 * D:],
         small[2, :buckets * heads].reshape(buckets, heads),
         small[8:].T,
-        jnp.concatenate(d_first, axis=0).astype(F32),
-        jnp.concatenate(d_second, axis=0).astype(F32),
+        lax.psum_scatter(d_tiles[:, 0], 'dp', scatter_dimension=1, tiled=True)[:, 0].astype(F32),
+        lax.psum_scatter(d_tiles[:, 1], 'dp', scatter_dimension=1, tiled=True)[:, 0].astype(F32),
     )
 
 

time: 630 us -> 659 us (1.046)
  Pallas kernels: 301 us -> 377 us
  blocking collectives: 41 us -> 0 us
  waiting for transfers between devices: 201 us -> 189 us
  local copies, waits for them, and re-layouts: 26.4 us -> 34.1 us
    all_to_all x6 -> x3, waiting for transfers between devices: 200 us -> 45.9 us  [exchange(): lax.all_to_all(values, 'expert', split_axis=0, concat_axis=0, tiled=True)]
    unnamed x6 -> x2, waiting for transfers between devices: 1.25 us -> 144 us
    pallas_call x5 -> x3, Pallas kernels: 186 us -> 261 us  [the longest x1 144 us: body(): call(experts_kernel, 'experts', (16,), [whole(local, L), whole(local, 1,...]
    all_to_all x1 -> x0, blocking collectives: 41 us -> none  [exchange(): lax.all_to_all(values, 'expert', split_axis=0, concat_axis=0, tiled=True)]
    squeeze x0 -> x1, local copies, waits for them, and re-layouts: none -> 14.1 us  [body(): d_tiles[:, 1]]
    unnamed x41 -> x33, local copies, waits for them, and re-layouts: 13.2 us -> 7.22 us
    all_to_all x6 -> x3, starting transfers between devices: 25.1 us -> 23.6 us  [exchange(): lax.all_to_all(values, 'expert', split_axis=0, concat_axis=0, tiled=True)]
  transfers between devices with their start and end apart: 10 -> 4, of which waited for: 5 -> 3; matrix products, arithmetic and copies ran while one was open for 3% -> 3% of each run, Pallas kernels for 33% -> 34%
where the time goes in v3:
time: 659 us; the launch traced here: 650 us
  Pallas kernels  377 us (57%)
  waiting for transfers between devices  189 us (29%)
  local copies, waits for them, and re-layouts  34.1 us (5%)
  starting transfers between devices  23.6 us (4%)
  between operations  15.3 us (2%)
  other arithmetic  10.6 us (2%)
    pallas_call x1, Pallas kernels, body(): call(experts_kernel, 'experts', (16,), [whole(local, L), whole(local, 1,...  144 us
    unnamed x2, waiting for transfers between devices  144 us
    pallas_call x1, Pallas kernels, body(): call(last_kernel, 'last', (L // T,), [part, whole(1, D), pl.BlockSpec((3,...  109 us
    all_to_all x3, waiting for transfers between devices, exchange(): lax.all_to_all(values, 'expert', split_axis=0, concat_axis=0, tiled=True)  45.9 us
    pallas_call x1, Pallas kernels, attn_bwd(): pl.pallas_call(attn_bwd_kernel, grid=(pairs,), in_specs=[blk(0), blk(pair...  35.9 us
    pallas_call x1, Pallas kernels, attn_fwd(): pl.pallas_call(attn_fwd_kernel, grid=(pairs,), in_specs=[SMEM, SMEM, blk(...  31.6 us
    all_to_all x3, starting transfers between devices, exchange(): lax.all_to_all(values, 'expert', split_axis=0, concat_axis=0, tiled=True)  23.6 us
    squeeze x1, local copies, waits for them, and re-layouts, body(): d_tiles[:, 1]  14.1 us
  transfers between devices with their start and end apart: 4, of which 3 were waited for; matrix products, arithmetic and copies ran while one was open for 3% of the time, Pallas kernels for 34%

profile of v3, /device:TPU:0, one launch (start us, length us, event | category | flops | bytes accessed | tf_op | source)
XLA Modules:
  0.0 650.1 jit_solution(5241021488220184201)
XLA Ops:
  7.8 1.7 copy.42.col_ref
  9.5 4.0 slots.1
  13.5 6.5 dispatch_cotangent.1
  20.0 6.5 all-to-all-start
  26.5 0.0 all-reduce.6.cloned.1.call-start
  26.6 0.6 broadcast_in_dim.6.gain_ref
  27.1 0.1 fusion.12
  27.2 0.1 copy.57
  27.3 0.1 copy.56
  27.4 0.1 convolution_bitcast_fusion
  27.6 0.6 reshape.180.w_ref
  28.2 0.6 broadcast_in_dim.7.gain_ref.refs_6_
  28.8 0.8 copy.45.wr_ref
  29.6 0.6 pad_maximum_fusion.far_ref
  30.2 8.0 %project.1 = (bf16[1024,768]{1,0:T(8,128)(2,1)}, bf16[1024,2304]{1,0:T(8,128)(2,1)}) custom-call(bf16[1024,768]{1,0:T(8,128)(2,1)} %x_ref.2, f32[1,768]{1,0:T(1,128)} %broadcast_in_dim.6.gain_ref, bf16[768,768]{1,0:T(8,128)(2,1)} %wq_ref.3, bf16[768,768]{1,0:T(8,128)(2,1)} %wk_ref.3, bf16[768,768]{1,0:T(8,128)(2,1)} %wv_ref.3), custom_call_target="tpu_custom_call" | custom-call | flops 3623878656 | bytes 11403264 | tf_op jit(solution)/shard_map/project/pallas_call | solution.py:752
  38.1 31.6 %attention_forward.1 = (bf16[1024,768]{1,0:T(8,128)(2,1)}, f32[1024,768]{1,0:T(8,128)}, bf16[12,1024,1024]{2,1,0:T(8,128)(2,1)}) custom-call(s32[1]{0:T(128)S(6)} %copy.65.len_ref, f32[2,12]{1,0:T(2,128)} %pad_maximum_fusion.far_ref, bf16[1024,2304]{1,0:T(8,128)(2,1)} %get-tuple-element.67.q_ref.k_ref.v_ref, ...), custom_call_target="tpu_custom_call" | custom-call | flops 12884901888 | bytes 34603008 | tf_op jit(solution)/shard_map/attention_forward/pallas_call | solution.py:619
  69.7 5.7 middle.1
  75.5 0.6 compare_convert_fusion.hot_ref
  76.1 22.0 %all-to-all-done.g_ref = bf16[8,2,128,768]{3,2,1,0:T(8,128)(2,1)} async-done(((bf16[8,2,128,768]{3,2,1,0:T(8,128)(2,1)}), bf16[8,2,128,768]{3,2,1,0:T(8,128)(2,1)}, u32[]{:S(2)}, u32[]{:S(2)}) %all-to-all-start) | async-done | bytes 3145760 | tf_op jit(solution)/shard_map/all_to_all | solution.py:737
  98.1 144.3 %experts.1 = (bf16[2,1024,768]{2,1,0:T(8,128)(2,1)}, bf16[8,128,768]{2,1,0:T(8,128)(2,1)}, bf16[8,128,768]{2,1,0:T(8,128)(2,1)}, bf16[2,2,4,768,768]{4,3,2,1,0:T...) custom-call(s32[2,1024]{1,0:T(2,128)} %get-tuple-element.65.srow_ref, ...), custom_call_target="tpu_custom_call" | custom-call | flops 57982058496 | bytes 69206016 | tf_op jit(solution)/shard_map/experts/pallas_call | solution.py:776
  242.5 14.1 %slice_bitcast_fusion = (bf16[2,4,768,768]{3,2,1,0:T(8,128)(2,1)}, bf16[2,4,768,768]{3,2,1,0:T(8,128)(2,1)}) fusion(bf16[2,2,4,768,768]{4,3,2,1,0:T(8,128)(2,1)} %get-tuple-element.91), kind=kLoop, calls=%fused_computation | loop fusion | bytes 37748736 | tf_op jit(solution)/shard_map/squeeze | solution.py:844
  256.6 0.0 all-reduce.6.cloned.1.call-update
  256.6 1.9 copy-done
  258.5 1.9 fusion.10
  260.4 12.8 %all-to-all-start.1 = ((bf16[8,128,768]{2,1,0:T(8,128)(2,1)}), bf16[8,128,768]{2,1,0:T(8,128)(2,1)S(1)}, u32[]{:S(2)}, u32[]{:S(2)}) async-start(bf16[8,128,768]{2,1,0:T(8,128)(2,1)} %bitcast.4), calls=%async_computation.1 | async-start | bytes 3145728 | tf_op jit(solution)/shard_map/all_to_all | solution.py:737
  273.2 0.0 copy-done.9
  273.2 0.6 dynamic-slice.14
  273.8 13.4 %combine.1 = (f32[1024,768]{1,0:T(8,128)}, bf16[1024,768]{1,0:T(8,128)(2,1)}, bf16[1024,768]{1,0:T(8,128)(2,1)}, f32[1,768]{1,0:T(1,128)}) custom-call(s32[1]{0:T(128)S(6)} %copy.65.len_ref, s32[1024,128]{1,0:T(8,128)} %get-tuple-element.64.scol_ref, bf16[1024,768]{1,0:T(8,128)(2,1)} %bitcast.47, bf16[1024,768]{1,0:T(8,128)(2,1)} %bitcast.48, ...), custom_call_target="tpu_custom_call" | custom-call | flops 4429185024 | bytes 16908288 | tf_op jit(solution)/shard_map/combine/pallas_call | solution.py:790
  287.2 23.8 %all-to-all-done.1 = bf16[8,128,768]{2,1,0:T(8,128)(2,1)S(1)} async-done(((bf16[8,128,768]{2,1,0:T(8,128)(2,1)}), bf16[8,128,768]{2,1,0:T(8,128)(2,1)S(1)}, u32[]{:S(2)}, u32[]{:S(2)}) %all-to-all-start.1) | async-done | bytes 1572896 | tf_op jit(solution)/shard_map/all_to_all | solution.py:737
  311.0 4.3 all-to-all-start.2
  315.3 0.0 copy-start.8
  315.3 35.9 %attention_backward.1 = (bf16[3,1024,768]{2,1,0:T(8,128)(2,1)}, f32[6,2,512]{2,1,0:T(2,128)}, f32[6,2,2,128]{3,2,1,0:T(2,128)}) custom-call(bf16[1024,2304]{1,0:T(8,128)(2,1)} %get-tuple-element.67.q_ref.k_ref.v_ref, bf16[1024,2304]{1,0:T(8,128)(2,1)} %get-tuple-element.67.q_ref.k_ref.v_ref, bf16[1024,2304]{1,0:T(8,128)(2,1)} %get-tuple-element.67.q_ref.k_ref.v_ref, ...), custom_call_target="tpu_custom_call" | custom-call | flops 25769803776 | bytes 34603008 | tf_op jit(solution)/shard_map/attention_backward/pallas_call | solution.py:709
  351.3 0.8 reshape.186
  352.1 0.8 reduce_sum.11
  352.9 0.1 fusion.11
  353.0 0.1 copy.58
  353.1 0.1 copy.47
  353.1 0.1 copy.59
  353.2 0.1 copy.48
  353.3 0.1 fusion.2
  353.5 0.1 slice_add_fusion.1
  353.6 0.1 scatter-add.6
  353.7 0.1 slice_add_fusion
  353.7 0.1 scatter-add.9
  353.8 0.1 copy.49
  353.9 0.1 reshape.189
  354.0 0.0 copy-done.4
  354.0 0.0 copy-done.8
  354.1 0.7 fusion.small_ref
  354.8 11.1 %weight_gradients.1 = bf16[4,768,768]{2,1,0:T(8,128)(2,1)} custom-call(bf16[1024,768]{1,0:T(8,128)(2,1)} %get-tuple-element.82.h_ref, bf16[1024,768]{1,0:T(8,128)(2,1)} %get-tuple-element.68.o_ref, bf16[3,1024,768]{2,1,0:T(8,128)(2,1)} %get-tuple-element.80.d_ref, bf16[1024,768]{1,0:T(8,128)(2,1)} %get-tuple-element.83.gb_ref), custom_call_target="tpu_custom_call" | custom-call | flops 4831838208 | bytes 14155776 | tf_op jit(solution)/shard_map/weight_gradients/pallas_call | solution.py:799
  365.9 108.5 %last.1 = (bf16[1024,768]{1,0:T(8,128)(2,1)}, bf16[3072,768]{1,0:T(8,128)(2,1)}, f32[24,768]{1,0:T(8,128)}) custom-call(bf16[1024,768]{1,0:T(8,128)(2,1)} %x_ref.2, f32[1,768]{1,0:T(1,128)} %broadcast_in_dim.6.gain_ref, bf16[3,1024,768]{2,1,0:T(8,128)(2,1)} %get-tuple-element.80.d_ref, bf16[768,768]{1,0:T(8,128)(2,1)} %wq_ref.3, bf16[768,768]{1,0:T(8,128)(2,1)} %wk_ref.3, ...), custom_call_target="tpu_custom_call" | custom-call | flops 3623878656 | bytes 19267584 | tf_op jit(solution)/shard_map/last/pallas_call | solution.py:814
  474.4 0.7 slice_reduce_fusion.2
  475.2 0.1 reshape_squeeze.11
  475.3 0.0 slice-start
  475.3 0.7 copy.50
  475.9 1.4 slice_reduce_fusion
  477.4 1.4 slice_bitcast_fusion.2
  478.8 0.0 all-to-all-done.2
  478.8 7.7 %mixed.1 = bf16[1024,768]{1,0:T(8,128)(2,1)} custom-call(s32[1]{0:T(128)S(6)} %copy.65.len_ref, s32[1024,128]{1,0:T(8,128)} %get-tuple-element.64.scol_ref, bf16[1024,768]{1,0:T(8,128)(2,1)} %bitcast.43, bf16[1024,768]{1,0:T(8,128)(2,1)} %bitcast.7.refs_1_, f32[1024,768]{1,0:T(8,128)} %get-tuple-element.73.refs_2_), custom_call_target="tpu_custom_call" | custom-call | flops 3221225472 | bytes 7864320 | tf_op jit(solution)/shard_map/mixed/pallas_call | solution.py:825
  486.6 3.8 fusion.9
  490.4 143.6 %all-reduce.6.cloned.1.call-done = (bf16[2,4,768,768]{3,2,1,0:T(8,128)(2,1)}, bf16[2,4,768,768]{3,2,1,0:T(8,128)(2,1)}) async-done(((bf16[2,4,768,768]{3,2,1,0:T(8,128)(2,1)}, bf16[2,4,768,768]{3,2,1,0:T(8,128)(2,1)}), (bf16[2,4,768,768]{3,2,1,0:T(8,128)(2,1)}, bf16[2,4,768,768]{3,2,1,0:T(8,128)(2,1)})) %all-reduce.6.cloned.1.call-update) | async-done | bytes 18874384
  634.0 7.7 %bitcast_convert_fusion = (f32[2,768,768]{2,1,0:T(8,128)}, f32[2,768,768]{2,1,0:T(8,128)}) fusion(bf16[2,4,768,768]{3,2,1,0:T(8,128)(2,1)} %get-tuple-element.131, u32[]{:T(128)} %bitcast.28, bf16[2,4,768,768]{3,2,1,0:T(8,128)(2,1)} %get-tuple-element.130), kind=kLoop, calls=%fused_computation.2 | loop fusion | flops 2359296 | bytes 14155780 | tf_op jit(solution)/shard_map/convert_element_type | solution.py:844
  641.7 0.0 copy-done.2
  641.7 1.1 copy.66
  (22 shorter events, 0.1 us)
Async XLA Ops:
  20.0 6.5 %copy-start.6 = (f32[768]{0:T(1024)S(1)}, f32[768]{0:T(1024)}, u32[]{:S(2)}) copy-start(f32[768]{0:T(1024)} %param.20) | copy-start | bytes 9220
  20.0 7.1 %copy-start.3 = (f32[32,12]{0,1:T(8,128)S(1)}, f32[32,12]{0,1:T(8,128)}, u32[]{:S(2)}) copy-start(f32[32,12]{0,1:T(8,128)} %param.26) | copy-start | bytes 4612
  20.0 8.2 %copy-start.7 = (f32[768]{0:T(1024)S(1)}, f32[768]{0:T(1024)}, u32[]{:S(2)}) copy-start(f32[768]{0:T(1024)} %param.21) | copy-start | bytes 9220
  20.0 8.8 %copy-start.5 = (bf16[768,16]{0,1:T(8,128)(2,1)S(1)}, bf16[768,16]{0,1:T(8,128)(2,1)}, u32[]{:S(2)}) copy-start(bf16[768,16]{0,1:T(8,128)(2,1)} %param.27) | copy-start | bytes 73732
  20.0 78.1 %all-to-all-start = ((bf16[8,2,128,768]{3,2,1,0:T(8,128)(2,1)}), bf16[8,2,128,768]{3,2,1,0:T(8,128)(2,1)}, u32[]{:S(2)}, u32[]{:S(2)}) async-start(bf16[8,2,128,768]{3,2,1,0:T(8,128)(2,1)} %dispatch_cotangent.1), calls=%async_computation | async-start | bytes 6291456 | tf_op jit(solution)/shard_map/all_to_all | solution.py:737
  26.5 607.5 %all-reduce.6.cloned.1.call-start = ((), (), s32[]{:S(2)}) async-start(), calls=%async_computation.3 | async-start | bytes 37748736
  256.6 1.9 copy-start
  260.4 12.8 %copy-start.9 = (u32[32]{0:T(128)S(1)}, u32[32]{0:T(128)}, u32[]{:S(2)}) copy-start(u32[32]{0:T(128)} %constant.103) | copy-start | bytes 388
  260.4 50.7 %all-to-all-start.1 = ((bf16[8,128,768]{2,1,0:T(8,128)(2,1)}), bf16[8,128,768]{2,1,0:T(8,128)(2,1)S(1)}, u32[]{:S(2)}, u32[]{:S(2)}) async-start(bf16[8,128,768]{2,1,0:T(8,128)(2,1)} %bitcast.4), calls=%async_computation.1 | async-start | bytes 3145728 | tf_op jit(solution)/shard_map/all_to_all | solution.py:737
  311.0 40.3 %copy-start.1 = (bf16[8,128,768]{2,1,0:T(8,128)(2,1)}, bf16[8,128,768]{2,1,0:T(8,128)(2,1)S(1)}, u32[]{:S(2)}) copy-start(bf16[8,128,768]{2,1,0:T(8,128)(2,1)S(1)} %all-to-all-done.1) | copy-start | bytes 4718596
  311.0 167.8 %all-to-all-start.2 = ((bf16[8,128,768]{2,1,0:T(8,128)(2,1)}), bf16[8,128,768]{2,1,0:T(8,128)(2,1)}, u32[]{:S(2)}, u32[]{:S(2)}) async-start(bf16[8,128,768]{2,1,0:T(8,128)(2,1)} %bitcast.6), calls=%async_computation.2 | async-start | bytes 3145728 | tf_op jit(solution)/shard_map/all_to_all | solution.py:737
  315.3 38.7 %copy-start.4 = (f32[16,768]{1,0:T(8,128)S(1)}, f32[16,768]{1,0:T(8,128)}, u32[]{:S(2)}) copy-start(f32[16,768]{1,0:T(8,128)} %get-tuple-element.87) | copy-start | bytes 147460
  315.3 38.7 %copy-start.8 = (f32[1,768]{1,0:T(1,128)S(1)}, f32[1,768]{1,0:T(1,128)}, u32[]{:S(2)}) copy-start(f32[1,768]{1,0:T(1,128)} %get-tuple-element.84) | copy-start | bytes 9220
  475.3 11.3 %slice-start = ((s8[4718592]{0:T(1024)(128)(4,1)}), s8[524288]{0:T(1024)(128)(4,1)S(1)}, s32[]{:S(2)}) async-start(s8[4718592]{0:T(1024)(128)(4,1)} %bitcast.40), calls=%async_computation.4 | async-start | bytes 1048576
  478.8 7.7 %slice-start.1 = ((s8[4718592]{0:T(1024)(128)(4,1)}), s8[4194304]{0:T(1024)(128)(4,1)S(1)}, s32[]{:S(2)}) async-start(s8[4718592]{0:T(1024)(128)(4,1)} %bitcast.40), calls=%async_computation.5 | async-start | bytes 8388608
  634.0 7.7 %copy-start.2 = (bf16[1024,768]{1,0:T(8,128)(2,1)S(1)}, bf16[1024,768]{1,0:T(8,128)(2,1)}, u32[]{:S(2)}) copy-start(bf16[1024,768]{1,0:T(8,128)(2,1)} %get-tuple-element.159) | copy-start | bytes 4718596
Sparse Core Ops, SparseCore 0:
  256.7 377.1 all-reduce.5

commit v4 on v3

--- a/solution.py
+++ b/solution.py
@@ -112,11 +112,11 @@
     return lax.rsqrt(jnp.mean(v * v, axis=1, keepdims=True) + EPSILON)
 
 
-def project_kernel(x_ref, gain_ref, wq_ref, wk_ref, wv_ref, h_ref, qkv_ref):
+def project_kernel(x_ref, gain_ref, wq_ref, wk_ref, wv_ref, ht_ref, qkv_ref):
     D = x_ref.shape[1]
     x = x_ref[...].astype(F32)
     h = (x * rms_scale(x) * gain_ref[...]).astype(BF)
-    h_ref[...] = h
+    ht_ref[...] = h.T
     for n, w_ref in enumerate((wq_ref, wk_ref, wv_ref)):
         qkv_ref[:, n * D:(n + 1) * D] = dot(h, w_ref[...]).astype(BF)
 
@@ -343,50 +343,10 @@
     return (iota((scol.shape[0], slots), 1) == scol[:, e:e + 1]).astype(F32).astype(BF)
 
 
-def combine_kernel(local, len_ref, scol_ref, *refs):
-    backs = refs[:local]
-    middle_ref, cot_ref, inv_ref, wo_ref, gain_ref, gm_ref, gb_ref, do_ref, gain_out = refs[local:]
-    r = pl.program_id(0)
-    scol = scol_ref[...]
-    gh = sum(dot(combine_hot(scol, b.shape[0], e), b[...]) for e, b in enumerate(backs))
-    live = iota((RB, 1), 0) + r * RB < len_ref[0]
-    up = jnp.where(live, gh, 0.0)
-    gv, gg = norm_back(middle_ref[...], gain_ref[...], up)
-    gm = jnp.where(live, cot_ref[...].astype(F32), 0.0) + gv
-    gm_ref[...] = gm
-    gb = gm.astype(BF)
-    gb_ref[...] = gb
-    do_ref[...] = (dot_nt(gb, wo_ref[...]) * inv_ref[...]).astype(BF)
-    gs = jnp.sum(gg, axis=0, keepdims=True)
-
-    @pl.when(r == 0)
-    def _():
-        gain_out[...] = gs
-
-    @pl.when(r > 0)
-    def _():
-        gain_out[...] += gs
-
-
-def weights_kernel(h_ref, o_ref, d_ref, gb_ref, out_ref, ht_s):
-    n = pl.program_id(0)
-
-    @pl.when(n == 0)
-    def _():
-        ht_s[...] = h_ref[...].T
-
-    @pl.when(n < 3)
-    def _():
-        out_ref[0] = dot(ht_s[...], d_ref[0]).astype(BF)
-
-    @pl.when(n == 3)
-    def _():
-        out_ref[0] = dot_tn(o_ref[...], gb_ref[...]).astype(BF)
-
-
 def bit_orders():
     def bits(axis):
         return [(axis, 1 << n) for n in range(lax.axis_size(axis).bit_length() - 1)]
+
     dp, ex = bits("dp"), bits("expert")
     return [ex[:1] + dp + ex[1:], ex[:1] + dp[::-1] + ex[1:]]
 
@@ -398,7 +358,7 @@
 
 
 def add_rows(acc, start, recv, offset, rows):
-    step = 48
+    step = next(n for n in (256, 192, 144, 128, 112, 96, 64, 48, 32, 16) if rows % n == 0)
 
     def one(i, _):
         to = pl.ds(pl.multiple_of(start + i * step, 16), step)
@@ -408,22 +368,24 @@
     lax.fori_loop(0, rows // step, one, 0)
 
 
-def halving_stages(order, base, rows, acc, recv, landing, out, send_sem, recv_sem, sem0):
-    stages = []
-    start, n, offset, sem = base, rows, landing, sem0
-    kept = []
-
-    def transfer(src, dst, who, sem):
-        return pltpu.make_async_remote_copy(src_ref=src, dst_ref=dst, send_sem=send_sem.at[sem], recv_sem=recv_sem.at[sem],
-                                            device_id=who, device_id_type=pl.DeviceIdType.MESH)
-
+def landing_rows(rows, count):
+    total = 0
+    for _ in range(count):
+        rows = rows // 2 if rows % 32 == 0 else rows
+        total += rows
+    return total
+
+
+def halving_stages(order, base, rows, acc, recv, landing, out, send_sem, recv_sem, own_sem, sem):
+    stages, kept = [], []
+    start, n, offset = base, rows, landing
     for axis, mask in order:
         bit, who = neighbour(axis, mask)
-        halve = n % 96 == 0
+        halve = n % 32 == 0
         m = n // 2 if halve else n
         keep = start + bit * m if halve else start
         give = start + (1 - bit) * m if halve else start
-        copy = transfer(acc.at[pl.ds(pl.multiple_of(give, 16), m)], recv.at[pl.ds(offset, m)], who, sem)
+        copy = remote(acc.at[pl.ds(pl.multiple_of(give, 16), m)], recv.at[pl.ds(offset, m)], send_sem.at[sem], recv_sem.at[sem], who)
 
         def finish(copy=copy, keep=keep, offset=offset, m=m):
             copy.wait()
@@ -435,29 +397,21 @@
         start, n = keep, m
         offset += m
         sem += 1
-    first = True
+    own = pltpu.make_async_copy(acc.at[pl.ds(pl.multiple_of(start, 16), n)], out.at[pl.ds(pl.multiple_of(start, 16), n)], own_sem)
+    stages.append((own.start, own.wait))
     for axis, mask, at, m in kept[::-1]:
         bit, who = neighbour(axis, mask)
         here = pl.ds(pl.multiple_of(at, 16), m)
-        copy = transfer(out.at[here], out.at[here], who, sem)
-
-        def begin(copy=copy, here=here, first=first):
-            if first:
-                out[here, :] = acc[here, :]
-            copy.start()
-
-        stages.append((begin, copy.wait))
-        first = False
+        copy = remote(out.at[here], out.at[here], send_sem.at[sem], recv_sem.at[sem], who)
+        stages.append((copy.start, copy.wait))
         sem += 1
     return stages
 
 
-def exchange_stages(order, acc, recv, send_sem, recv_sem, sem0):
+def whole_stages(order, acc, recv, send_sem, recv_sem, sem):
     stages = []
     for n, (axis, mask) in enumerate(order):
-        bit, who = neighbour(axis, mask)
-        copy = pltpu.make_async_remote_copy(src_ref=acc.at[n], dst_ref=recv.at[n], send_sem=send_sem.at[sem0 + n],
-                                            recv_sem=recv_sem.at[sem0 + n], device_id=who, device_id_type=pl.DeviceIdType.MESH)
+        copy = remote(acc.at[n], recv.at[n], send_sem.at[sem + n], recv_sem.at[sem + n], neighbour(axis, mask)[1])
 
         def finish(copy=copy, n=n):
             copy.wait()
@@ -467,83 +421,213 @@
     return stages
 
 
-def last_kernel(x_ref, gain_ref, d_ref, wq_ref, wk_ref, wv_ref, gm_ref, dw_ref, small_ref,
-                token_ref, sums_ref, small_out, acc, recv, out, sacc, srecv, gain_s, send_sem, recv_sem, local_sem):
-    r = pl.program_id(0)
-    steps = pl.num_programs(0)
+class Chain:
+    def __init__(self, *lists):
+        self.lists, self.at = lists, 0
+        self.count = max(len(stages) for stages in lists)
+
+    def advance(self):
+        for stages in self.lists:
+            if 0 < self.at <= len(stages):
+                stages[self.at - 1][1]()
+            if self.at < len(stages):
+                stages[self.at][0]()
+        self.at += 1
+
+    def done(self):
+        return self.at > self.count
+
+
+SMALL = 24
+PAIRS_OF = ((0, 3), (3, 5), (5, 6))
+
+
+def backward_kernel(len_ref, scol_ref, back0_ref, back1_ref, middle_ref, cot_ref, inv_ref, wo_ref, gain2_ref,
+                    q_ref, k_ref, v_ref, o_ref, p_ref, ht_ref, wq_ref, wk_ref, wv_ref, x_ref, gain1_ref, dr_ref,
+                    rows_ref, d_ref, part_ref,
+                    token_ref, sums_ref, small_ref, e0_ref, e1_ref, last_ref, more_ref,
+                    do_s, gb_s, gm_s, gh_s, acc_s, recv_s, sacc_s, srecv_s, fwd_s, tmp_s,
+                    send_sem, recv_sem, e_send, e_recv, e_own, r_send, r_recv, load_sem, out_sem):
+    s = pl.program_id(0)
+    me_dp = lax.axis_index("dp")
+    by_x, by_y, by_xy = dp_partners(me_dp)
+    pairs = do_s.shape[0]
+    L, D = gh_s.shape
+    combine_steps = L // RB
+    first_pair, first_token = combine_steps, combine_steps + pairs
+    last = first_token + combine_steps - 1
+    peers, most, _ = e0_ref.shape
     orders = bit_orders()
-    total = acc.shape[0]
-    half = total // 2
-    parts = [halving_stages(order, n * half, half, acc, recv, n * (recv.shape[0] // 2), out, send_sem, recv_sem, 2 * len(order) * n) for n, order in enumerate(orders)]
-    smalls = exchange_stages(orders[0], sacc, srecv, send_sem, recv_sem, 4 * len(orders[0]))
-    n_rs = len(orders[0])
-
-    @pl.when(r == 0)
-    def _():
-        barrier = pltpu.get_barrier_semaphore()
-        for axis, mask in orders[0]:
-            pl.semaphore_signal(barrier, inc=1, device_id=neighbour(axis, mask)[1], device_id_type=pl.DeviceIdType.MESH)
-        load = pltpu.make_async_copy(dw_ref, acc, local_sem)
-        load.start()
-        load.wait()
-        pl.semaphore_wait(barrier, len(orders[0]))
-        for part in parts:
-            part[0][0]()
-
-    for s in range(1, n_rs):
-        @pl.when(r == s)
-        def _(s=s):
-            for part in parts:
-                part[s - 1][1]()
-                part[s][0]()
-
-    gh = dot_nt(d_ref[0], wq_ref[...]) + dot_nt(d_ref[1], wk_ref[...]) + dot_nt(d_ref[2], wv_ref[...])
-    gv, gg = norm_back(x_ref[...].astype(F32), gain_ref[...], gh)
-    token_ref[...] = (gm_ref[...] + gv).astype(BF)
-    gs = jnp.sum(gg, axis=0, keepdims=True)
-
-    @pl.when(r == 0)
-    def _():
-        gain_s[0:1] = gs
-
-    @pl.when(r > 0)
-    def _():
-        gain_s[0:1] += gs
-
-    @pl.when(r == steps - 1)
-    def _():
-        sacc[0] = small_ref[...]
-        sacc[0, 0:1] = gain_s[0:1]
-        smalls[0][0]()
-        done = 0
-        for s in range(n_rs, max(len(part) for part in parts) + 1):
-            for part in parts:
-                if s <= len(part):
-                    part[s - 1][1]()
-                if s < len(part):
-                    part[s][0]()
-            if done < len(smalls):
-                smalls[done][1]()
-                done += 1
-                if done < len(smalls):
-                    smalls[done][0]()
-        while done < len(smalls):
-            smalls[done][1]()
-            done += 1
-            if done < len(smalls):
-                smalls[done][0]()
-        sums_ref[...] = out[...]
-        small_out[...] = sacc[len(smalls)]
-
-
-def mixed_kernel(local, len_ref, scol_ref, *refs):
-    rows = refs[:local]
-    middle_ref, out_ref = refs[local:]
-    r = pl.program_id(0)
+    count = len(orders[0])
+
+    tile_rows = 4 * D
+    chains = []
+    landing, sem = 0, 0
+    for low, high in PAIRS_OF:
+        half = (high - low) * tile_rows // 2
+        lists = []
+        for n, order in enumerate(orders):
+            stages = halving_stages(order, low * tile_rows + n * half, half, acc_s, recv_s, landing, sums_ref, send_sem, recv_sem, out_sem.at[len(chains), n], sem)
+            landing += landing_rows(half, count)
+            sem += len(stages)
+            lists.append(stages)
+        chains.append(Chain(*lists))
+    small_chain = Chain(whole_stages(orders[0], sacc_s, srecv_s, send_sem, recv_sem, sem))
+
+    def block(which):
+        return lambda j: rows_ref.at[which, pl.ds(pl.multiple_of(j * most, 16), most)]
+
+    homes = [Exchange(block(n), lambda j, ref=ref: ref.at[j], e_send.at[n], e_recv.at[n], e_own.at[n]) for n, ref in enumerate((e0_ref, e1_ref))]
+
+    rest = [remote(d_ref.at[1, m, (by_x, by_y)[m]], last_ref.at[m], r_send.at[m], r_recv.at[m], {"dp": (by_x, by_y)[m]}) for m in range(2)]
+    second = [[remote(fwd_s.at[n, m], more_ref.at[n, m], r_send.at[2 + 2 * n + m], r_recv.at[2 + 2 * n + m], {"dp": (by_y, by_x)[m]}) for m in range(2)] for n in range(2)]
+
+    def loads(n, m):
+        return [pltpu.make_async_copy(d_ref.at[n, m, (by_y, by_x)[m]], tmp_s.at[0], load_sem.at[0]),
+                pltpu.make_async_copy(part_ref.at[n, m, 0], tmp_s.at[1], load_sem.at[1])]
+
+    @pl.when(s == 0)
+    def _():
+        greet([{"dp": by_x}, {"dp": by_y}])
+        for c in rest:
+            c.start()
+        for home in homes:
+            home.start()
+        for c in loads(0, 0):
+            c.start()
+
+    for t in range(4):
+        @pl.when(s == t + 1)
+        def _(t=t):
+            n, m = t // 2, t % 2
+            for c in loads(n, m):
+                c.wait()
+            fwd_s[n, m] = (tmp_s[0].astype(F32) + tmp_s[1].astype(F32)).astype(BF)
+            second[n][m].start()
+            if t < 3:
+                for c in loads((t + 1) // 2, (t + 1) % 2):
+                    c.start()
+
+    @pl.when(s < combine_steps)
+    def _():
+        here = pl.ds(pl.multiple_of(s * RB, RB), RB)
+        scol = scol_ref[...]
+        gh = dot(combine_hot(scol, back0_ref.shape[0], 0), back0_ref[...]) + dot(combine_hot(scol, back1_ref.shape[0], 1), back1_ref[...])
+        live = iota((RB, 1), 0) + s * RB < len_ref[0]
+        gv, gg = norm_back(middle_ref[...], gain2_ref[...], jnp.where(live, gh, 0.0))
+        gm = jnp.where(live, cot_ref[...].astype(F32), 0.0) + gv
+        gm_s[here, :] = gm
+        gb = gm.astype(BF)
+        gb_s[here, :] = gb
+        do = (dot_nt(gb, wo_ref[...]) * inv_ref[...]).astype(BF)
+        for p in range(pairs):
+            do_s[p, here, :] = do[:, p * 128:(p + 1) * 128]
+        gs = jnp.sum(gg, axis=0, keepdims=True)
+
+        @pl.when(s == 0)
+        def _():
+            sacc_s[0] = jnp.zeros_like(small_ref)
+            sacc_s[0, 1:2, :] = gs
+            gh_s[...] = jnp.zeros_like(gh_s)
+
+        @pl.when(s > 0)
+        def _():
+            sacc_s[0, 1:2, :] += gs
+
+    @pl.when((s >= first_pair) & (s < first_token))
+    def _():
+        pair = s - first_pair
+
+        def middle_event():
+            for low, chain in enumerate(chains):
+                for t in range(PAIRS_OF[low][1], pairs):
+                    @pl.when(pair == t)
+                    def _(chain=chain):
+                        chain.advance()
+
+        dq, dk, dv = attention_back(
+            q_ref[...], k_ref[...], v_ref[...], do_s[pair], o_ref[...], p_ref,
+            sacc_s, 2 * pair)
+        d3 = jnp.concatenate([dq, dk, dv], axis=1)
+        w3 = jnp.concatenate([wq_ref[...], wk_ref[...], wv_ref[...]], axis=1)
+        gh_s[...] += dot_nt(d3, w3)
+        dw = dot(ht_ref[...], d3).astype(BF)
+        base = pair * tile_rows
+        for n in range(3):
+            acc_s[pl.ds(pl.multiple_of(base + n * D, 128), D), :] = dw[:, n * 128:(n + 1) * 128]
+        dwo = dot_tn(o_ref[...], gb_s[...]).astype(BF)
+        for n in range(pairs):
+            acc_s[pl.ds(pl.multiple_of(base + 3 * D + n * 128, 128), 128), :] = dwo[:, n * 128:(n + 1) * 128]
+
+    for t in range(pairs):
+        ready = [chain for (low, high), chain in zip(PAIRS_OF, chains) if high <= t + 1]
+        if ready:
+            @pl.when(s == first_pair + t)
+            def _(ready=ready):
+                for chain in ready:
+                    chain.advance()
+
+    @pl.when(s >= first_token)
+    def _():
+        here = pl.ds(pl.multiple_of((s - first_token) * RB, RB), RB)
+        gv, gg = norm_back(x_ref[...].astype(F32), gain1_ref[...], gh_s[here, :])
+        token_ref[...] = (gm_s[here, :] + gv).astype(BF)
+        gs = jnp.sum(gg, axis=0, keepdims=True)
+        sacc_s[0, 0:1, :] += gs
+
+    for t in range(first_token, last):
+        @pl.when(s == t)
+        def _():
+            for chain in chains:
+                if not chain.done():
+                    chain.advance()
+
+    @pl.when(s == last)
+    def _():
+        sacc_s[0, SMALL:, :] = dr_ref[...]
+        live = [*chains, small_chain]
+        while live:
+            for chain in live:
+                chain.advance()
+            live = [chain for chain in live if not chain.done()]
+        small_ref[...] = sacc_s[count]
+        for c in rest + second[0] + second[1]:
+            c.wait()
+        for home in homes:
+            home.wait()
+
+
+def finish_kernel(place_ref, len_ref, scol_ref, rows0_ref, rows1_ref, middle_ref, sums_ref, small_ref, hot_ref, own_ref, part_ref, rest_ref, more_ref,
+                  mixed_ref, dq_ref, dk_ref, dv_ref, do_ref, gains_ref, table_ref, router_ref, first_ref, second_ref):
+    s = pl.program_id(0)
+    T = mixed_ref.shape[0]
     scol = scol_ref[...]
-    got = sum(dot(combine_hot(scol, b.shape[0], e), b[...]) for e, b in enumerate(rows))
-    live = iota((RB, 1), 0) + r * RB < len_ref[0]
-    out_ref[...] = jnp.where(live, middle_ref[...] + got, 0.0).astype(BF)
+    got = dot(combine_hot(scol, rows0_ref.shape[0], 0), rows0_ref[...]) + dot(combine_hot(scol, rows1_ref.shape[0], 1), rows1_ref[...])
+    live = iota((T, 1), 0) + s * T < len_ref[0]
+    mixed_ref[...] = jnp.where(live, middle_ref[...] + got, 0.0).astype(BF)
+    D = dq_ref.shape[0]
+    pairs = D // 128
+    for n, ref in enumerate((dq_ref, dk_ref, dv_ref)):
+        ref[...] = sums_ref[0, n * D:(n + 1) * D, :].astype(F32)
+    for n in range(pairs):
+        do_ref[:, n * 128:(n + 1) * 128] = sums_ref[0, 3 * D + n * 128:3 * D + (n + 1) * 128, :].astype(F32)
+    for m, ref in enumerate((first_ref, second_ref)):
+        ref[0] = own_ref[0, m, 0].astype(F32) + part_ref[0, m, 0].astype(F32) + more_ref[0, m].astype(F32)
+        ref[1] = own_ref[1, m, 0].astype(F32) + rest_ref[m].astype(F32) + more_ref[1, m].astype(F32)
+
+    @pl.when(s == 0)
+    def _():
+        gains_ref[...] = small_ref[0:8, :]
+        heads = table_ref.shape[1]
+        per_head = small_ref[8:SMALL, :]
+        table = lax.dot_general(hot_ref[...], per_head[:, :WIDE], (((1,), (1,)), ((), ())), precision=HIGHEST, preferred_element_type=F32)
+        buckets = table.shape[0]
+        left = jnp.sum(per_head[:, WIDE:WIDE + 128].T, axis=0, keepdims=True)
+        right = jnp.sum(per_head[:, WIDE + 128:].T, axis=0, keepdims=True)
+        bucket = iota(table.shape, 0)
+        table = table + jnp.where(bucket == buckets // 2 - 1, left, 0.0) + jnp.where(bucket == buckets - 1, right, 0.0)
+        table_ref[...] = table[:, :heads]
+        router_ref[...] = small_ref[SMALL:, :].T
 
 
 def near_bias(w_row):
@@ -628,17 +712,13 @@
     )(lengths, far, qkv, qkv, qkv, w)
 
 
-def attn_bwd_kernel(q_ref, k_ref, v_ref, do_ref, o_ref, p_ref, d_ref, near_ref, blk_ref):
-    L = q_ref.shape[0]
+def attention_back(q, k, v, do, o, p_ref, sums, sums_row):
+    L = q.shape[0]
     nb = L // SUB
-    q = q_ref[...]
-    k = k_ref[...]
-    v = v_ref[...]
-    do = do_ref[...]
     lane = iota((L, 128), 1)
     row = iota((L, 128), 0)
     blk = row // SUB
-    prod = do.astype(F32) * o_ref[...].astype(F32)
+    prod = do.astype(F32) * o.astype(F32)
     zero = jnp.zeros_like(q)
     dk = dv = None
     dqs = []
@@ -684,38 +764,19 @@
         far = pltpu.roll(dq, 64, 1) if a == 0 else dq
         left = jnp.sum(jnp.where((lane < 8) & (lane <= blk - 2), far, 0.0), axis=0, keepdims=True)
         right = jnp.sum(jnp.where((lane < 8) & (lane >= blk + 2), far, 0.0), axis=0, keepdims=True)
-        blk_ref[0, a, 0:1, :] = left
-        blk_ref[0, a, 1:2, :] = right
         full = jnp.concatenate([near, jnp.zeros((SUB, 128), F32)], axis=1)
         rows = SUB
         while rows > 8:
             rows //= 2
             full = full[:rows] + pltpu.roll(full[rows:], 512 - rows, 1)
-        line = iota((8, 512), 0)
+        place = iota((8, 512), 0)
         for step in (4, 2, 1):
-            full = jnp.where((line & step) > 0, pltpu.roll(full, 512 - step, 1), full)
+            full = jnp.where((place & step) > 0, pltpu.roll(full, 512 - step, 1), full)
         diag = jnp.sum(full, axis=0, keepdims=True)
-        near_ref[0, a:a + 1, :] = diag
-    d_ref[0] = jnp.where(lane < 64, dqs[0], dqs[1]).astype(BF)
-    d_ref[1] = dk.astype(BF)
-    d_ref[2] = dv.astype(BF)
-
-
-def attn_bwd(qkv, do, o, p):
-    L = qkv.shape[0]
-    D = qkv.shape[1] // 3
-    pairs = D // 128
-    blk = lambda off: pl.BlockSpec((L, 128), lambda i, off=off: (0, off + i))
-    return pl.pallas_call(
-        attn_bwd_kernel,
-        grid=(pairs,),
-        in_specs=[blk(0), blk(pairs), blk(2 * pairs), blk(0), blk(0), pl.BlockSpec((2, L, L), lambda i: (i, 0, 0))],
-        out_specs=[pl.BlockSpec((3, L, 128), lambda i: (0, 0, i)), pl.BlockSpec((1, 2, 512), lambda i: (i, 0, 0)), pl.BlockSpec((1, 2, 2, 128), lambda i: (i, 0, 0, 0))],
-        out_shape=[jax.ShapeDtypeStruct((3, L, D), BF), jax.ShapeDtypeStruct((pairs, 2, 512), F32), jax.ShapeDtypeStruct((pairs, 2, 2, 128), F32)],
-        compiler_params=pltpu.CompilerParams(vmem_limit_bytes=BIG),
-        cost_estimate=pl.CostEstimate(flops=8 * 2 * pairs * L * L * 256, bytes_accessed=2 * pairs * L * L * 2 + 12 * L * D, transcendentals=0),
-        name="attention_backward",
-    )(qkv, qkv, qkv, do, o, p)
+        line = jnp.concatenate([diag, left, right], axis=1)
+        kept = sums[0, 8:SMALL, :]
+        sums[0, 8:SMALL, :] = jnp.where(iota(kept.shape, 0) == sums_row + a, line, kept)
+    return jnp.where(lane < 64, dqs[0], dqs[1]).astype(BF), dk.astype(BF), dv.astype(BF)
 
 
 def body(tokens, cotangent, gain_one, gain_two, query_weight, key_weight, value_weight, out_weight, bias_table,
@@ -749,10 +810,10 @@
     g_sent, tokens = lax.optimization_barrier((g_sent, tokens))
     g_got = exchange(g_sent)
 
-    h_one, qkv = call(
+    h_one_t, qkv = call(
         project_kernel, "project", (steps,),
-        [rows_of(D), whole(1, D), whole(D, D), whole(D, D), whole(D, D)], [rows_of(D), rows_of(3 * D)],
-        [struct((L, D), BF), struct((L, 3 * D), BF)], flops=6 * L * D * D, moved=6 * D * D + 10 * L * D,
+        [rows_of(D), whole(1, D), whole(D, D), whole(D, D), whole(D, D)], [pl.BlockSpec((D, RB), lambda i: (0, i)), rows_of(3 * D)],
+        [struct((D, L), BF), struct((L, 3 * D), BF)], flops=6 * L * D * D, moved=6 * D * D + 10 * L * D,
     )(tokens, gain_1, query_weight, key_weight, value_weight)
 
     places = jnp.arange(WIDE, dtype=I32)
@@ -784,65 +845,81 @@
          dma((2, peers)), dma((2, peers)), dma((2,)), dma((2, peers)), dma((2, peers)), dma((2,)), dma((2, 2)), dma((6,)), dma((6,))],
         flops=24 * S * D * FF, moved=24 * D * FF + 16 * S * D, transcendentals=2 * S * FF, vmem=62 * 2**20, collective_id=2, has_side_effects=True,
     )(srow, hot, h_two, g_got, expert_in, expert_out, router_weight)
-    backs = [b.reshape(S, D) for b in backs]
-    rows_got = [exchange(rows_sent[e].reshape(peers, most, D)).reshape(S, D) for e in range(local)]
-
-    gm, gb, do, d_gain_2 = call(
-        functools.partial(combine_kernel, local), "combine", (steps,),
-        [SMEM, rows_of(128)] + [whole(S, D)] * local + [rows_of(D)] * 3 + [whole(D, D), whole(1, D)],
-        [rows_of(D), rows_of(D), rows_of(D), whole(1, D)],
-        [struct((L, D), F32), struct((L, D), BF), struct((L, D), BF), struct((1, D), F32)],
-        flops=2 * local * S * L * D + 2 * L * D * D, moved=2 * D * D + 20 * L * D,
-    )(lengths, scol, *backs, middle, cotangent, inv, out_weight, gain_2)
-    d_heads, near_sums, far_sums = attn_bwd(qkv, do, o, p)
-    d_heads, rows_got[0] = lax.optimization_barrier((d_heads, rows_got[0]))
-    d_weights = call(
-        weights_kernel, "weight_gradients", (4,),
-        [whole(L, D), whole(L, D), pl.BlockSpec((1, L, D), lambda n: (jnp.minimum(n, 2), 0, 0)), whole(L, D)],
-        pl.BlockSpec((1, D, D), lambda n: (n, 0, 0)), struct((4, D, D), BF), [pltpu.VMEM((D, L), BF)],
-        flops=8 * L * D * D, moved=8 * D * D + 12 * L * D,
-    )(h_one, o, d_heads, gb)
-    d_table = jnp.dot(near_sums.reshape(heads, WIDE), hot_near.T, precision=HIGHEST).T
-    far_sums = jnp.sum(far_sums.reshape(heads, 2, 128), axis=2)
-    d_table = d_table.at[edge - 1].add(far_sums[:, 0]).at[buckets - 1].add(far_sums[:, 1])
-    d_table = jnp.pad(d_table.reshape(1, buckets * heads), ((0, 5), (0, D - buckets * heads)))
-    small = jnp.concatenate([jnp.zeros((1, D), F32), d_gain_2, d_table, d_router], axis=0)
-    T = L // 8
+    pairs = heads // 2
+    combine_steps = L // RB
+    first_token = combine_steps + pairs
     orders = (n_dp * peers).bit_length() - 1
-    part = pl.BlockSpec((T, D), lambda r: (r, 0))
-    sems = 5 * orders
-    grad_tokens, sums, small = call(
-        last_kernel, "last", (L // T,),
-        [part, whole(1, D), pl.BlockSpec((3, T, D), lambda r: (0, r, 0))] + [whole(D, D)] * 3
-        + [part, pl.BlockSpec(memory_space=pl.ANY), whole(*small.shape)],
-        [part, whole(4 * D, D), whole(*small.shape)],
-        [struct((L, D), BF), struct((4 * D, D), BF), struct(small.shape, F32)],
-        [pltpu.VMEM((4 * D, D), BF), pltpu.VMEM((4 * D + 96 * orders, D), BF), pltpu.VMEM((4 * D, D), BF)]
-        + [pltpu.VMEM((orders + 1, *small.shape), F32), pltpu.VMEM((orders, *small.shape), F32), pltpu.VMEM((8, D), F32),
-           pltpu.SemaphoreType.DMA((sems,)), pltpu.SemaphoreType.DMA((sems,)), pltpu.SemaphoreType.DMA],
-        flops=6 * L * D * D, moved=6 * D * D + 20 * L * D, collective_id=1, has_side_effects=True,
-    )(tokens, gain_1, d_heads, query_weight, key_weight, value_weight, gm, d_weights.reshape(4 * D, D), small)
-    mixed = call(
-        functools.partial(mixed_kernel, local), "mixed", (steps,),
-        [SMEM, rows_of(128)] + [whole(S, D)] * local + [rows_of(D)], rows_of(D), struct((L, D), BF),
-        flops=2 * local * S * L * D, moved=10 * S * D,
-    )(lengths, scol, *rows_got, middle)
-
-    sums = sums.astype(F32)
-    return (
-        mixed,
-        grad_tokens,
-        small[0],
-        small[1],
-        sums[:D],
-        sums[D:2 * D],
-        sums[2 * D:3 * D],
-        sums[3 * D:],
-        small[2, :buckets * heads].reshape(buckets, heads),
-        small[8:].T,
-        lax.psum_scatter(d_tiles[:, 0], 'dp', scatter_dimension=1, tiled=True)[:, 0].astype(F32),
-        lax.psum_scatter(d_tiles[:, 1], 'dp', scatter_dimension=1, tiled=True)[:, 0].astype(F32),
-    )
+    halves = [(high - low) * 2 * D for low, high in PAIRS_OF for _ in range(2)]
+    landing = sum(landing_rows(rows, orders) for rows in halves)
+    sems = 6 * (2 * orders + 1) + orders
+    tiles = pairs * 4 * D
+    small_rows = SMALL + experts
+
+    def once(*shape):
+        return pl.BlockSpec(shape, lambda *i: (0,) * len(shape), pipeline_mode=pl.Buffered(1))
+
+    def early(width):
+        return pl.BlockSpec((RB, width), lambda s: (jnp.minimum(s, combine_steps - 1), 0))
+
+    def late(width):
+        return pl.BlockSpec((RB, width), lambda s: (jnp.maximum(s - first_token, 0), 0))
+
+    def pair_of(s):
+        return jnp.clip(s - combine_steps, 0, pairs - 1)
+
+    def pair(first=0):
+        return pl.BlockSpec((L, 128), lambda s: (0, first + pair_of(s)))
+
+    def pair_weight():
+        return pl.BlockSpec((D, 128), lambda s: (0, pair_of(s)))
+
+    grad_tokens, sums, small, *rows_got, rest, more = call(
+        backward_kernel, "backward", (first_token + combine_steps,),
+        [SMEM, early(128), once(S, D), once(S, D), early(D), early(D), early(D), once(D, D), once(1, D),
+         pair(0), pair(pairs), pair(2 * pairs), pair(0), pl.BlockSpec((2, L, L), lambda s: (pair_of(s), 0, 0)), once(D, L)]
+        + [pair_weight()] * 3 + [late(D), once(1, D), once(experts, D), anywhere, anywhere, anywhere],
+        [late(D), anywhere, whole(small_rows, D), anywhere, anywhere, anywhere, anywhere],
+        [struct((L, D), BF), struct((tiles, 128), BF), struct((small_rows, D), F32), struct((peers, most, D), BF), struct((peers, most, D), BF),
+         struct((2, D, D), BF), struct((2, 2, D, D), BF)],
+        [pltpu.VMEM((pairs, L, 128), BF), pltpu.VMEM((L, D), BF), pltpu.VMEM((L, D), F32), pltpu.VMEM((L, D), F32),
+         pltpu.VMEM((tiles, 128), BF), pltpu.VMEM((landing, 128), BF), pltpu.VMEM((orders + 1, small_rows, D), F32), pltpu.VMEM((orders, small_rows, D), F32),
+         pltpu.VMEM((2, 2, D, D), BF), pltpu.VMEM((2, D, D), BF),
+         dma((sems,)), dma((sems,)), dma((2, peers)), dma((2, peers)), dma((2,)), dma((6,)), dma((6,)), dma((2,)), dma((len(PAIRS_OF), 2))],
+        flops=8 * heads * L * L * 256 + 4 * S * L * D, moved=2 * heads * L * L + 60 * L * D, vmem=63 * 2**20, collective_id=3, has_side_effects=True,
+    )(lengths, scol, backs[0].reshape(S, D), backs[1].reshape(S, D), middle, cotangent, inv, out_weight, gain_2,
+      qkv, qkv, qkv, o, p, h_one_t, query_weight, key_weight, value_weight, tokens, gain_1, d_router, rows_sent, d_tiles, d_parts)
+
+    FS = 8
+    T, R = L // FS, D // FS
+
+    def last_pair(s):
+        return jnp.minimum(s, pairs - 1)
+
+    def const(*shape):
+        return pl.BlockSpec(shape, lambda s, me: (0,) * len(shape))
+
+    rows_t = pl.BlockSpec((T, D), lambda s, me: (s, 0))
+    weight_pair = pl.BlockSpec((D, 128), lambda s, me: (0, last_pair(s)))
+    grad_part = pl.BlockSpec((2, R, D), lambda s, me: (0, s, 0))
+    mixed, d_query, d_key, d_value, d_out, gains, d_table, d_router, d_first, d_second = pl.pallas_call(
+        finish_kernel,
+        grid_spec=pltpu.PrefetchScalarGridSpec(
+            num_scalar_prefetch=1,
+            grid=(FS,),
+            in_specs=[SMEM, pl.BlockSpec((T, 128), lambda s, me: (s, 0)), const(S, D), const(S, D), rows_t,
+                      pl.BlockSpec((1, 4 * D, 128), lambda s, me: (last_pair(s), 0, 0)), const(small_rows, D), const(buckets, WIDE),
+                      pl.BlockSpec((2, 2, 1, R, D), lambda s, me: (0, 0, me[0], s, 0)), pl.BlockSpec((1, 2, 1, R, D), lambda s, me: (0, 0, 1, s, 0)),
+                      pl.BlockSpec((2, R, D), lambda s, me: (0, s, 0)), pl.BlockSpec((2, 2, R, D), lambda s, me: (0, 0, s, 0))],
+            out_specs=[rows_t, weight_pair, weight_pair, weight_pair, pl.BlockSpec((128, D), lambda s, me: (last_pair(s), 0)),
+                       const(8, D), const(buckets, heads), const(D, experts), grad_part, grad_part],
+        ),
+        out_shape=[struct((L, D), BF)] + [struct((D, D), F32)] * 4 + [struct((8, D), F32), struct((buckets, heads), F32), struct((D, experts), F32)] + [struct((2, D, D), F32)] * 2,
+        compiler_params=pltpu.CompilerParams(vmem_limit_bytes=BIG),
+        cost_estimate=pl.CostEstimate(flops=4 * S * L * D, bytes_accessed=60 * D * D, transcendentals=0),
+        name="finish",
+    )(lax.axis_index("dp").reshape(1), lengths, scol, rows_got[0].reshape(S, D), rows_got[1].reshape(S, D), middle, sums.reshape(pairs, 4 * D, 128), small, hot_near,
+      d_tiles, d_parts, rest, more)
+    return (mixed, grad_tokens, gains[0], gains[1], d_query, d_key, d_value, d_out, d_table, d_router, d_first, d_second)
 
 
 def solution(mesh):

time: 659 us -> 444 us (0.67)
  waiting for transfers between devices: 189 us -> 21.4 us
  local copies, waits for them, and re-layouts: 34.1 us -> 10.3 us
  starting transfers between devices: 23.6 us -> 6.48 us
  Pallas kernels: 377 us -> 393 us
  between operations: 15.3 us -> 1.53 us
  other arithmetic: 10.6 us -> 1.86 us
    unnamed x2 -> x0, waiting for transfers between devices: 144 us -> none
    all_to_all x3 -> x1, waiting for transfers between devices: 45.9 us -> 21.4 us  [exchange(): lax.all_to_all(values, 'expert', split_axis=0, concat_axis=0, tiled=True)]
    all_to_all x3 -> x1, starting transfers between devices: 23.6 us -> 6.48 us  [exchange(): lax.all_to_all(values, 'expert', split_axis=0, concat_axis=0, tiled=True)]
    squeeze x1 -> x0, local copies, waits for them, and re-layouts: 14.1 us -> none  [body(): d_tiles[:, 1]]
    pallas_call x1, Pallas kernels: 144 us -> 154 us  [body(): call(experts_kernel, 'experts', (16,), [whole(local, L), whole(local, 1,...]
    pallas_call x5 -> x2, Pallas kernels: 177 us -> 184 us  [the longest x1 163 us: body(): call(backward_kernel, 'backward', (first_token + combine_steps,), [SMEM,...]
    convert_element_type x1, other arithmetic: 7.69 us -> 0.64 us  [body(): (bucket_of(offsets)[None, :] == jnp.arange(buckets, dtype=I32)[:, None])....]
  transfers between devices with their start and end apart: 4 -> 1, of which waited for: 3 -> 1; matrix products, arithmetic and copies ran while one was open for 3% -> 1% of each run, Pallas kernels for 34% -> 10%
where the time goes in v4:
time: 444 us; the launch traced here: 435 us
  Pallas kernels  393 us (89%)
  waiting for transfers between devices  21.4 us (5%)
  local copies, waits for them, and re-layouts  10.3 us (2%)
  starting transfers between devices  6.48 us (1%)
    pallas_call x1, Pallas kernels, body(): call(backward_kernel, 'backward', (first_token + combine_steps,), [SMEM,...  163 us
    pallas_call x1, Pallas kernels, body(): call(experts_kernel, 'experts', (16,), [whole(local, L), whole(local, 1,...  154 us
    pallas_call x1, Pallas kernels, attn_fwd(): pl.pallas_call(attn_fwd_kernel, grid=(pairs,), in_specs=[SMEM, SMEM, blk(...  31.6 us
    all_to_all x1, waiting for transfers between devices, exchange(): lax.all_to_all(values, 'expert', split_axis=0, concat_axis=0, tiled=True)  21.4 us
    pallas_call x1, Pallas kernels, body(): pl.pallas_call(finish_kernel, grid_spec=pltpu.PrefetchScalarGridSpec(num_...  20.6 us
  transfers between devices with their start and end apart: 1, of which 1 were waited for; matrix products, arithmetic and copies ran while one was open for 1% of the time, Pallas kernels for 10%

profile of v4, /device:TPU:0, one launch (start us, length us, event | category | flops | bytes accessed | tf_op | source)
XLA Modules:
  0.0 435.0 jit_solution(1124184103969364309)
XLA Ops:
  1.3 1.7 copy.26.col_ref
  3.0 4.0 slots.1
  7.0 6.5 %dispatch_cotangent.1 = bf16[8,2,128,768]{3,2,1,0:T(8,128)(2,1)} custom-call(s32[1]{0:T(128)S(6)} %copy.35.len_ref, s32[2,1024]{1,0:T(2,128)} %get-tuple-element.47.srow_ref, bf16[1024,768]{1,0:T(8,128)(2,1)} %cot_ref.3), custom_call_target="tpu_custom_call" | custom-call | flops 3221225472 | bytes 4718592 | tf_op jit(solution)/shard_map/dispatch_cotangent/pallas_call | solution.py:805
  13.5 0.0 copy-start.3
  13.5 0.0 copy-start.1
  13.5 0.0 copy-start.4
  13.5 0.0 copy-start.2
  13.5 6.5 %all-to-all-start = ((bf16[8,2,128,768]{3,2,1,0:T(8,128)(2,1)}), bf16[8,2,128,768]{3,2,1,0:T(8,128)(2,1)}, u32[]{:S(2)}, u32[]{:S(2)}) async-start(bf16[8,2,128,768]{3,2,1,0:T(8,128)(2,1)} %dispatch_cotangent.1), calls=%async_computation | async-start | bytes 6291456 | tf_op jit(solution)/shard_map/all_to_all | solution.py:798
  20.0 0.0 copy-done.3
  20.0 0.6 broadcast_in_dim.4.gain_ref.gain1_ref
  20.6 0.0 copy-done.1
  20.6 0.1 fusion.6
  20.7 0.1 copy.32
  20.8 0.1 copy.33
  20.9 0.1 convolution_bitcast_fusion
  21.0 0.6 reshape.121.w_ref
  21.7 0.0 copy-done.4
  21.7 0.6 broadcast_in_dim.5.gain_ref.gain2_ref
  22.2 0.0 copy-done.2
  22.2 0.8 copy.29.wr_ref
  23.1 0.6 pad_maximum_fusion.far_ref
  23.6 8.0 %project.1 = (bf16[768,1024]{1,0:T(8,128)(2,1)}, bf16[1024,2304]{1,0:T(8,128)(2,1)}) custom-call(bf16[1024,768]{1,0:T(8,128)(2,1)} %x_ref.2, f32[1,768]{1,0:T(1,128)} %broadcast_in_dim.4.gain_ref.gain1_ref, bf16[768,768]{1,0:T(8,128)(2,1)} %wq_ref.3, bf16[768,768]{1,0:T(8,128)(2,1)} %wk_ref.3, bf16[768,768]{1,0:T(8,128)(2,1)} %wv_ref.3), custom_call_target="tpu_custom_call" | custom-call | flops 3623878656 | bytes 11403264 | tf_op jit(solution)/shard_map/project/pallas_call | solution.py:813
  31.6 31.6 %attention_forward.1 = (bf16[1024,768]{1,0:T(8,128)(2,1)}, f32[1024,768]{1,0:T(8,128)}, bf16[12,1024,1024]{2,1,0:T(8,128)(2,1)}) custom-call(s32[1]{0:T(128)S(6)} %copy.35.len_ref, f32[2,12]{1,0:T(2,128)} %pad_maximum_fusion.far_ref, bf16[1024,2304]{1,0:T(8,128)(2,1)} %get-tuple-element.49.q_ref.k_ref.v_ref, ...), custom_call_target="tpu_custom_call" | custom-call | flops 12884901888 | bytes 34603008 | tf_op jit(solution)/shard_map/attention_forward/pallas_call | solution.py:703
  63.2 5.7 %middle.1 = (f32[1024,768]{1,0:T(8,128)}, bf16[1024,768]{1,0:T(8,128)(2,1)}) custom-call(s32[1]{0:T(128)S(6)} %copy.35.len_ref, bf16[1024,768]{1,0:T(8,128)(2,1)} %x_ref.2, bf16[1024,768]{1,0:T(8,128)(2,1)} %get-tuple-element.50.o_ref, bf16[768,768]{1,0:T(8,128)(2,1)} %wo_ref.3, f32[1,768]{1,0:T(1,128)} %broadcast_in_dim.5.gain_ref.gain2_ref), custom_call_target="tpu_custom_call" | custom-call | flops 1207959552 | bytes 9043968 | tf_op jit(solution)/shard_map/middle/pallas_call | solution.py:827
  69.0 0.6 compare_convert_fusion.hot_ref
  69.6 0.6 fusion.hot_ref
  70.2 21.4 %all-to-all-done.g_ref = bf16[8,2,128,768]{3,2,1,0:T(8,128)(2,1)} async-done(((bf16[8,2,128,768]{3,2,1,0:T(8,128)(2,1)}), bf16[8,2,128,768]{3,2,1,0:T(8,128)(2,1)}, u32[]{:S(2)}, u32[]{:S(2)}) %all-to-all-start) | async-done | bytes 3145760 | tf_op jit(solution)/shard_map/all_to_all | solution.py:798
  91.7 153.6 %experts.1 = (bf16[2,1024,768]{2,1,0:T(8,128)(2,1)}, bf16[8,128,768]{2,1,0:T(8,128)(2,1)}, bf16[8,128,768]{2,1,0:T(8,128)(2,1)}, bf16[2,2,4,768,768]{4,3,2,1,0:T...) custom-call(s32[2,1024]{1,0:T(2,128)} %get-tuple-element.47.srow_ref, ...), custom_call_target="tpu_custom_call" | custom-call | flops 57982058496 | bytes 69206016 | tf_op jit(solution)/shard_map/experts/pallas_call | solution.py:837
  245.3 163.2 %backward.1 = (bf16[1024,768]{1,0:T(8,128)(2,1)}, bf16[18432,128]{1,0:T(8,128)(2,1)}, f32[40,768]{1,0:T(8,128)}, bf16[8,128,768]{2,1,0:T(8,128)(2,1)}, bf16[8,12...) custom-call(s32[1]{0:T(128)S(6)} %copy.35.len_ref, ...), custom_call_target="tpu_custom_call" | custom-call | flops 28991029248 | bytes 72351744 | tf_op jit(solution)/shard_map/backward/pallas_call | solution.py:876
  408.5 0.0 copy-start
  408.5 20.6 %finish.1 = (bf16[1024,768]{1,0:T(8,128)(2,1)}, f32[768,768]{1,0:T(8,128)}, f32[768,768]{1,0:T(8,128)}, f32[768,768]{1,0:T(8,128)}, f32[768,768]{1,0:T(8,128)}, ...) custom-call(s32[1]{0:T(128)} %bitcast.place_ref, ...), custom_call_target="tpu_custom_call" | custom-call | flops 3221225472 | bytes 35389440 | tf_op jit(solution)/shard_map/finish/pallas_call | solution.py:904
  429.1 1.8 copy.31
  430.9 1.4 slice_reduce_fusion
  432.3 1.4 copy.30
  433.7 0.0 copy-done
  433.7 1.1 copy.36
  (2 shorter events, 0.0 us)
Async XLA Ops:
  13.5 6.5 %copy-start.3 = (f32[768]{0:T(1024)S(1)}, f32[768]{0:T(1024)}, u32[]{:S(2)}) copy-start(f32[768]{0:T(1024)} %param.16) | copy-start | bytes 9220
  13.5 7.1 %copy-start.1 = (f32[32,12]{0,1:T(8,128)S(1)}, f32[32,12]{0,1:T(8,128)}, u32[]{:S(2)}) copy-start(f32[32,12]{0,1:T(8,128)} %param.22) | copy-start | bytes 4612
  13.5 8.1 %copy-start.4 = (f32[768]{0:T(1024)S(1)}, f32[768]{0:T(1024)}, u32[]{:S(2)}) copy-start(f32[768]{0:T(1024)} %param.17) | copy-start | bytes 9220
  13.5 8.7 %copy-start.2 = (bf16[768,16]{0,1:T(8,128)(2,1)S(1)}, bf16[768,16]{0,1:T(8,128)(2,1)}, u32[]{:S(2)}) copy-start(bf16[768,16]{0,1:T(8,128)(2,1)} %param.23) | copy-start | bytes 73732
  13.5 78.1 %all-to-all-start = ((bf16[8,2,128,768]{3,2,1,0:T(8,128)(2,1)}), bf16[8,2,128,768]{3,2,1,0:T(8,128)(2,1)}, u32[]{:S(2)}, u32[]{:S(2)}) async-start(bf16[8,2,128,768]{3,2,1,0:T(8,128)(2,1)} %dispatch_cotangent.1), calls=%async_computation | async-start | bytes 6291456 | tf_op jit(solution)/shard_map/all_to_all | solution.py:798
  408.5 25.2 %copy-start = (bf16[1024,768]{1,0:T(8,128)(2,1)S(1)}, bf16[1024,768]{1,0:T(8,128)(2,1)}, u32[]{:S(2)}) copy-start(bf16[1024,768]{1,0:T(8,128)(2,1)} %get-tuple-element.109) | copy-start | bytes 4718596

commit v5 on v4

v5 whole, which is shorter than its diff:
```python
import functools

import jax
import jax.numpy as jnp
from jax import lax
from jax.experimental import pallas as pl
from jax.experimental.pallas import tpu as pltpu
from jax.sharding import PartitionSpec as P

BF = jnp.bfloat16
F32 = jnp.float32
I32 = jnp.int32
EPSILON = 1e-06
THRESHOLDS = (12, 16, 23, 32, 46, 64, 91)
HIGHEST = lax.Precision.HIGHEST
SUB = 128
WIDE = 512
QT = 256
RB = 256
BIG = 56 * 2**20
GELU_C = 0.7978845608028654
GELU_A = 0.044715


def bucket_of(offsets):
    distance = jnp.abs(offsets)
    distant = 8 + sum(((distance >= limit).astype(I32) for limit in THRESHOLDS))
    nearby = jnp.where(distance < 8, distance, distant)
    return nearby + 16 * (offsets > 0).astype(I32)


def dot(a, b):
    return lax.dot_general(a, b, (((1,), (0,)), ((), ())), preferred_element_type=F32)


def dot_nt(a, b):
    return lax.dot_general(a, b, (((1,), (1,)), ((), ())), preferred_element_type=F32)


def dot_tn(a, b):
    return lax.dot_general(a, b, (((0,), (0,)), ((), ())), preferred_element_type=F32)


def iota(shape, dim):
    return lax.broadcasted_iota(I32, shape, dim)


SMEM = pl.BlockSpec(memory_space=pltpu.SMEM)


def whole(*shape):
    return pl.BlockSpec(shape, lambda *i: (0,) * len(shape))


def rows_of(width):
    return pl.BlockSpec((RB, width), lambda i: (i, 0))


def struct(shape, kind):
    return jax.ShapeDtypeStruct(shape, kind)


def call(kernel, name, grid, in_specs, out_specs, out_shape, scratch=(), flops=0, moved=0, transcendentals=0, vmem=BIG, **params):
    return pl.pallas_call(
        kernel,
        grid=grid,
        in_specs=in_specs,
        out_specs=out_specs,
        out_shape=out_shape,
        scratch_shapes=list(scratch),
        compiler_params=pltpu.CompilerParams(vmem_limit_bytes=vmem, **params),
        cost_estimate=pl.CostEstimate(flops=int(flops), bytes_accessed=int(moved), transcendentals=int(transcendentals)),
        name=name,
    )


def slots_of(local, most, experts, route):
    L = route.shape[1]
    hot = (iota((experts, L), 0) == route).astype(F32)
    upper = (iota((L, L), 0) < iota((L, L), 1)).astype(F32).astype(BF)
    rank = jnp.sum(dot(hot.astype(BF), upper) * hot, axis=0, keepdims=True).astype(I32)
    slot = (route // local) * most + rank
    rows = [jnp.where(route % local == e, slot, -1) for e in range(local)]
    line = iota((128, L), 0)
    table = jnp.full((128, L), -1, I32)
    for e in range(local):
        table = jnp.where(line == e, rows[e], table)
    return rows, table.astype(F32).T.astype(I32)


def near_offsets(shape, dim):
    place = iota(shape, dim)
    return jnp.where(place < 3 * SUB, place - SUB, place - WIDE - SUB)


def hot_offsets(buckets):
    return (bucket_of(near_offsets((buckets, WIDE), 1)) == iota((buckets, WIDE), 0)).astype(F32)


def dispatch_rows(srow, values, rows):
    hot = (iota((rows, srow.shape[1]), 0) == srow).astype(F32).astype(BF)
    return dot(hot, values).astype(BF)


def rms_scale(v):
    return lax.rsqrt(jnp.mean(v * v, axis=1, keepdims=True) + EPSILON)


def dp_partners(me):
    first, second = me % 2, me // 2
    return me + 1 - 2 * first, me + 2 - 4 * second, 3 - me


def remote(src, dst, send_sem, recv_sem, who):
    return pltpu.make_async_remote_copy(src_ref=src, dst_ref=dst, send_sem=send_sem, recv_sem=recv_sem, device_id=who,
                                        device_id_type=pl.DeviceIdType.MESH)


class Exchange:
    def __init__(self, src, dst, send_sems, recv_sems, own_sem, low=1, high=None):
        self.me = lax.axis_index("expert")
        self.n = lax.axis_size("expert")
        self.src, self.dst, self.send, self.recv, self.own = src, dst, send_sems, recv_sems, own_sem
        self.low, self.high = low, self.n if high is None else high

    def copy(self, k):
        to = lax.rem(self.me + k, self.n)
        return remote(self.src(to), self.dst(self.me), self.send.at[k], self.recv.at[k], {"expert": to})

    def mine(self):
        return pltpu.make_async_copy(self.src(self.me), self.dst(self.me), self.own)

    def each(self, what):
        def one(k, _):
            what(self.copy(k))
            return 0

        lax.fori_loop(self.low, self.high, one, 0)

    def start(self):
        self.each(lambda c: c.start())
        if self.low == 1:
            self.mine().start()

    def wait(self):
        self.each(lambda c: c.wait())
        if self.low == 1:
            self.mine().wait()


def greet(who):
    barrier = pltpu.get_barrier_semaphore()
    for device in who:
        pl.semaphore_signal(barrier, inc=1, device_id=device, device_id_type=pl.DeviceIdType.MESH)
    me, n = lax.axis_index("expert"), lax.axis_size("expert")

    def one(k, _):
        pl.semaphore_signal(barrier, inc=1, device_id={"expert": lax.rem(me + k, n)}, device_id_type=pl.DeviceIdType.MESH)
        return 0

    lax.fori_loop(1, n, one, 0)
    pl.semaphore_wait(barrier, len(who) + n - 1)


def forward_kernel(local, experts, len_ref, far_ref, route_ref, cot_ref, x_ref, gain1_ref, wq_ref, wk_ref, wv_ref, table_ref,
                   wo_ref, gain2_ref,
                   scol_ref, ht_ref, qkv_ref, o_ref, inv_ref, p_ref, middle_ref, send_ref, g0_ref, g1_ref, g1_sent_ref,
                   srow_s, h_s, g_s, qkv_s, o_s, near_s, g_send, g_recv, g_own, keep_sem):
    s = pl.program_id(0)
    L, D = cot_ref.shape
    pairs = D // 128
    blocks = L // RB
    peers, most, _ = g0_ref.shape

    def block(which):
        return lambda j: g_s.at[which, pl.ds(pl.multiple_of(j * most, 16), most)]

    moves = [Exchange(block(0), lambda j: g0_ref.at[j], g_send.at[0], g_recv.at[0], g_own.at[0]),
             Exchange(block(1), lambda j: g1_ref.at[j], g_send.at[1], g_recv.at[1], g_own.at[1], 1, peers // 2 + 1)]
    keep = pltpu.make_async_copy(g_s.at[1], g1_sent_ref, keep_sem)

    @pl.when(s == 0)
    def _():
        rows, columns = slots_of(local, most, experts, route_ref[...])
        scol_ref[...] = columns
        live = iota((L, 1), 0) < len_ref[0]
        values = jnp.where(live, cot_ref[...].astype(F32), 0.0).astype(BF)
        for e in range(local):
            srow_s[e:e + 1, :] = rows[e]
        g_s[0] = dispatch_rows(rows[0], values, peers * most)
        greet([])
        moves[0].start()
        g_s[1] = dispatch_rows(rows[1], values, peers * most)
        moves[1].start()
        keep.start()
        near = lax.dot_general(table_ref[...], hot_offsets(table_ref.shape[0]), (((0,), (0,)), ((), ())), precision=HIGHEST, preferred_element_type=F32)
        for p in range(pairs):
            near_s[p] = near[2 * p:2 * p + 2]

    @pl.when(s < blocks)
    def _():
        here = pl.ds(pl.multiple_of(s * RB, RB), RB)
        x = x_ref[...].astype(F32)
        h = (x * rms_scale(x) * gain1_ref[...].reshape(1, D)).astype(BF)
        ht_ref[...] = h.T
        for n, w_ref in enumerate((wq_ref, wk_ref, wv_ref)):
            part = dot(h, w_ref[...]).astype(BF)
            qkv_ref[:, n * D:(n + 1) * D] = part
            for p in range(pairs):
                qkv_s[n, p, here, :] = part[:, p * 128:(p + 1) * 128]

    @pl.when((s >= blocks) & (s < blocks + pairs))
    def _():
        pair = s - blocks
        o, inv = attention_pair(len_ref, far_ref, pair, qkv_s[0, pair], qkv_s[1, pair], qkv_s[2, pair], near_s[pair], p_ref)
        inv_ref[...] = inv
        o_ref[...] = o
        o_s[pair] = o

    @pl.when(s >= blocks + pairs)
    def _():
        r = s - blocks - pairs
        here = pl.ds(pl.multiple_of(r * RB, RB), RB)
        o = jnp.concatenate([o_s[p, here, :] for p in range(pairs)], axis=1)
        middle = x_ref[...].astype(F32) + dot(o, wo_ref[...])
        middle_ref[...] = middle
        live = iota((RB, 1), 0) + r * RB < len_ref[0]
        h = middle * rms_scale(middle) * gain2_ref[...].reshape(1, D)
        h_s[here, :] = jnp.where(live, h, 0.0).astype(BF)

    @pl.when(s == pl.num_programs(0) - 1)
    def _():
        for e in range(local):
            send_ref[e] = dispatch_rows(srow_s[e:e + 1, :], h_s[...], peers * most)
        keep.wait()
        for move in moves:
            move.wait()


def router(h, wr):
    logits = dot(h, wr)
    ex = jnp.exp(logits - jnp.max(logits, axis=1, keepdims=True))
    return ex / jnp.sum(ex, axis=1, keepdims=True)


def tile_order(step, me_dp):
    by_x, by_y, by_xy = dp_partners(me_dp)
    t = jnp.where(step < 8, step // 2, step % 4)
    return jnp.where(t == 0, by_xy, jnp.where(t == 1, by_x, jnp.where(t == 2, by_y, me_dp)))


def weight_tile(step, me_dp):
    return tile_order(jnp.minimum(step, 11), me_dp)


def experts_kernel(g0_ref, w1_ref, w2_ref, wr_ref, h_ref, g1_sent_ref, g1_ref,
                   rows_ref, back0_ref, back1_ref, d_ref, part_ref, more_ref, dr_ref,
                   send_s, land_s, gland_s, ht_s, gr_s, gate_s, probs_s, act_s, gp_s, rows_s, sent_s, stage_s, fwd_s, tmp_s,
                   h_send, h_recv, h_own, b_send, b_recv, b_own, d_local, r_send, r_recv, load_sem, g_load):
    step = pl.program_id(0)
    e = step // 8
    tile = tile_order(step, lax.axis_index("dp"))
    products = ((step < 8) & (step % 2 == 0)) | ((step >= 8) & (step < 12))
    first = (step == 0) | (step == 8)
    last = (step == 6) | (step == 11)
    _, peers, most, D = land_s.shape
    S = peers * most
    RC = 2 * RB
    group = RC // most
    me_dp = lax.axis_index("dp")
    mine = (iota((1, wr_ref.shape[1]), 1) == 2 * lax.axis_index("expert") + e).astype(F32)
    by_x, by_y, by_xy = dp_partners(me_dp)
    backs = (back0_ref, back1_ref)

    def block(buffer, which):
        return lambda j: buffer.at[which, pl.ds(pl.multiple_of(j * most, 16), most)]

    h_moves = [Exchange(block(h_ref, n), lambda j, n=n: land_s.at[n, j], h_send.at[n], h_recv.at[n], h_own.at[n]) for n in range(2)]
    b_moves = [Exchange(block(send_s, n), lambda j, n=n: backs[n].at[j], b_send.at[n], b_recv.at[n], b_own.at[n]) for n in range(2)]
    order = (by_xy, by_x, by_y, me_dp)
    g_move = Exchange(lambda j: g1_sent_ref.at[pl.ds(pl.multiple_of(j * most, 16), most)], lambda j: gland_s.at[j], h_send.at[2], h_recv.at[2], h_own.at[2],
                      peers // 2 + 1)

    def here_already(what):
        def one(k, _):
            j = lax.rem(lax.axis_index("expert") + peers - k, peers)
            what(pltpu.make_async_copy(g1_ref.at[j], gland_s.at[j], g_load.at[k]))
            return 0

        lax.fori_loop(0, peers // 2 + 1, one, 0)


    def store(n, t):
        return [pltpu.make_async_copy(stage_s.at[t % 2, m], d_ref.at[n, m, order[t]], d_local.at[t % 2, m]) for m in range(2)]

    def first_stage(n, m, k, sem):
        which = (by_xy, (by_x, by_y)[m])[k]
        return remote(d_ref.at[n, m, which], part_ref.at[n, m, k], r_send.at[sem], r_recv.at[sem], {"dp": (by_x, by_y)[m]})

    early = [first_stage(0, 0, 0, 0), first_stage(0, 1, 0, 1), first_stage(0, 0, 1, 2), first_stage(0, 1, 1, 3), first_stage(1, 0, 0, 4), first_stage(1, 1, 0, 5)]
    second = [remote(fwd_s.at[m], more_ref.at[m], r_send.at[6 + m], r_recv.at[6 + m], {"dp": (by_y, by_x)[m]}) for m in range(2)]

    def loads(m):
        return [pltpu.make_async_copy(d_ref.at[0, m, (by_y, by_x)[m]], tmp_s.at[m, 0], load_sem.at[m, 0]),
                pltpu.make_async_copy(part_ref.at[0, m, 0], tmp_s.at[m, 1], load_sem.at[m, 1])]

    @pl.when(step == 0)
    def _():
        greet([{"dp": by_x}, {"dp": by_y}])
        h_moves[0].start()
        h_moves[0].wait()
        h_moves[1].start()
        g_move.start()
        here_already(lambda c: c.start())

    turns = [(0, t, 2 * t + 1, (early[0:2], early[2:3], early[3:4], [])[t]) for t in range(4)]
    turns += [(1, t, 12 + t, (early[4:6], [], [], [])[t]) for t in range(4)]
    @pl.when(step == 8)
    def _():
        for c in early[0:2]:
            c.wait()
        for c in loads(0) + loads(1):
            c.start()
        for m in range(2):
            for c in loads(m):
                c.wait()
            fwd_s[m] = (tmp_s[m, 0].astype(F32) + tmp_s[m, 1].astype(F32)).astype(BF)
            second[m].start()
        h_moves[1].wait()
        g_move.wait()
        here_already(lambda c: c.wait())
        b_moves[0].start()

    @pl.when(first)
    def _():
        h = land_s[e].reshape(S, D)
        probs = router(h, wr_ref[...])
        probs_s[...] = probs
        gate = jnp.sum(probs * mine, axis=1, keepdims=True)
        gate_s[...] = jnp.broadcast_to(gate, gate_s.shape)

        @pl.when(e == 0)
        def _():
            gr_s[...] = (gate * g0_ref[...].astype(F32)).astype(BF)

        @pl.when(e == 1)
        def _():
            gr_s[...] = (gate * gland_s[...].reshape(S, D).astype(F32)).astype(BF)

        rows_s[...] = jnp.zeros_like(rows_s)
        sent_s[...] = jnp.zeros_like(sent_s)

    @pl.when(products)
    def _():
        w1 = w1_ref[0]
        w2 = w2_ref[0]
        for c in range(S // RC):
            sl = slice(c * RC, (c + 1) * RC)
            v = dot(land_s[e, c * group:(c + 1) * group].reshape(RC, D), w1)
            ga = dot_nt(gr_s[sl], w2)
            v2 = v * v
            t = jnp.tanh(v * (GELU_C + (GELU_C * GELU_A) * v2))
            half = 0.5 + 0.5 * t
            act = v * half
            slope = half + 2.0 * act * (1.0 - half) * (GELU_C + (3.0 * GELU_C * GELU_A) * v2)
            actb = act.astype(BF)
            gpre = (ga * slope).astype(BF)
            act_s[tile, sl] = actb
            gp_s[tile, sl] = gpre
            rows_s[sl] += dot(actb, w2)
            sent_s[sl] += dot_nt(gpre, w1)

    @pl.when(last)
    def _():
        rows = rows_s[...].astype(BF).astype(F32)
        gate = gate_s[:, :1]
        rows_ref[0] = (gate * rows).astype(BF)

        @pl.when(e == 0)
        def _():
            gate_s[:, 1:2] = jnp.sum(rows * g0_ref[...].astype(F32), axis=1, keepdims=True)

        @pl.when(e == 1)
        def _():
            gate_s[:, 1:2] = jnp.sum(rows * gland_s[...].reshape(S, D).astype(F32), axis=1, keepdims=True)

        grad_gate = gate_s[:, 1:2]
        h = land_s[e].reshape(S, D)
        gl = (grad_gate * gate * (mine - probs_s[...])).astype(BF)
        send_s[e] = (sent_s[...] + dot_nt(gl, wr_ref[...])).astype(BF)
        dr = dot_tn(gl, h)

        @pl.when(e == 0)
        def _():
            dr_ref[...] = dr

        @pl.when(e > 0)
        def _():
            dr_ref[...] += dr

    @pl.when(step == 11)
    def _():
        b_moves[1].start()

    @pl.when((step == 1) | (step == 12))
    def _():
        ht_s[...] = land_s[e].reshape(S, D).T

    @pl.when(jnp.logical_not(products))
    def _():
        slot = jnp.where(step < 8, step // 2, step) % 2
        stage_s[slot, 0] = dot(ht_s[...], gp_s[tile]).astype(BF)
        stage_s[slot, 1] = dot_tn(act_s[tile], gr_s[...]).astype(BF)

    for n, t, at, sends in turns[:-1]:
        @pl.when(step == at + 1)
        def _(n=n, t=t, sends=sends):
            for c in store(n, t):
                c.wait()
            for c in sends:
                c.start()

    for n, t, at, _ in turns:
        @pl.when(step == at)
        def _(n=n, t=t):
            for c in store(n, t):
                c.start()

    @pl.when(step == 15)
    def _():
        for c in store(1, 3):
            c.wait()
        for n in range(2):
            b_moves[n].wait()
        for c in early[2:] + second:
            c.wait()


def norm_back(v, gain, upstream):
    r = rms_scale(v)
    w = upstream * gain
    grad = r * w - v * (r * r * r) * jnp.mean(v * w, axis=1, keepdims=True)
    return grad, v * r * upstream


def combine_hot(scol, slots, e):
    return (iota((scol.shape[0], slots), 1) == scol[:, e:e + 1]).astype(F32).astype(BF)


def groups_of(direct):
    def bits(axis):
        return [1 << n for n in range(lax.axis_size(axis).bit_length() - 1)]

    dp, ex = bits("dp"), bits("expert")
    head = [("expert", tuple(ex[:1]))]
    rest = [("expert", tuple(ex[n:n + 2])) for n in range(1, len(ex), 2)]
    if direct:
        return [head + [("dp", tuple(dp))] + rest]
    ones = [("dp", (mask,)) for mask in dp]
    return [head + ones + rest, head + ones[::-1] + rest]


def members(axis, masks):
    me = lax.axis_index(axis)
    bits = [(me // mask) % 2 for mask in masks]
    place = sum(bit << n for n, bit in enumerate(bits))
    partners = []
    for relation in range(1, 1 << len(masks)):
        who, other = me, place
        for n, (mask, bit) in enumerate(zip(masks, bits)):
            if relation >> n & 1:
                who = who + mask * (1 - 2 * bit)
                other = other + (1 - 2 * bit) * (1 << n)
        partners.append(({axis: who}, other))
    return place, partners


def group_sizes(groups, rows):
    sizes = []
    for _, masks in groups:
        split = rows % (16 << len(masks)) == 0
        rows = rows >> len(masks) if split else rows
        sizes.append((rows, split, (1 << len(masks)) - 1))
    return sizes


def landing_rows(groups, rows):
    return sum(m * count for m, _, count in group_sizes(groups, rows))


def sem_count(groups, rows):
    return sum(count * (2 if split else 1) for _, split, count in group_sizes(groups, rows))


def add_rows(acc, start, recv, offset, rows, count):
    step = next(n for n in (256, 192, 128, 96, 64, 48, 32, 16) if rows % n == 0)

    def one(i, _):
        to = pl.ds(pl.multiple_of(start + i * step, 16), step)
        total = acc[to, :].astype(F32)
        for n in range(count):
            total = total + recv[pl.ds(pl.multiple_of(offset + n * rows + i * step, 16), step), :].astype(F32)
        acc[to, :] = total.astype(acc.dtype)
        return 0

    lax.fori_loop(0, rows // step, one, 0)


def sum_stages(groups, base, rows, acc, recv, landing, out, send_sem, recv_sem, own_sem, sem):
    stages, kept = [], []
    start, offset = base, landing

    def all_of(copies, after=None):
        def begin():
            for c in copies:
                c.start()

        def finish():
            for c in copies:
                c.wait()
            if after is not None:
                after()

        return begin, finish

    for (axis, masks), (m, split, count) in zip(groups, group_sizes(groups, rows)):
        place, partners = members(axis, masks)
        keep = start + place * m if split else start
        copies = []
        for n, (who, other) in enumerate(partners):
            give = start + other * m if split else start
            copies.append(remote(acc.at[pl.ds(pl.multiple_of(give, 16), m)], recv.at[pl.ds(offset + n * m, m)],
                                 send_sem.at[sem + n], recv_sem.at[sem + n], who))
        stages.append(all_of(copies, functools.partial(add_rows, acc, keep, recv, offset, m, count)))
        if split:
            kept.append((partners, keep, m))
        start = keep
        offset += m * count
        sem += count
    for number, (partners, at, m) in enumerate(kept[::-1]):
        here = pl.ds(pl.multiple_of(at, 16), m)
        source = acc if number == 0 else out
        copies = [remote(source.at[here], out.at[here], send_sem.at[sem + n], recv_sem.at[sem + n], who) for n, (who, _) in enumerate(partners)]
        if number == 0:
            copies.append(pltpu.make_async_copy(acc.at[here], out.at[here], own_sem))
        stages.append(all_of(copies))
        sem += len(partners)
    return stages


def whole_stages(groups, acc, recv, send_sem, recv_sem, sem):
    stages = []
    for n, (axis, masks) in enumerate(groups):
        copies = [remote(acc.at[n], recv.at[n, r], send_sem.at[sem + r], recv_sem.at[sem + r], who) for r, (who, _) in enumerate(members(axis, masks)[1])]

        def begin(copies=copies):
            for c in copies:
                c.start()

        def finish(copies=copies, n=n):
            total = acc[n]
            for r, c in enumerate(copies):
                c.wait()
                total = total + recv[n, r]
            acc[n + 1] = total

        stages.append((begin, finish))
        sem += len(copies)
    return stages


class Chain:
    def __init__(self, *lists):
        self.lists = lists
        self.steps = max(len(stages) for stages in lists) + 1

    def step(self, n):
        for stages in self.lists:
            if 0 < n <= len(stages):
                stages[n - 1][1]()
            if n < len(stages):
                stages[n][0]()


SMALL = 24
PAIRS_OF = ((0, 2), (2, 4), (4, 6))


CHUNK_AT = ((5, 6, 9, 11, 13, 15, 16), (7, 8, 10, 12, 14, 16), (9, 10, 12, 14, 16), (13, 15, 16), (9, 10, 12, 14, 16))


def chunk_lists(D):
    chunks = []
    for n, (low, high) in enumerate(PAIRS_OF):
        ways = groups_of(n == len(PAIRS_OF) - 1)
        rows = (high - low) * 4 * D // len(ways)
        chunks.append([(groups, low * 4 * D + w * rows, rows) for w, groups in enumerate(ways)])
    return chunks


def backward_kernel(len_ref, scol_ref, back0_ref, back1_ref, middle_ref, cot_ref, inv_ref, wo_ref, gain2_ref,
                    q_ref, k_ref, v_ref, o_ref, p_ref, ht_ref, wq_ref, wk_ref, wv_ref, x_ref, gain1_ref, dr_ref,
                    rows_ref, d_ref, part_ref,
                    token_ref, mixed_ref, sums_ref, small_ref, e0_ref, e1_ref, last_ref, more_ref,
                    backs_s, do_s, gb_s, gm_s, d3_s, acc_s, recv_s, sacc_s, srecv_s, fwd_s, tmp_s,
                    send_sem, recv_sem, e_send, e_recv, e_own, r_send, r_recv, load_sem, back_sem, out_sem):
    s = pl.program_id(0)
    me_dp = lax.axis_index("dp")
    by_x, by_y, by_xy = dp_partners(me_dp)
    pairs = do_s.shape[0]
    L, D = gm_s.shape
    combine_steps = L // RB
    first_pair, first_token = combine_steps, combine_steps + pairs
    first_mixed = first_token + combine_steps
    last = first_mixed + combine_steps - 1
    peers, most, _ = e0_ref.shape
    smalls = groups_of(True)[0]

    tile_rows = 4 * D
    chains = []
    landing, sem = 0, 0
    for c, lists in enumerate(chunk_lists(D)):
        made = []
        for n, (groups, base, rows) in enumerate(lists):
            made.append(sum_stages(groups, base, rows, acc_s, recv_s, landing, sums_ref, send_sem, recv_sem, out_sem.at[c, n], sem))
            landing += landing_rows(groups, rows)
            sem += sem_count(groups, rows)
        chains.append(Chain(*made))
    router_rows = dr_ref.shape[0] * pairs
    router_chain = Chain(sum_stages(smalls, pairs * tile_rows, router_rows, acc_s, recv_s, landing, sums_ref, send_sem, recv_sem, out_sem.at[len(chains), 0], sem))
    landing += landing_rows(smalls, router_rows)
    sem += sem_count(smalls, router_rows)
    small_chain = Chain(whole_stages(smalls, sacc_s, srecv_s, send_sem, recv_sem, sem))

    def block(which):
        return lambda j: rows_ref.at[which, pl.ds(pl.multiple_of(j * most, 16), most)]

    homes = [Exchange(block(n), lambda j, ref=ref: ref.at[j], e_send.at[n], e_recv.at[n], e_own.at[n]) for n, ref in enumerate((e0_ref, e1_ref))]

    fetch = [pltpu.make_async_copy(ref, backs_s.at[n], back_sem.at[n]) for n, ref in enumerate((back0_ref, back1_ref))]
    outputs = [pltpu.make_async_copy(ref, backs_s.at[n], back_sem.at[n]) for n, ref in enumerate((e0_ref, e1_ref))]

    rest = [remote(d_ref.at[1, m, (by_x, by_y)[m]], last_ref.at[m], r_send.at[m], r_recv.at[m], {"dp": (by_x, by_y)[m]}) for m in range(2)]
    second = [remote(fwd_s.at[m], more_ref.at[m], r_send.at[2 + m], r_recv.at[2 + m], {"dp": (by_y, by_x)[m]}) for m in range(2)]

    def loads(m):
        return [pltpu.make_async_copy(d_ref.at[1, m, (by_y, by_x)[m]], tmp_s.at[0], load_sem.at[0]),
                pltpu.make_async_copy(part_ref.at[1, m, 0], tmp_s.at[1], load_sem.at[1])]

    @pl.when(s == 0)
    def _():
        greet([{"dp": by_x}, {"dp": by_y}, {"dp": by_xy}])
        for c in rest:
            c.start()
        homes[0].start()
        for c in loads(0) + fetch:
            c.start()
        for n in range(pairs):
            acc_s[pl.ds(pairs * tile_rows + n * dr_ref.shape[0], dr_ref.shape[0]), :] = dr_ref[:, n * 128:(n + 1) * 128].astype(BF)
        for c in fetch:
            c.wait()

    @pl.when(s == first_pair + 1)
    def _():
        homes[1].start()

    for m in range(2):
        @pl.when(s == m + 1)
        def _(m=m):
            for c in loads(m):
                c.wait()
            fwd_s[m] = (tmp_s[0].astype(F32) + tmp_s[1].astype(F32)).astype(BF)
            second[m].start()
            if m == 0:
                for c in loads(1):
                    c.start()

    def gathered():
        scol = scol_ref[...]
        S = peers * most
        return sum(dot(combine_hot(scol, S, n), backs_s[n].reshape(S, D)) for n in range(2))

    @pl.when(s < combine_steps)
    def _():
        here = pl.ds(pl.multiple_of(s * RB, RB), RB)
        live = iota((RB, 1), 0) + s * RB < len_ref[0]
        gv, gg = norm_back(middle_ref[...], gain2_ref[...].reshape(1, D), jnp.where(live, gathered(), 0.0))
        gm = jnp.where(live, cot_ref[...].astype(F32), 0.0) + gv
        gm_s[here, :] = gm
        gb = gm.astype(BF)
        gb_s[here, :] = gb
        do = (dot_nt(gb, wo_ref[...]) * inv_ref[...]).astype(BF)
        for p in range(pairs):
            do_s[p, here, :] = do[:, p * 128:(p + 1) * 128]
        gs = jnp.sum(gg, axis=0, keepdims=True)

        @pl.when(s == 0)
        def _():
            sacc_s[0] = jnp.zeros_like(small_ref)
            sacc_s[0, 1:2, :] = gs

        @pl.when(s > 0)
        def _():
            sacc_s[0, 1:2, :] += gs

    @pl.when((s >= first_pair) & (s < first_token))
    def _():
        pair = s - first_pair

        dq, dk, dv = attention_back(
            q_ref[...], k_ref[...], v_ref[...], do_s[pair], o_ref[...], p_ref,
            sacc_s, 2 * pair)
        d3 = jnp.concatenate([dq, dk, dv], axis=1)
        for n, part in enumerate((dq, dk, dv)):
            d3_s[n, pair] = part
        dw = dot(ht_ref[...], d3).astype(BF)
        base = pair * tile_rows
        for n in range(3):
            acc_s[pl.ds(pl.multiple_of(base + n * D, 128), D), :] = dw[:, n * 128:(n + 1) * 128]
        dwo = dot_tn(o_ref[...], gb_s[...]).astype(BF)
        for n in range(pairs):
            acc_s[pl.ds(pl.multiple_of(base + 3 * D + n * 128, 128), 128), :] = dwo[:, n * 128:(n + 1) * 128]

    @pl.when((s >= first_token) & (s < first_mixed))
    def _():
        r = s - first_token
        here = pl.ds(pl.multiple_of(r * RB, RB), RB)
        gh = sum(dot_nt(jnp.concatenate([d3_s[n, p, here, :] for p in range(pairs)], axis=1), w[...]) for n, w in enumerate((wq_ref, wk_ref, wv_ref)))
        gv, gg = norm_back(x_ref[...].astype(F32), gain1_ref[...].reshape(1, D), gh)
        token_ref[...] = (gm_s[here, :] + gv).astype(BF)
        sacc_s[0, 0:1, :] += jnp.sum(gg, axis=0, keepdims=True)

    @pl.when(s == first_mixed)
    def _():
        for home in homes:
            home.wait()
        for c in outputs:
            c.start()
        for c in outputs:
            c.wait()

    @pl.when(s >= first_mixed)
    def _():
        r = s - first_mixed
        live = iota((RB, 1), 0) + r * RB < len_ref[0]
        mixed_ref[...] = jnp.where(live, middle_ref[...] + gathered(), 0.0).astype(BF)

    chunk_steps = [dict(zip(at, range(len(at)))) for at in CHUNK_AT]
    for t in range(first_pair, last):
        now = [(chain, taken[t]) for chain, taken in zip([*chains, small_chain, router_chain], chunk_steps) if t in taken]
        if now:
            @pl.when(s == t)
            def _(now=now):
                for chain, n in now:
                    chain.step(n)

    @pl.when(s == last)
    def _():
        todo = [(chain, len([t for t in taken if t < last])) for chain, taken in zip([*chains, small_chain, router_chain], chunk_steps)]
        for t in range(max(chain.steps - n for chain, n in todo)):
            for chain, n in todo:
                chain.step(n + t)
        small_ref[...] = sacc_s[len(smalls)]
        for c in rest + second:
            c.wait()


def finish_kernel(place_ref, sums_ref, router_sum_ref, small_ref, own_ref, part_ref, rest_ref, more0_ref, more1_ref,
                  dq_ref, dk_ref, dv_ref, do_ref, gain1_ref, gain2_ref, table_ref, router_ref, first_ref, second_ref):
    s = pl.program_id(0)
    D = dq_ref.shape[0]
    pairs = D // 128
    for n, ref in enumerate((dq_ref, dk_ref, dv_ref)):
        ref[...] = sums_ref[n * D:(n + 1) * D, :].astype(F32)
    for n in range(pairs):
        do_ref[:, n * 128:(n + 1) * 128] = sums_ref[3 * D + n * 128:3 * D + (n + 1) * 128, :].astype(F32)
    for m, ref in enumerate((first_ref, second_ref)):
        ref[0] = own_ref[0, m, 0].astype(F32) + part_ref[0, m, 0].astype(F32) + more0_ref[m].astype(F32)
        ref[1] = own_ref[1, m, 0].astype(F32) + rest_ref[m].astype(F32) + more1_ref[m].astype(F32)

    @pl.when(s == 0)
    def _():
        gain1_ref[...] = small_ref[0:1, :].reshape(D)
        gain2_ref[...] = small_ref[1:2, :].reshape(D)
        heads = table_ref.shape[1]
        per_head = small_ref[8:SMALL, :]
        buckets = table_ref.shape[0]
        table = lax.dot_general(hot_offsets(buckets), per_head[:, :WIDE], (((1,), (1,)), ((), ())), precision=HIGHEST, preferred_element_type=F32)
        left = jnp.sum(per_head[:, WIDE:WIDE + 128].T, axis=0, keepdims=True)
        right = jnp.sum(per_head[:, WIDE + 128:].T, axis=0, keepdims=True)
        bucket = iota(table.shape, 0)
        table = table + jnp.where(bucket == buckets // 2 - 1, left, 0.0) + jnp.where(bucket == buckets - 1, right, 0.0)
        table_ref[...] = table[:, :heads]
        experts = router_ref.shape[1]
        sums = router_sum_ref[...].astype(F32)
        for n in range(pairs):
            router_ref[n * 128:(n + 1) * 128, :] = sums[n * experts:(n + 1) * experts].T


def near_bias(w_row):
    full = jnp.broadcast_to(w_row, (SUB, 512))
    return pltpu.roll(full, 0, 1, stride=1, stride_axis=0)[:, :384]


def attention_pair(len_ref, far_ref, pair, q, k, v, w, p_ref):
    L = q.shape[0]
    nb = L // SUB
    seq_len = len_ref[0]
    lane = iota((L, 128), 1)
    row = iota((L, 128), 0)
    blk = row // SUB
    outs = []
    for a in range(2):
        head = 2 * pair + a
        own = (lane < 64) if a == 0 else (lane >= 64)
        base = 64 if a == 0 else 0
        al = lane - base
        c_left = far_ref[0, head]
        c_right = far_ref[1, head]
        kb = al % 8
        val = jnp.where(kb <= blk - 2, c_left, jnp.where(kb >= blk + 2, c_right, 0.0))
        hi = val.astype(BF).astype(F32)
        r1 = val - hi
        mid = r1.astype(BF).astype(F32)
        lo = r1 - mid
        qaug = jnp.where(al < 8, hi, jnp.where(al < 16, mid, jnp.where(al < 24, lo, jnp.where(al == 24, 1.0, 0.0)))).astype(BF)
        kaug = jnp.where(al < 24, (kb == blk).astype(F32), jnp.where((al == 24) & (row >= seq_len), -1e30, 0.0)).astype(BF)
        qa = jnp.where(own, q, qaug)
        ka = jnp.where(own, k, kaug)
        va = jnp.where(own, v, jnp.ones_like(v))
        near = near_bias(w[a:a + 1, :])
        parts = []
        for t in range(L // QT):
            s = dot_nt(qa[t * QT:(t + 1) * QT], ka)
            rows = []
            for u in range(QT // SUB):
                b = t * (QT // SUB) + u
                lo_b, hi_b = max(b - 1, 0), min(b + 2, nb)
                su = s[u * SUB:(u + 1) * SUB]
                pieces = []
                if lo_b > 0:
                    pieces.append(su[:, :lo_b * SUB])
                pieces.append(su[:, lo_b * SUB:hi_b * SUB] + near[:, (lo_b - b + 1) * SUB:(hi_b - b + 1) * SUB])
                if hi_b < nb:
                    pieces.append(su[:, hi_b * SUB:])
                rows.append(jnp.concatenate(pieces, axis=1))
            s = jnp.concatenate(rows, axis=0)
            m = jnp.max(s, axis=1, keepdims=True)
            p = jnp.exp(s - m).astype(BF)
            p_ref[a, t * QT:(t + 1) * QT, :] = p
            parts.append(dot(p, va))
        outs.append(jnp.concatenate(parts, axis=0))
    first = lane < 64
    num = jnp.where(first, outs[0], outs[1])
    den = pltpu.roll(jnp.where(first, outs[1], outs[0]), 64, 1)
    inv = 1.0 / den
    return (num * inv).astype(BF), inv


def attention_back(q, k, v, do, o, p_ref, sums, sums_row):
    L = q.shape[0]
    nb = L // SUB
    lane = iota((L, 128), 1)
    row = iota((L, 128), 0)
    blk = row // SUB
    prod = do.astype(F32) * o.astype(F32)
    zero = jnp.zeros_like(q)
    dk = dv = None
    dqs = []
    for a in range(2):
        own = (lane < 64) if a == 0 else (lane >= 64)
        base = 64 if a == 0 else 0
        al = lane - base
        inner = jnp.sum(jnp.where(own, prod, 0.0), axis=1, keepdims=True)
        hi = inner.astype(BF)
        lo = (inner - hi.astype(F32)).astype(BF)
        doa = jnp.where(own, do, jnp.where(al == 0, hi, jnp.where(al == 1, lo, zero)))
        va = jnp.where(own, v, jnp.where((al == 0) | (al == 1), -1.0, 0.0).astype(BF))
        ka = jnp.where(own, k, (al == blk).astype(F32).astype(BF))
        qm = jnp.where(own, q, zero)
        dom = jnp.where(own, do, zero)
        near = None
        dq = []
        dsl = []
        for t in range(L // QT):
            sl = slice(t * QT, (t + 1) * QT)
            x = dot_nt(doa[sl], va)
            pt = p_ref[a, sl, :]
            dsf = pt.astype(F32) * x
            ds = dsf.astype(BF)
            dq.append(dot(ds, ka))
            ck = dot_tn(ds, qm[sl])
            cv = dot_tn(pt, dom[sl])
            dk = ck if dk is None else dk + ck
            dv = cv if dv is None else dv + cv
            for u in range(QT // SUB):
                b = t * (QT // SUB) + u
                pieces = []
                if b == 0:
                    pieces.append(jnp.zeros((SUB, SUB), F32))
                lo_b, hi_b = max(b - 1, 0), min(b + 2, nb)
                pieces.append(dsf[u * SUB:(u + 1) * SUB, lo_b * SUB:hi_b * SUB])
                if b == nb - 1:
                    pieces.append(jnp.zeros((SUB, SUB), F32))
                piece = jnp.concatenate(pieces, axis=1) if len(pieces) > 1 else pieces[0]
                near = piece if near is None else near + piece
        dq = jnp.concatenate(dq, axis=0)
        dqs.append(dq)
        far = pltpu.roll(dq, 64, 1) if a == 0 else dq
        left = jnp.sum(jnp.where((lane < 8) & (lane <= blk - 2), far, 0.0), axis=0, keepdims=True)
        right = jnp.sum(jnp.where((lane < 8) & (lane >= blk + 2), far, 0.0), axis=0, keepdims=True)
        full = jnp.concatenate([near, jnp.zeros((SUB, 128), F32)], axis=1)
        rows = SUB
        while rows > 8:
            rows //= 2
            full = full[:rows] + pltpu.roll(full[rows:], 512 - rows, 1)
        place = iota((8, 512), 0)
        for step in (4, 2, 1):
            full = jnp.where((place & step) > 0, pltpu.roll(full, 512 - step, 1), full)
        diag = jnp.sum(full, axis=0, keepdims=True)
        line = jnp.concatenate([diag, left, right], axis=1)
        kept = sums[0, 8:SMALL, :]
        sums[0, 8:SMALL, :] = jnp.where(iota(kept.shape, 0) == sums_row + a, line, kept)
    return jnp.where(lane < 64, dqs[0], dqs[1]).astype(BF), dk.astype(BF), dv.astype(BF)


def body(tokens, cotangent, gain_one, gain_two, query_weight, key_weight, value_weight, out_weight, bias_table,
         router_weight, expert_in, expert_out, lengths, routes):
    L, D = tokens.shape
    buckets, heads = bias_table.shape
    experts = router_weight.shape[1]
    local = expert_in.shape[0]
    peers = lax.axis_size("expert")
    n_dp = lax.axis_size("dp")
    most = 2 * L // experts
    S = peers * most
    steps = L // RB
    me = lax.axis_index("expert")
    def once(*shape):
        return pl.BlockSpec(shape, lambda *i: (0,) * len(shape), pipeline_mode=pl.Buffered(1))

    edge = buckets // 2
    far = jnp.stack([bias_table[edge - 1], bias_table[buckets - 1]])
    pairs = heads // 2
    anywhere = pl.BlockSpec(memory_space=pl.ANY)
    dma = pltpu.SemaphoreType.DMA

    def clipped(s, low, count):
        return jnp.clip(s - low, 0, count - 1)

    first_rows = lambda width: pl.BlockSpec((RB, width), lambda s: (clipped(s, 0, steps), 0))
    last_rows = lambda width: pl.BlockSpec((RB, width), lambda s: (clipped(s, steps + pairs, steps), 0))
    at_pair = pl.BlockSpec((L, 128), lambda s: (0, clipped(s, steps, pairs)))
    scol, h_one_t, qkv, o, inv, p, middle, h_sent, g_first, g_second, g_sent = call(
        functools.partial(forward_kernel, local, experts), "forward", (2 * steps + pairs,),
        [SMEM, SMEM, once(1, L), once(L, D), pl.BlockSpec((RB, D), lambda s: (jnp.where(s < steps + pairs, clipped(s, 0, steps), s - steps - pairs), 0)),
         once(D), once(D, D), once(D, D), once(D, D), once(buckets, heads), once(D, D), once(D)],
        [whole(L, 128), pl.BlockSpec((D, RB), lambda s: (0, clipped(s, 0, steps))), first_rows(3 * D), at_pair, at_pair,
         pl.BlockSpec((2, L, L), lambda s: (clipped(s, steps, pairs), 0, 0)), last_rows(D), whole(local, S, D), anywhere, anywhere, anywhere],
        [struct((L, 128), I32), struct((D, L), BF), struct((L, 3 * D), BF), struct((L, D), BF), struct((L, D), F32),
         struct((heads, L, L), BF), struct((L, D), F32), struct((local, S, D), BF), struct((peers, most, D), BF), struct((peers, most, D), BF), struct((S, D), BF)],
        [pltpu.VMEM((local, L), I32), pltpu.VMEM((L, D), BF), pltpu.VMEM((2, S, D), BF), pltpu.VMEM((3, pairs, L, 128), BF), pltpu.VMEM((pairs, L, 128), BF), pltpu.VMEM((pairs, 2, WIDE), F32), dma((2, peers)), dma((2, peers)), dma((2,)), dma],
        flops=8 * L * D * D + 4 * heads * L * L * 256, moved=2 * heads * L * L + 40 * L * D, transcendentals=heads * L * L,
        collective_id=1, has_side_effects=True,
    )(lengths, far, routes.reshape(1, L), cotangent, tokens, gain_one, query_weight, key_weight, value_weight, bias_table, out_weight, gain_two)
    g_first = g_first.reshape(S, D)

    FF = expert_in.shape[2]
    FT = FF // 4
    rows_sent, *backs, d_tiles, d_parts, more_0, d_router = call(
        experts_kernel, "experts", (16,),
        [once(S, D),
         pl.BlockSpec((1, D, FT), lambda s: (s // 8, 0, weight_tile(s, lax.axis_index("dp")))),
         pl.BlockSpec((1, FT, D), lambda s: (s // 8, weight_tile(s, lax.axis_index("dp")), 0)), whole(D, experts), anywhere, anywhere, anywhere],
        [pl.BlockSpec((1, S, D), lambda s: (s // 8, 0, 0)), anywhere, anywhere, anywhere, anywhere, anywhere, whole(experts, D)],
        [struct((2, S, D), BF), struct((peers, most, D), BF), struct((peers, most, D), BF), struct((2, 2, 4, D, D), BF), struct((2, 2, 2, D, D), BF),
         struct((2, D, D), BF), struct((experts, D), F32)],
        [pltpu.VMEM((2, S, D), BF), pltpu.VMEM((2, peers, most, D), BF), pltpu.VMEM((peers, most, D), BF), pltpu.VMEM((D, S), BF), pltpu.VMEM((S, D), BF), pltpu.VMEM((S, 128), F32), pltpu.VMEM((S, experts), F32),
         pltpu.VMEM((4, S, FT), BF), pltpu.VMEM((4, S, FT), BF), pltpu.VMEM((S, D), F32), pltpu.VMEM((S, D), F32), pltpu.VMEM((2, 2, D, D), BF),
         pltpu.VMEM((2, D, D), BF), pltpu.VMEM((2, 2, D, D), BF),
         dma((3, peers)), dma((3, peers)), dma((3,)), dma((2, peers)), dma((2, peers)), dma((2,)), dma((2, 2)), dma((8,)), dma((8,)), dma((2, 2)), dma((peers,))],
        flops=24 * S * D * FF, moved=24 * D * FF + 16 * S * D, transcendentals=2 * S * FF, vmem=63 * 2**20, collective_id=2, has_side_effects=True,
    )(g_first, expert_in, expert_out, router_weight, h_sent, g_sent, g_second)

    combine_steps = L // RB
    first_token = combine_steps + pairs
    first_mixed = first_token + combine_steps
    lists = [item for chunk in chunk_lists(D) for item in chunk]
    smalls = groups_of(True)[0]
    router_rows = experts * pairs
    lists.append((smalls, 0, router_rows))
    landing = sum(landing_rows(groups, rows) for groups, _, rows in lists)
    sems = sum(sem_count(groups, rows) for groups, _, rows in lists) + sum((1 << len(masks)) - 1 for _, masks in smalls)
    tiles = pairs * 4 * D + router_rows

    def early(width):
        return pl.BlockSpec((RB, width), lambda s: (jnp.minimum(s, combine_steps - 1), 0))

    def both(width):
        return pl.BlockSpec((RB, width), lambda s: (jnp.where(s < first_mixed, jnp.minimum(s, combine_steps - 1), s - first_mixed), 0))

    def late(width):
        return pl.BlockSpec((RB, width), lambda s: (jnp.clip(s - first_token, 0, combine_steps - 1), 0))

    def output(width):
        return pl.BlockSpec((RB, width), lambda s: (jnp.maximum(s - first_mixed, 0), 0))

    def pair_of(s):
        return jnp.clip(s - combine_steps, 0, pairs - 1)

    def pair(first=0):
        return pl.BlockSpec((L, 128), lambda s: (0, first + pair_of(s)))

    grad_tokens, mixed, sums, small, _, _, rest, more_1 = call(
        backward_kernel, "backward", (first_mixed + combine_steps,),
        [SMEM, both(128), anywhere, anywhere, both(D), early(D), early(D), once(D, D), once(D),
         pair(0), pair(pairs), pair(2 * pairs), pair(0), pl.BlockSpec((2, L, L), lambda s: (pair_of(s), 0, 0)), once(D, L)]
        + [once(D, D)] * 3 + [late(D), once(D), once(experts, D), anywhere, anywhere, anywhere],
        [late(D), output(D), anywhere, whole(SMALL, D), anywhere, anywhere, anywhere, anywhere],
        [struct((L, D), BF), struct((L, D), BF), struct((tiles, 128), BF), struct((SMALL, D), F32), struct((peers, most, D), BF), struct((peers, most, D), BF),
         struct((2, D, D), BF), struct((2, D, D), BF)],
        [pltpu.VMEM((2, peers, most, D), BF), pltpu.VMEM((pairs, L, 128), BF), pltpu.VMEM((L, D), BF), pltpu.VMEM((L, D), F32), pltpu.VMEM((3, pairs, L, 128), BF),
         pltpu.VMEM((tiles, 128), BF), pltpu.VMEM((landing, 128), BF), pltpu.VMEM((len(smalls) + 1, SMALL, D), F32), pltpu.VMEM((len(smalls), 3, SMALL, D), F32),
         pltpu.VMEM((2, D, D), BF), pltpu.VMEM((2, D, D), BF),
         dma((sems,)), dma((sems,)), dma((2, peers)), dma((2, peers)), dma((2,)), dma((4,)), dma((4,)), dma((2,)), dma((2,)), dma((len(PAIRS_OF) + 1, 2))],
        flops=8 * heads * L * L * 256 + 4 * S * L * D, moved=2 * heads * L * L + 60 * L * D, vmem=63 * 2**20, collective_id=3, has_side_effects=True,
    )(lengths, scol, *backs, middle, cotangent, inv, out_weight, gain_two,
      qkv, qkv, qkv, o, p, h_one_t, query_weight, key_weight, value_weight, tokens, gain_one, d_router, rows_sent, d_tiles, d_parts)

    FS = 8
    R = D // FS

    def last_pair(s):
        return jnp.minimum(s, pairs - 1)

    def const(*shape):
        return pl.BlockSpec(shape, lambda s, me: (0,) * len(shape))

    weight_pair = pl.BlockSpec((D, 128), lambda s, me: (0, last_pair(s)))
    grad_part = pl.BlockSpec((2, R, D), lambda s, me: (0, s, 0))
    d_query, d_key, d_value, d_out, d_gain_1, d_gain_2, d_table, d_router, d_first, d_second = pl.pallas_call(
        finish_kernel,
        grid_spec=pltpu.PrefetchScalarGridSpec(
            num_scalar_prefetch=1,
            grid=(FS,),
            in_specs=[pl.BlockSpec((4 * D, 128), lambda s, me: (last_pair(s), 0)), pl.BlockSpec((router_rows, 128), lambda s, me: (pairs * 4 * D // router_rows, 0)),
                      const(SMALL, D),
                      pl.BlockSpec((2, 2, 1, R, D), lambda s, me: (0, 0, me[0], s, 0)), pl.BlockSpec((1, 2, 1, R, D), lambda s, me: (0, 0, 1, s, 0)),
                      grad_part, grad_part, grad_part],
            out_specs=[weight_pair, weight_pair, weight_pair, pl.BlockSpec((128, D), lambda s, me: (last_pair(s), 0)),
                       const(D), const(D), const(buckets, heads), const(D, experts), grad_part, grad_part],
        ),
        out_shape=[struct((D, D), F32)] * 4 + [struct((D,), F32)] * 2 + [struct((buckets, heads), F32), struct((D, experts), F32)] + [struct((2, D, D), F32)] * 2,
        compiler_params=pltpu.CompilerParams(vmem_limit_bytes=BIG),
        cost_estimate=pl.CostEstimate(flops=D * D, bytes_accessed=60 * D * D, transcendentals=0),
        name="finish",
    )(lax.axis_index("dp").reshape(1), sums, sums, small, d_tiles, d_parts, rest, more_0, more_1)
    return (mixed, grad_tokens, d_gain_1, d_gain_2, d_query, d_key, d_value, d_out, d_table, d_router, d_first, d_second)


def solution(mesh):
    rows = P(("dp", "expert"), None)
    return jax.shard_map(
        body,
        mesh=mesh,
        in_specs=(rows, rows, P(), P(), P(), P(), P(), P(), P(), P(), P("expert", None, None), P("expert", None, None), P(("dp", "expert")), rows),
        out_specs=(rows, rows, P(), P(), P(), P(), P(), P(), P(), P(), P("expert", None, "dp"), P("expert", "dp", None)),
        check_vma=False,
    )
```

time: 444 us -> 400 us (0.901); the launches traced: 435 us -> 396 us
  waiting for transfers between devices: 21.4 us -> 0 us
  Pallas kernels: 393 us -> 386 us
  starting transfers between devices: 6.48 us -> 0 us
    all_to_all x1 -> x0, waiting for transfers between devices: 21.4 us -> none  [exchange(): lax.all_to_all(values, 'expert', split_axis=0, concat_axis=0, tiled=True)]
    all_to_all x1 -> x0, starting transfers between devices: 6.48 us -> none  [exchange(): lax.all_to_all(values, 'expert', split_axis=0, concat_axis=0, tiled=True)]
    pallas_call x1, Pallas kernels: 20.6 us -> 15.7 us  [body(): pl.pallas_call(finish_kernel, grid_spec=pltpu.PrefetchScalarGridSpec(num_...]
    pallas_call x7 -> x3, Pallas kernels: 373 us -> 371 us  [the longest x1 155 us: body(): call(experts_kernel, 'experts', (16,), [once(S, D), pl.BlockSpec((1, D, F...]
  transfers between devices with their start and end apart: 1 -> 0, of which waited for: 1 -> 0; matrix products, arithmetic and copies ran while one was open for 1% -> 0% of each run, Pallas kernels for 10% -> 0%
where the time goes in v5:
time: 400 us; the launch traced here: 396 us
  Pallas kernels  386 us (96%)
  local copies, waits for them, and re-layouts  7.16 us (2%)
    pallas_call x1, Pallas kernels, body(): call(experts_kernel, 'experts', (16,), [once(S, D), pl.BlockSpec((1, D, F...  155 us
    pallas_call x1, Pallas kernels, body(): call(backward_kernel, 'backward', (first_mixed + combine_steps,), [SMEM,...  146 us
    pallas_call x1, Pallas kernels, body(): call(functools.partial(forward_kernel, local, experts), 'forward', (2 * s...  69.7 us
    pallas_call x1, Pallas kernels, body(): pl.pallas_call(finish_kernel, grid_spec=pltpu.PrefetchScalarGridSpec(num_...  15.7 us

profile of v5, /device:TPU:0, one launch (start us, length us, event | category | flops | bytes accessed | tf_op | source)
XLA Modules:
  0.0 395.5 jit_solution(10110197808039741432)
XLA Ops:
  0.6 0.8 copy.26.table_ref
  1.4 0.0 copy-start.3
  1.4 0.6 pad_maximum_fusion.far_ref
  2.7 0.0 copy-done.3
  2.7 0.0 copy-start.2
  2.7 69.7 %forward.1 = (s32[1024,128]{1,0:T(8,128)}, bf16[768,1024]{1,0:T(8,128)(2,1)}, bf16[1024,2304]{1,0:T(8,128)(2,1)}, bf16[1024,768]{1,0:T(8,128)(2,1)}, f32[1024,76...) custom-call(s32[1]{0:T(128)S(6)} %copy.34.len_ref, ...), custom_call_target="tpu_custom_call" | custom-call | flops 17716740096 | bytes 56623104 | tf_op jit(solution)/shard_map/forward/pallas_call | solution.py:954
  72.4 0.0 copy-done.2
  72.4 0.8 copy.29.wr_ref
  73.3 154.5 %experts.1 = (bf16[2,1024,768]{2,1,0:T(8,128)(2,1)}, bf16[8,128,768]{2,1,0:T(8,128)(2,1)}, bf16[8,128,768]{2,1,0:T(8,128)(2,1)}, bf16[2,2,4,768,768]{4,3,2,1,0:T...) custom-call(bf16[1024,768]{1,0:T(8,128)(2,1)} %bitcast.4, ...), custom_call_target="tpu_custom_call" | custom-call | flops 57982058496 | bytes 69206016 | tf_op jit(solution)/shard_map/experts/pallas_call | solution.py:970
  227.8 146.3 %backward.1 = (bf16[1024,768]{1,0:T(8,128)(2,1)}, bf16[1024,768]{1,0:T(8,128)(2,1)}, bf16[18528,128]{1,0:T(8,128)(2,1)}, f32[24,768]{1,0:T(8,128)}, bf16[8,128,7...) custom-call(s32[1]{0:T(128)S(6)} %copy.34.len_ref, ...), custom_call_target="tpu_custom_call" | custom-call | flops 28991029248 | bytes 72351744 | tf_op jit(solution)/shard_map/backward/pallas_call | solution.py:1014
  374.1 0.0 copy-start.1
  374.1 15.7 %finish.1 = (f32[768,768]{1,0:T(8,128)}, f32[768,768]{1,0:T(8,128)}, f32[768,768]{1,0:T(8,128)}, f32[768,768]{1,0:T(8,128)}, f32[768]{0:T(1024)}, /*index=5*/f32...) custom-call(s32[1]{0:T(128)} %bitcast.2.place_ref, ...), custom_call_target="tpu_custom_call" | custom-call | flops 589824 | bytes 35389440 | tf_op jit(solution)/shard_map/finish/pallas_call | solution.py:1041
  389.8 0.0 copy-start
  389.8 1.9 copy.31
  391.7 1.4 copy.30
  393.0 0.0 copy-done.1
  393.0 1.1 copy.35
  394.2 0.0 copy-done
  394.2 1.1 copy.36
  (1 shorter events, 0.0 us)
Async XLA Ops:
  1.4 1.2 copy-start.3
  2.7 69.8 %copy-start.2 = (bf16[768,16]{0,1:T(8,128)(2,1)S(1)}, bf16[768,16]{0,1:T(8,128)(2,1)}, u32[]{:S(2)}) copy-start(bf16[768,16]{0,1:T(8,128)(2,1)} %param.23) | copy-start | bytes 73732
  374.1 19.0 %copy-start.1 = (bf16[1024,768]{1,0:T(8,128)(2,1)S(1)}, bf16[1024,768]{1,0:T(8,128)(2,1)}, u32[]{:S(2)}) copy-start(bf16[1024,768]{1,0:T(8,128)(2,1)} %get-tuple-element.106) | copy-start | bytes 4718596
  389.8 4.4 %copy-start = (bf16[1024,768]{1,0:T(8,128)(2,1)S(1)}, bf16[1024,768]{1,0:T(8,128)(2,1)}, u32[]{:S(2)}) copy-start(bf16[1024,768]{1,0:T(8,128)(2,1)} %get-tuple-element.107) | copy-start | bytes 4718596
